TPU v7x, 128 devices: a whole 4x4x4 slice. The times are simulated.
128 devices in a mesh: dp: 4 (over z), expert: 32 (over x, y, core).
Axes of the slice: x: 4, y: 4, z: 4, core: 2. Of those that a mesh axis runs over, the one named last changes fastest.
Arguments:
- tokens: bfloat16 [16384, 1024], P(('dp', 'expert')), may hold values from -6 to 6
- cotangent: bfloat16 [16384, 1024], P(('dp', 'expert')), may hold values from -6 to 6
- routes_first: int32 [16384, 1], P(('dp', 'expert')), may hold values from 0 to 31; in each aligned block of 64 rows (0 to 63, 64 to 127, ...) at most 4 rows name the same one
- routes_second: int32 [16384, 1], P(('dp', 'expert')), may hold values from 0 to 63; in each aligned block of 64 rows (0 to 63, 64 to 127, ...) at most 2 rows name the same one
- inner_first: bfloat16 [1024, 3072], P('expert'), may hold values from -0.1875 to 0.1875
- outer_first: bfloat16 [1024, 1024], P('expert'), may hold values from -0.5 to 0.5
- widen_first: bfloat16 [1024, 4096], P('expert'), may hold values from -0.1875 to 0.1875
- narrow_first: bfloat16 [4096, 1024], P('expert'), may hold values from -0.09375 to 0.09375
- mixer_first: bfloat16 [1024, 2], P('expert'), may hold values from -0.1875 to 0.1875
- gain_first: bfloat16 [1024], P('expert'), may hold values from 0.5 to 1.5
- regain_first: bfloat16 [1024], P('expert'), may hold values from 0.5 to 1.5
- inner_second: bfloat16 [1024, 3072], P('expert'), may hold values from -0.1875 to 0.1875
- outer_second: bfloat16 [1024, 1024], P('expert'), may hold values from -0.5 to 0.5
- widen_second: bfloat16 [1024, 4096], P('expert'), may hold values from -0.1875 to 0.1875
- narrow_second: bfloat16 [4096, 1024], P('expert'), may hold values from -0.09375 to 0.09375
- mixer_second: bfloat16 [1024, 2], P('expert'), may hold values from -0.1875 to 0.1875
- gain_second: bfloat16 [1024], P('expert'), may hold values from 0.5 to 1.5
- regain_second: bfloat16 [1024], P('expert'), may hold values from 0.5 to 1.5
- expand_first: bfloat16 [32, 1024, 4096], P('expert', None, 'dp'), may hold values from -0.1875 to 0.1875
- reduce_first: bfloat16 [32, 4096, 1024], P('expert', 'dp'), may hold values from -0.09375 to 0.09375
- expand_second: bfloat16 [128, 1024, 2048], P(('dp', 'expert')), may hold values from -0.1875 to 0.1875
- reduce_second: bfloat16 [128, 2048, 1024], P(('dp', 'expert')), may hold values from -0.09375 to 0.09375
Outputs:
- first_output: bfloat16 [16384, 1024], P(('dp', 'expert'))
- second_output: bfloat16 [16384, 1024], P(('dp', 'expert'))
- gradient_tokens: float32 [16384, 1024], P(('dp', 'expert'))
- gradient_inner_first: float32 [1024, 3072], P('expert')
- gradient_outer_first: float32 [1024, 1024], P('expert')
- gradient_widen_first: float32 [1024, 4096], P('expert')
- gradient_narrow_first: float32 [4096, 1024], P('expert')
- gradient_mixer_first: float32 [1024, 2], P('expert')
- gradient_gain_first: float32 [1024], P('expert')
- gradient_regain_first: float32 [1024], P('expert')
- gradient_inner_second: float32 [1024, 3072], P('expert')
- gradient_outer_second: float32 [1024, 1024], P('expert')
- gradient_widen_second: float32 [1024, 4096], P('expert')
- gradient_narrow_second: float32 [4096, 1024], P('expert')
- gradient_mixer_second: float32 [1024, 2], P('expert')
- gradient_gain_second: float32 [1024], P('expert')
- gradient_regain_second: float32 [1024], P('expert')
- gradient_expand_first: float32 [32, 1024, 4096], P('expert', None, 'dp')
- gradient_reduce_first: float32 [32, 4096, 1024], P('expert', 'dp')
- gradient_expand_second: float32 [128, 1024, 2048], P(('dp', 'expert'))
- gradient_reduce_second: float32 [128, 2048, 1024], P(('dp', 'expert'))
Inputs may be any that keep to these rules, and one draw needn't show every extreme that they name: `routes_first`: in each aligned block of 64 rows (one sequence) no expert is named by more than 4 rows. `routes_second`: in each aligned block of 64 rows (one sequence) no expert is named by more than 2 rows.
All inputs are finite; a program needn't handle non-finite values.
Results may differ from a plain program's by a relative error of at most 0.035.
Values may be sent and summed in bfloat16 or wider, within the bound.
No kernel may reach another device: no remote copies, remote signals or barrier semaphores. Data moves between devices by JAX's collectives and lax.ppermute only.
A program may use at most 320 MiB of HBM per device.

v0:
```python
import jax
import jax.numpy as jnp
from jax import lax
from jax.sharding import PartitionSpec as P

HEADS = 16
HEAD = 64
SEQ = 64
MICRO = 2


highest = lax.Precision.HIGHEST
epsilon = 1e-05


def shortened(shard):
    return jax.tree.map(lambda a: a.astype(jnp.bfloat16) if a.dtype == jnp.float32 else a, shard)


def layer_norm(values, gain):
    center = values - jnp.mean(values, axis=-1, keepdims=True)
    spread = jnp.mean(center * center, axis=-1, keepdims=True)
    return center * lax.rsqrt(spread + epsilon) * gain


def softmax_rows(values):
    top = jnp.max(values, axis=-1, keepdims=True)
    raised = jnp.exp(values - top)
    return raised / jnp.sum(raised, axis=-1, keepdims=True)


def gather_dense(weights):
    return (
        lax.all_gather(weights[0], "expert", axis=0, tiled=True),
        lax.all_gather(weights[1], "expert", axis=0, tiled=True),
        lax.all_gather(weights[2], "expert", axis=0, tiled=True),
        lax.all_gather(weights[3], "expert", axis=0, tiled=True),
        lax.all_gather(weights[4], "expert", axis=0, tiled=True),
        lax.all_gather(weights[5], "expert", axis=0, tiled=True),
        lax.all_gather(weights[6], "expert", axis=0, tiled=True),
    )


def sum_dense(gradients):
    shards = jax.tree.map(
        lambda part: part.astype(jnp.float32),
        lax.psum_scatter(shortened(gradients), "expert", scatter_dimension=0, tiled=True),
    )
    return jax.tree.map(lambda part: part.astype(jnp.float32), lax.psum(shortened(shards), "dp"))


def accumulate(total, update):
    if total is None:
        return update
    return jax.tree.map(jnp.add, total, update)


def slot_table(route, experts, capacity):
    chosen = route[:, 0]
    one_hot = (chosen[:, None] == jnp.arange(experts, dtype=jnp.int32)[None, :]).astype(jnp.int32)
    position = jnp.sum((jnp.cumsum(one_hot, axis=0) - 1) * one_hot, axis=1)
    slot = chosen * capacity + position
    return (slot[:, None] == jnp.arange(experts * capacity, dtype=jnp.int32)[None, :]).astype(
        jnp.bfloat16
    )


def to_owners(rows, table, groups, fan):
    buffer = jnp.einsum("sc,sd->cd", table, rows, preferred_element_type=jnp.float32).astype(
        jnp.bfloat16
    )
    width = buffer.shape[-1]
    spread = jnp.repeat(buffer.reshape(groups, -1, width), fan, axis=0).reshape(-1, width)
    return lax.all_to_all(spread, ("dp", "expert"), split_axis=0, concat_axis=0, tiled=True)


def from_owners(parts, table, groups, fan):
    width = parts.shape[-1]
    back = lax.all_to_all(parts, ("dp", "expert"), split_axis=0, concat_axis=0, tiled=True)
    summed = jnp.sum(back.astype(jnp.float32).reshape(groups, fan, -1, width), axis=1).reshape(
        -1, width
    )
    return jnp.dot(table.astype(jnp.float32), summed, precision=highest)


def owner_forward(received, expander, reducer):
    widened = jnp.dot(received, expander[0], preferred_element_type=jnp.float32)
    active = jax.nn.gelu(widened).astype(jnp.bfloat16)
    parts = jnp.dot(active, reducer[0], preferred_element_type=jnp.float32).astype(jnp.bfloat16)
    return (widened, active, parts)


def owner_backward(received, expander, reducer, widened, active, incoming):
    grad_reducer = jnp.einsum("rf,rd->fd", active, incoming, preferred_element_type=jnp.float32)
    grad_active = jnp.einsum("rd,fd->rf", incoming, reducer[0], preferred_element_type=jnp.float32)
    gelu_pullback = jax.vjp(jax.nn.gelu, widened)[1]
    grad_widened = gelu_pullback(grad_active)[0].astype(jnp.bfloat16)
    grad_expander = jnp.einsum(
        "rd,rf->df", received, grad_widened, preferred_element_type=jnp.float32
    )
    grad_rows = jnp.einsum(
        "rf,df->rd", grad_widened, expander[0], preferred_element_type=jnp.float32
    ).astype(jnp.bfloat16)
    return ((grad_expander[None], grad_reducer[None]), grad_rows)


def dense_forward(stream, weights):
    inner, outer, widen, narrow, mixer, gain, regain = weights
    length = stream.shape[0]
    normed = layer_norm(stream, gain.astype(jnp.float32)).astype(jnp.bfloat16)
    joint = (
        jnp.dot(normed, inner, preferred_element_type=jnp.float32)
        .astype(jnp.bfloat16)
        .reshape(length, 3, HEADS, HEAD)
    )
    query = joint[:, 0]
    keys = joint[:, 1]
    values = joint[:, 2]
    scores = jnp.einsum("qhd,khd->hqk", query, keys, preferred_element_type=jnp.float32) * HEAD ** (
        -0.5
    )
    causal = jnp.arange(length)[:, None] >= jnp.arange(length)[None, :]
    attention = softmax_rows(jnp.where(causal, scores, -1e30))
    attention_low = attention.astype(jnp.bfloat16)
    mixed = (
        jnp.einsum("hqk,khd->qhd", attention_low, values, preferred_element_type=jnp.float32)
        .astype(jnp.bfloat16)
        .reshape(length, HEADS * HEAD)
    )
    middle = stream + jnp.dot(mixed, outer, preferred_element_type=jnp.float32)
    normed_two = layer_norm(middle, regain.astype(jnp.float32)).astype(jnp.bfloat16)
    widened = jnp.dot(normed_two, widen, preferred_element_type=jnp.float32)
    active = jax.nn.gelu(widened).astype(jnp.bfloat16)
    dense = jnp.dot(active, narrow, preferred_element_type=jnp.float32)
    shares = softmax_rows(
        jnp.dot(normed_two.astype(jnp.float32), mixer.astype(jnp.float32), precision=highest)
    )
    return (
        normed,
        query,
        keys,
        values,
        attention,
        attention_low,
        mixed,
        middle,
        normed_two,
        widened,
        active,
        dense,
        shares,
    )


def dense_backward(stream, weights, saved, upstream, expert, returned):
    inner, outer, widen, narrow, mixer, gain, regain = weights
    (
        normed,
        query,
        keys,
        values,
        attention,
        attention_low,
        mixed,
        middle,
        normed_two,
        widened,
        active,
        dense,
        shares,
    ) = saved
    length = stream.shape[0]
    grad_dense = (upstream * shares[:, 0:1]).astype(jnp.bfloat16)
    grad_shares = jnp.concatenate(
        [
            jnp.sum(upstream * dense, axis=1, keepdims=True),
            jnp.sum(upstream * expert, axis=1, keepdims=True),
        ],
        axis=1,
    )
    grad_logits = shares * (grad_shares - jnp.sum(shares * grad_shares, axis=1, keepdims=True))
    grad_mixer = jnp.einsum(
        "sd,sk->dk", normed_two.astype(jnp.float32), grad_logits, precision=highest
    )
    grad_narrow = jnp.einsum("sf,sd->fd", active, grad_dense, preferred_element_type=jnp.float32)
    grad_active = jnp.einsum("sd,fd->sf", grad_dense, narrow, preferred_element_type=jnp.float32)
    gelu_pullback = jax.vjp(jax.nn.gelu, widened)[1]
    grad_widened = gelu_pullback(grad_active)[0].astype(jnp.bfloat16)
    grad_widen = jnp.einsum(
        "sd,sf->df", normed_two, grad_widened, preferred_element_type=jnp.float32
    )
    grad_normed_two = jnp.einsum(
        "sk,dk->sd", grad_logits, mixer.astype(jnp.float32), precision=highest
    )
    grad_normed_two = (
        grad_normed_two
        + jnp.einsum("sf,df->sd", grad_widened, widen, preferred_element_type=jnp.float32)
        + returned
    )
    norm_pullback = jax.vjp(layer_norm, middle, regain.astype(jnp.float32))[1]
    grad_from_norm, grad_regain = norm_pullback(grad_normed_two)
    grad_middle = upstream + grad_from_norm
    grad_attended = grad_middle.astype(jnp.bfloat16)
    grad_outer = jnp.einsum("sd,se->de", mixed, grad_attended, preferred_element_type=jnp.float32)
    grad_mixed = (
        jnp.einsum("se,de->sd", grad_attended, outer, preferred_element_type=jnp.float32)
        .astype(jnp.bfloat16)
        .reshape(length, HEADS, HEAD)
    )
    grad_values = jnp.einsum(
        "hqk,qhd->khd", attention_low, grad_mixed, preferred_element_type=jnp.float32
    )
    grad_attention = jnp.einsum(
        "qhd,khd->hqk", grad_mixed, values, preferred_element_type=jnp.float32
    )
    grad_scores = (
        attention * (grad_attention - jnp.sum(attention * grad_attention, axis=-1, keepdims=True))
    ).astype(jnp.bfloat16)
    grad_query = jnp.einsum(
        "hqk,khd->qhd", grad_scores, keys, preferred_element_type=jnp.float32
    ) * HEAD ** (-0.5)
    grad_keys = jnp.einsum(
        "hqk,qhd->khd", grad_scores, query, preferred_element_type=jnp.float32
    ) * HEAD ** (-0.5)
    grad_joint = (
        jnp.stack([grad_query, grad_keys, grad_values], axis=1)
        .astype(jnp.bfloat16)
        .reshape(length, 3 * HEADS * HEAD)
    )
    grad_inner = jnp.einsum("sd,se->de", normed, grad_joint, preferred_element_type=jnp.float32)
    grad_normed = jnp.einsum("se,de->sd", grad_joint, inner, preferred_element_type=jnp.float32)
    first_pullback = jax.vjp(layer_norm, stream, gain.astype(jnp.float32))[1]
    grad_from_first, grad_gain = first_pullback(grad_normed)
    return (
        grad_middle + grad_from_first,
        (grad_inner, grad_outer, grad_widen, grad_narrow, grad_mixer, grad_gain, grad_regain),
    )


def on_device(
    tokens,
    cotangent,
    routes_first,
    routes_second,
    inner_first,
    outer_first,
    widen_first,
    narrow_first,
    mixer_first,
    gain_first,
    regain_first,
    inner_second,
    outer_second,
    widen_second,
    narrow_second,
    mixer_second,
    gain_second,
    regain_second,
    expand_first,
    reduce_first,
    expand_second,
    reduce_second,
):
    owners = lax.axis_size("expert")
    replicas = lax.axis_size("dp")
    gathered = [
        gather_dense(
            (
                inner_first,
                outer_first,
                widen_first,
                narrow_first,
                mixer_first,
                gain_first,
                regain_first,
            )
        ),
        gather_dense(
            (
                inner_second,
                outer_second,
                widen_second,
                narrow_second,
                mixer_second,
                gain_second,
                regain_second,
            )
        ),
    ]
    plans = [
        (routes_first, expand_first, reduce_first, 1, replicas),
        (routes_second, expand_second, reduce_second, replicas // 2, 2),
    ]
    kept = []
    outputs = [[], []]
    for micro in range(MICRO):
        stream = tokens[micro * SEQ : (micro + 1) * SEQ].astype(jnp.float32)
        record = []
        for index in range(2):
            route, expander, reducer, groups, fan = plans[index]
            experts = owners * groups
            capacity = 2 * SEQ // experts
            saved = dense_forward(stream, gathered[index])
            table = slot_table(route[micro * SEQ : (micro + 1) * SEQ], experts, capacity)
            received = to_owners(saved[8], table, groups, fan)
            widened, active, parts = owner_forward(received, expander, reducer)
            expert = from_owners(parts, table, groups, fan)
            shares = saved[12]
            record.append((stream, saved, table, received, widened, active, expert))
            stream = saved[7] + shares[:, 0:1] * saved[11] + shares[:, 1:2] * expert
            outputs[index].append(stream.astype(jnp.bfloat16))
        kept.append(record)
    totals = [None, None]
    expert_totals = [None, None]
    input_grads = []
    for micro in range(MICRO):
        upstream = cotangent[micro * SEQ : (micro + 1) * SEQ].astype(jnp.float32)
        for index in (1, 0):
            stream, saved, table, received, widened, active, expert = kept[micro][index]
            route, expander, reducer, groups, fan = plans[index]
            grad_expert = (upstream * saved[12][:, 1:2]).astype(jnp.bfloat16)
            incoming = to_owners(grad_expert, table, groups, fan)
            expert_grads, grad_rows = owner_backward(
                received, expander, reducer, widened, active, incoming
            )
            returned = from_owners(grad_rows, table, groups, fan)
            upstream, dense_grads = dense_backward(
                stream, gathered[index], saved, upstream, expert, returned
            )
            totals[index] = accumulate(totals[index], dense_grads)
            expert_totals[index] = accumulate(expert_totals[index], expert_grads)
        input_grads.append(upstream)
    finals = [sum_dense(totals[0]), sum_dense(totals[1])]
    first_output = jnp.concatenate(outputs[0], axis=0)
    second_output = jnp.concatenate(outputs[1], axis=0)
    gradient_tokens = jnp.concatenate(input_grads, axis=0)
    return (
        (first_output, second_output, gradient_tokens)
        + tuple(finals[0])
        + tuple(finals[1])
        + tuple(expert_totals[0])
        + tuple(expert_totals[1])
    )


def solution(mesh):
    placed = (
        P(("dp", "expert"), None),
        P(("dp", "expert"), None),
        P(("dp", "expert"), None),
        P(("dp", "expert"), None),
        P("expert", None),
        P("expert", None),
        P("expert", None),
        P("expert", None),
        P("expert", None),
        P("expert"),
        P("expert"),
        P("expert", None),
        P("expert", None),
        P("expert", None),
        P("expert", None),
        P("expert", None),
        P("expert"),
        P("expert"),
        P("expert", None, "dp"),
        P("expert", "dp", None),
        P(("dp", "expert"), None, None),
        P(("dp", "expert"), None, None),
    )
    return jax.shard_map(
        on_device,
        mesh=mesh,
        in_specs=placed,
        out_specs=(
            P(("dp", "expert"), None),
            P(("dp", "expert"), None),
            P(("dp", "expert"), None),
            P("expert", None),
            P("expert", None),
            P("expert", None),
            P("expert", None),
            P("expert", None),
            P("expert"),
            P("expert"),
            P("expert", None),
            P("expert", None),
            P("expert", None),
            P("expert", None),
            P("expert", None),
            P("expert"),
            P("expert"),
            P("expert", None, "dp"),
            P("expert", "dp", None),
            P(("dp", "expert"), None, None),
            P(("dp", "expert"), None, None),
        ),
        check_vma=False,
    )
```

profile of v0, /device:TPU:0, one launch (start us, length us, event | category | flops | bytes accessed | tf_op | source)
XLA Modules:
  0.0 1617.7 jit_solution(16110146174910025305)
XLA Ops:
  20.3 68.8 %all-reduce.9 = (bf16[1024]{0:T(1024)(128)(2,1)S(1)}, bf16[1024]{0:T(1024)(128)(2,1)S(1)}, bf16[1024]{0:T(1024)(128)(2,1)S(1)}, bf16[1024]{0:T(1024)(128)(2,1)S(1)}) all-reduce(bf16[1024]{0:T(1024)(128)(2,1)S(1)} %dynamic-update-slice, bf16[1024]{0:T(1024)(128)(2,1)S(1)} %dynamic-update-slice.1, ...), channel_id=1, replica_groups=mesh['dp'=4,'expert'=32] {'expert'}, use_global_device_ids=true, to_apply=%add | all-reduce | flops 4096 | bytes 16384
  89.3 17.5 %all-gather = bf16[32,32,2]{1,2,0:T(2,128)(2,1)S(1)} all-gather(bf16[1,32,2]{1,2,0:T(2,128)(2,1)S(1)} %bitcast.484), channel_id=1, replica_groups=mesh['dp'=4,'expert'=32] {'expert'}, dimensions={0}, use_global_device_ids=true | all-gather | bytes 4224 | tf_op jit(solution)/shard_map/all_gather | solution.py:38
  107.5 21.6 %all-gather.1 = bf16[32,32,2]{1,2,0:T(2,128)(2,1)S(1)} all-gather(bf16[1,32,2]{1,2,0:T(2,128)(2,1)S(1)} %bitcast.485), channel_id=1, replica_groups=mesh['dp'=4,'expert'=32] {'expert'}, dimensions={0}, use_global_device_ids=true | all-gather | bytes 4224 | tf_op jit(solution)/shard_map/all_gather | solution.py:38
  159.5 10.6 all-to-all-start
  173.2 18.9 %all-to-all-done = bf16[128,4,1024]{2,1,0:T(4,128)(2,1)} async-done(((bf16[128,4,1024]{2,1,0:T(4,128)(2,1)}), bf16[128,4,1024]{2,1,0:T(4,128)(2,1)}, u32[]{:S(2)}, u32[]{:S(2)}) %all-to-all-start) | async-done | bytes 1048608 | tf_op jit(solution)/shard_map/all_to_all | solution.py:74
  209.3 18.1 %all-to-all-done.2 = bf16[128,4,1024]{2,1,0:T(4,128)(2,1)} async-done(((bf16[128,4,1024]{2,1,0:T(4,128)(2,1)}), bf16[128,4,1024]{2,1,0:T(4,128)(2,1)}, u32[]{:S(2)}, u32[]{:S(2)}) %all-to-all-start.2) | async-done | bytes 1048608 | tf_op jit(solution)/shard_map/all_to_all | solution.py:74
  244.0 8.7 all-to-all-done.1
  263.6 17.8 %all-to-all-done.3 = bf16[128,4,1024]{2,1,0:T(4,128)(2,1)S(1)} async-done(((bf16[128,4,1024]{2,1,0:T(4,128)(2,1)}), bf16[128,4,1024]{2,1,0:T(4,128)(2,1)S(1)}, u32[]{:S(2)}, u32[]{:S(2)}) %all-to-all-start.3) | async-done | bytes 1048608 | tf_op jit(solution)/shard_map/all_to_all | solution.py:79
  365.2 24.8 %all-gather.23.cloned.1.call-done = bf16[1024,4096]{1,0:T(8,128)(2,1)} async-done(((bf16[32,4096]{1,0:T(8,128)(2,1)}), bf16[1024,4096]{1,0:T(8,128)(2,1)}) %all-gather.23.cloned.1.call-update) | async-done | bytes 8388624 | tf_op jit(solution)/shard_map/all_gather | solution.py:36
  396.1 48.5 %all-gather.25.cloned.1.call-done = bf16[4096,1024]{1,0:T(8,128)(2,1)} async-done(((bf16[128,1024]{1,0:T(8,128)(2,1)}), bf16[4096,1024]{1,0:T(8,128)(2,1)}) %all-gather.25.cloned.1.call-update) | async-done | bytes 8388624 | tf_op jit(solution)/shard_map/all_gather | solution.py:37
  453.2 8.8 all-to-all-start.4
  475.1 8.6 all-to-all-start.7
  496.8 8.5 all-to-all-start.5
  574.2 10.4 all-to-all-start.12
  597.8 9.9 all-to-all-start.9
  620.8 10.1 all-to-all-start.13
  751.4 10.4 all-to-all-start.11
  780.9 8.6 all-to-all-start.15
  858.1 9.5 fusion.226
  867.6 11.6 add_convert_fusion
  888.5 11.6 add_convert_fusion.1
  901.1 8.3 fusion.278
  909.3 11.7 add_convert_fusion.2
  930.3 11.5 add_convert_fusion.3
  974.6 72.6 %reduce-scatter.23.cloned.1.call-done = bf16[32,3072]{1,0:T(8,128)(2,1)} async-done(((bf16[1024,3072]{1,0:T(8,128)(2,1)}), bf16[32,3072]{1,0:T(8,128)(2,1)}) %reduce-scatter.23.cloned.1.call-update) | async-done | bytes 196624 | tf_op jit(solution)/shard_map/reduce_scatter | solution.py:47
  1047.2 89.6 %reduce-scatter.15.cloned.1.call-done = bf16[32,3072]{1,0:T(8,128)(2,1)} async-done(((bf16[1024,3072]{1,0:T(8,128)(2,1)}), bf16[32,3072]{1,0:T(8,128)(2,1)}) %reduce-scatter.15.cloned.1.call-update) | async-done | bytes 196624 | tf_op jit(solution)/shard_map/reduce_scatter | solution.py:47
  1136.8 95.5 %reduce-scatter.29.cloned.1.call-done = bf16[128,1024]{1,0:T(8,128)(2,1)} async-done(((bf16[4096,1024]{1,0:T(8,128)(2,1)}), bf16[128,1024]{1,0:T(8,128)(2,1)}) %reduce-scatter.29.cloned.1.call-update) | async-done | bytes 262160 | tf_op jit(solution)/shard_map/reduce_scatter | solution.py:47
  1232.3 96.0 %reduce-scatter.27.cloned.1.call-done = bf16[32,4096]{1,0:T(8,128)(2,1)} async-done(((bf16[1024,4096]{1,0:T(8,128)(2,1)}), bf16[32,4096]{1,0:T(8,128)(2,1)}) %reduce-scatter.27.cloned.1.call-update) | async-done | bytes 262160 | tf_op jit(solution)/shard_map/reduce_scatter | solution.py:47
  1328.3 95.6 %reduce-scatter.21.cloned.1.call-done = bf16[128,1024]{1,0:T(8,128)(2,1)} async-done(((bf16[4096,1024]{1,0:T(8,128)(2,1)}), bf16[128,1024]{1,0:T(8,128)(2,1)}) %reduce-scatter.21.cloned.1.call-update) | async-done | bytes 262160 | tf_op jit(solution)/shard_map/reduce_scatter | solution.py:47
  1423.9 96.0 %reduce-scatter.19.cloned.1.call-done = bf16[32,4096]{1,0:T(8,128)(2,1)} async-done(((bf16[1024,4096]{1,0:T(8,128)(2,1)}), bf16[32,4096]{1,0:T(8,128)(2,1)}) %reduce-scatter.19.cloned.1.call-update) | async-done | bytes 262160 | tf_op jit(solution)/shard_map/reduce_scatter | solution.py:47
  1520.4 64.3 %all-reduce.8 = (bf16[1024]{0:T(1024)(128)(2,1)S(1)}, bf16[1024]{0:T(1024)(128)(2,1)S(1)}, bf16[1024]{0:T(1024)(128)(2,1)S(1)}, bf16[1024]{0:T(1024)(128)(2,1)S(1)}) all-reduce(bf16[1024]{0:T(1024)(128)(2,1)S(1)} %add_convert_fusion.13, ...), channel_id=7, replica_groups=mesh['dp'=4,'expert'=32] {'expert'}, use_global_device_ids=true, to_apply=%region_92.93.clone | all-reduce | flops 4096 | bytes 16384
  1585.0 10.6 all-reduce.10
  (1038 shorter events, 582.8 us)
Async XLA Ops:
  7.3 125.5 %all-gather.11.cloned.1.call-start = ((), (), s32[]{:S(2)}) async-start(), calls=%async_computation.26 | async-start | bytes 6488064 | tf_op jit(solution)/shard_map/all_gather | solution.py:34
  8.1 141.7 %all-gather.13.cloned.1.call-start = ((), (), s32[]{:S(2)}) async-start(), calls=%async_computation.27 | async-start | bytes 2162688 | tf_op jit(solution)/shard_map/all_gather | solution.py:35
  8.8 276.8 %all-gather.15.cloned.1.call-start = ((), (), s32[]{:S(2)}) async-start(), calls=%async_computation.28 | async-start | bytes 8650752 | tf_op jit(solution)/shard_map/all_gather | solution.py:36
  9.5 281.0 %all-gather.17.cloned.1.call-start = ((), (), s32[]{:S(2)}) async-start(), calls=%async_computation.29 | async-start | bytes 8650752 | tf_op jit(solution)/shard_map/all_gather | solution.py:37
  10.1 287.6 %all-gather.19.cloned.1.call-start = ((), (), s32[]{:S(2)}) async-start(), calls=%async_computation.30 | async-start | bytes 6488064 | tf_op jit(solution)/shard_map/all_gather | solution.py:34
  10.7 325.6 %all-gather.21.cloned.1.call-start = ((), (), s32[]{:S(2)}) async-start(), calls=%async_computation.31 | async-start | bytes 2162688 | tf_op jit(solution)/shard_map/all_gather | solution.py:35
  11.3 378.7 %all-gather.23.cloned.1.call-start = ((), (), s32[]{:S(2)}) async-start(), calls=%async_computation.32 | async-start | bytes 8650752 | tf_op jit(solution)/shard_map/all_gather | solution.py:36
  12.0 432.5 %all-gather.25.cloned.1.call-start = ((), (), s32[]{:S(2)}) async-start(), calls=%async_computation.33 | async-start | bytes 8650752 | tf_op jit(solution)/shard_map/all_gather | solution.py:37
  159.5 32.6 %all-to-all-start = ((bf16[128,4,1024]{2,1,0:T(4,128)(2,1)}), bf16[128,4,1024]{2,1,0:T(4,128)(2,1)}, u32[]{:S(2)}, u32[]{:S(2)}) async-start(bf16[128,4,1024]{2,1,0:T(4,128)(2,1)} %all_to_all.112), calls=%async_computation | async-start | bytes 2097152 | tf_op jit(solution)/shard_map/all_to_all | solution.py:74
  192.1 35.3 %all-to-all-start.2 = ((bf16[128,4,1024]{2,1,0:T(4,128)(2,1)}), bf16[128,4,1024]{2,1,0:T(4,128)(2,1)}, u32[]{:S(2)}, u32[]{:S(2)}) async-start(bf16[128,4,1024]{2,1,0:T(4,128)(2,1)} %all_to_all.117), calls=%async_computation.2 | async-start | bytes 2097152 | tf_op jit(solution)/shard_map/all_to_all | solution.py:74
  227.4 25.3 %all-to-all-start.1 = ((bf16[128,4,1024]{2,1,0:T(4,128)(2,1)}), bf16[128,4,1024]{2,1,0:T(4,128)(2,1)}, u32[]{:S(2)}, u32[]{:S(2)}) async-start(bf16[128,4,1024]{2,1,0:T(4,128)(2,1)} %all_to_all.115), calls=%async_computation.1 | async-start | bytes 2097152 | tf_op jit(solution)/shard_map/all_to_all | solution.py:79
  252.7 28.7 %all-to-all-start.3 = ((bf16[128,4,1024]{2,1,0:T(4,128)(2,1)}), bf16[128,4,1024]{2,1,0:T(4,128)(2,1)S(1)}, u32[]{:S(2)}, u32[]{:S(2)}) async-start(bf16[128,4,1024]{2,1,0:T(4,128)(2,1)} %all_to_all.120), calls=%async_computation.3 | async-start | bytes 2097152 | tf_op jit(solution)/shard_map/all_to_all | solution.py:79
  357.3 95.8 %all-to-all-start.6 = ((bf16[128,2,1024]{2,1,0:T(2,128)(2,1)}), bf16[128,2,1024]{2,1,0:T(2,128)(2,1)}, u32[]{:S(2)}, u32[]{:S(2)}) async-start(bf16[128,2,1024]{2,1,0:T(2,128)(2,1)} %all_to_all.127), calls=%async_computation.6 | async-start | bytes 1048576 | tf_op jit(solution)/shard_map/all_to_all | solution.py:74
  505.3 437.6 %reduce-scatter.33.cloned.1.call-start = ((), (), s32[]{:S(2)}) async-start(), calls=%async_computation.43 | async-start | bytes 270336
  542.8 31.4 %all-to-all-start.8 = ((bf16[128,2,1024]{2,1,0:T(2,128)(2,1)}), bf16[128,2,1024]{2,1,0:T(2,128)(2,1)}, u32[]{:S(2)}, u32[]{:S(2)}) async-start(bf16[128,2,1024]{2,1,0:T(2,128)(2,1)} %all_to_all.132), calls=%async_computation.8 | async-start | bytes 1048576 | tf_op jit(solution)/shard_map/all_to_all | solution.py:74
  574.2 23.6 %all-to-all-start.12 = ((bf16[128,2,1024]{2,1,0:T(2,128)(2,1)}), bf16[128,2,1024]{2,1,0:T(2,128)(2,1)}, u32[]{:S(2)}, u32[]{:S(2)}) async-start(bf16[128,2,1024]{2,1,0:T(2,128)(2,1)} %all_to_all.142), calls=%async_computation.12 | async-start | bytes 1048576 | tf_op jit(solution)/shard_map/all_to_all | solution.py:74
  597.8 23.0 %all-to-all-start.9 = ((bf16[128,2,1024]{2,1,0:T(2,128)(2,1)}), bf16[128,2,1024]{2,1,0:T(2,128)(2,1)}, u32[]{:S(2)}, u32[]{:S(2)}) async-start(bf16[128,2,1024]{2,1,0:T(2,128)(2,1)} %all_to_all.135), calls=%async_computation.9 | async-start | bytes 1048576 | tf_op jit(solution)/shard_map/all_to_all | solution.py:79
  620.8 23.2 %all-to-all-start.13 = ((bf16[128,2,1024]{2,1,0:T(2,128)(2,1)}), bf16[128,2,1024]{2,1,0:T(2,128)(2,1)}, u32[]{:S(2)}, u32[]{:S(2)}) async-start(bf16[128,2,1024]{2,1,0:T(2,128)(2,1)} %all_to_all.145), calls=%async_computation.13 | async-start | bytes 1048576 | tf_op jit(solution)/shard_map/all_to_all | solution.py:79
  698.9 26.5 %all-to-all-start.10 = ((bf16[128,4,1024]{2,1,0:T(4,128)(2,1)}), bf16[128,4,1024]{2,1,0:T(4,128)(2,1)}, u32[]{:S(2)}, u32[]{:S(2)}) async-start(bf16[128,4,1024]{2,1,0:T(4,128)(2,1)} %all_to_all.137), calls=%async_computation.10 | async-start | bytes 2097152 | tf_op jit(solution)/shard_map/all_to_all | solution.py:74
  706.7 251.9 %reduce-scatter.31.cloned.1.call-start = ((), (), s32[]{:S(2)}) async-start(), calls=%async_computation.42 | async-start | bytes 270336
  713.2 261.3 %reduce-scatter.25.cloned.1.call-start = ((), (), s32[]{:S(2)}) async-start(), calls=%async_computation.39 | async-start | bytes 2162688 | tf_op jit(solution)/shard_map/reduce_scatter | solution.py:47
  725.3 26.1 %all-to-all-start.14 = ((bf16[128,4,1024]{2,1,0:T(4,128)(2,1)}), bf16[128,4,1024]{2,1,0:T(4,128)(2,1)}, u32[]{:S(2)}, u32[]{:S(2)}) async-start(bf16[128,4,1024]{2,1,0:T(4,128)(2,1)} %all_to_all.147), calls=%async_computation.14 | async-start | bytes 2097152 | tf_op jit(solution)/shard_map/all_to_all | solution.py:74
  751.4 29.5 %all-to-all-start.11 = ((bf16[128,4,1024]{2,1,0:T(4,128)(2,1)}), bf16[128,4,1024]{2,1,0:T(4,128)(2,1)}, u32[]{:S(2)}, u32[]{:S(2)}) async-start(bf16[128,4,1024]{2,1,0:T(4,128)(2,1)} %all_to_all.140), calls=%async_computation.11 | async-start | bytes 2097152 | tf_op jit(solution)/shard_map/all_to_all | solution.py:79
  780.9 27.3 %all-to-all-start.15 = ((bf16[128,4,1024]{2,1,0:T(4,128)(2,1)}), bf16[128,4,1024]{2,1,0:T(4,128)(2,1)}, u32[]{:S(2)}, u32[]{:S(2)}) async-start(bf16[128,4,1024]{2,1,0:T(4,128)(2,1)} %all_to_all.150), calls=%async_computation.15 | async-start | bytes 2097152 | tf_op jit(solution)/shard_map/all_to_all | solution.py:79
  789.6 185.0 %reduce-scatter.17.cloned.1.call-start = ((), (), s32[]{:S(2)}) async-start(), calls=%async_computation.35 | async-start | bytes 2162688 | tf_op jit(solution)/shard_map/reduce_scatter | solution.py:47
  820.9 226.3 %reduce-scatter.23.cloned.1.call-start = ((), (), s32[]{:S(2)}) async-start(), calls=%async_computation.38 | async-start | bytes 6488064 | tf_op jit(solution)/shard_map/reduce_scatter | solution.py:47
  828.4 308.4 %reduce-scatter.15.cloned.1.call-start = ((), (), s32[]{:S(2)}) async-start(), calls=%async_computation.34 | async-start | bytes 6488064 | tf_op jit(solution)/shard_map/reduce_scatter | solution.py:47
  857.2 375.1 %reduce-scatter.29.cloned.1.call-start = ((), (), s32[]{:S(2)}) async-start(), calls=%async_computation.41 | async-start | bytes 8650752 | tf_op jit(solution)/shard_map/reduce_scatter | solution.py:47
  879.2 449.2 %reduce-scatter.27.cloned.1.call-start = ((), (), s32[]{:S(2)}) async-start(), calls=%async_computation.40 | async-start | bytes 8650752 | tf_op jit(solution)/shard_map/reduce_scatter | solution.py:47
  900.2 523.7 %reduce-scatter.21.cloned.1.call-start = ((), (), s32[]{:S(2)}) async-start(), calls=%async_computation.37 | async-start | bytes 8650752 | tf_op jit(solution)/shard_map/reduce_scatter | solution.py:47
  921.1 598.9 %reduce-scatter.19.cloned.1.call-start = ((), (), s32[]{:S(2)}) async-start(), calls=%async_computation.36 | async-start | bytes 8650752 | tf_op jit(solution)/shard_map/reduce_scatter | solution.py:47
  941.9 658.1 %all-reduce.14.cloned.1.call-start = ((), (), s32[]{:S(2)}) async-start(), calls=%async_computation.44 | async-start | bytes 3145728 | tf_op jit(solution)/shard_map/psum | solution.py:49
  (320 other events, 6182.2 us)
Sparse Core Ops, SparseCore 0:
  10.4 51.6 all-gather.10
  64.4 42.8 all-gather.12
  109.6 51.9 all-gather.14
  163.7 67.0 all-gather.16
  232.9 53.4 all-gather.18
  288.5 42.9 all-gather.20
  333.8 56.1 all-gather.22
  392.3 52.1 all-gather.24
  534.6 74.5 reduce-scatter.32
  713.3 80.5 reduce-scatter.30
  797.4 78.7 reduce-scatter.24
  879.6 78.0 reduce-scatter.16
  961.5 85.6 reduce-scatter.22
  1051.2 85.5 reduce-scatter.14
  1140.3 91.9 reduce-scatter.28
  1236.3 91.9 reduce-scatter.26
  1331.9 91.9 reduce-scatter.20
  1427.9 91.9 reduce-scatter.18
  1522.9 51.3 all-reduce.13
where the time goes:
time: 1630 us; the launch traced here: 1620 us
  waiting for transfers between devices  705 us (43%)
  matrix products  371 us (23%)
  blocking collectives  183 us (11%)
  local copies, waits for them, and re-layouts  145 us (9%)
  starting transfers between devices  131 us (8%)
  other arithmetic  62.8 us (4%)
  between operations  19.8 us (1%)
    reduce_scatter x8, waiting for transfers between devices, sum_dense(): lax.psum_scatter(shortened(gradients), 'expert', scatter_dimension=0, til...  545 us
    unnamed x2, blocking collectives  133 us
    all_to_all x8, starting transfers between devices, from_owners(): lax.all_to_all(parts, ('dp', 'expert'), split_axis=0, concat_axis=0, tile...  66.6 us
    all_to_all x8, starting transfers between devices, to_owners(): lax.all_to_all(spread, ('dp', 'expert'), split_axis=0, concat_axis=0, til...  62.8 us
    all_gather x2, waiting for transfers between devices, gather_dense(): lax.all_gather(weights[3], 'expert', axis=0, tiled=True)  48.5 us
    all_to_all x8, waiting for transfers between devices, to_owners(): lax.all_to_all(spread, ('dp', 'expert'), split_axis=0, concat_axis=0, til...  42.7 us
    unnamed x657, local copies, waits for them, and re-layouts  41.1 us
    dot_general x4, matrix products, dense_backward(): jnp.einsum('sf,sd->fd', active, grad_dense, preferred_element_type=jnp.fl...  41 us
  transfers between devices with their start and end apart: 35, of which 21 were waited for; matrix products, arithmetic and copies ran while one was open for 30% of the time, Pallas kernels for 0%

commit v1 on v0

v1 whole, which is shorter than its diff:
```python
import jax
import jax.numpy as jnp
from jax import lax
from jax.sharding import Mesh, PartitionSpec as P

HEADS = 16
HEAD = 64
SEQ = 64
ALL = ("z", "x", "y", "c")
PLANE = ("x", "y")
SIZES = {"z": 4, "x": 4, "y": 4, "c": 2}
highest = lax.Precision.HIGHEST
epsilon = 1e-05
bf16 = jnp.bfloat16
f32 = jnp.float32


def shift(value, axis, step):
    size = SIZES[axis]
    return lax.ppermute(value, axis, [(i, (i + step) % size) for i in range(size)])


def swap(value):
    return shift(value, "c", 1)


def dot(a, b):
    return jnp.dot(a, b, preferred_element_type=f32)


def dot_tn(a, b):
    return lax.dot_general(a, b, (((0,), (0,)), ((), ())), preferred_element_type=f32)


def dot_nt(a, b):
    return lax.dot_general(a, b, (((1,), (1,)), ((), ())), preferred_element_type=f32)


def in_order(core, mine, twin, axis):
    return jnp.where(
        core == 0,
        jnp.concatenate([mine, twin], axis=axis),
        jnp.concatenate([twin, mine], axis=axis),
    )


def half_of(value, which, axis):
    size = value.shape[axis] // 2
    return lax.dynamic_slice_in_dim(value, which * size, size, axis)


def layer_norm(values, gain):
    center = values - jnp.mean(values, axis=-1, keepdims=True)
    spread = jnp.mean(center * center, axis=-1, keepdims=True)
    return center * lax.rsqrt(spread + epsilon) * gain


def softmax_rows(values):
    top = jnp.max(values, axis=-1, keepdims=True)
    raised = jnp.exp(values - top)
    return raised / jnp.sum(raised, axis=-1, keepdims=True)


def gather_column(value):
    group = jnp.concatenate(
        [value, shift(value, "z", 1), shift(value, "z", -1), shift(value, "z", 2)], axis=0
    )
    return jnp.concatenate([group, swap(group)], axis=0)


def scatter_column(terms):
    rows = terms.shape[0] // 8
    half = terms[: 4 * rows] + swap(terms[4 * rows :].astype(bf16)).astype(f32)
    low = half[rows:].astype(bf16)
    return (
        half[:rows]
        + shift(low[:rows], "z", -1).astype(f32)
        + shift(low[rows : 2 * rows], "z", 1).astype(f32)
        + shift(low[2 * rows :], "z", 2).astype(f32)
    )


def sum_over_z(value):
    own = value.astype(f32)
    opposite = shift(value, "z", 2).astype(f32)
    before = shift(value, "z", 1).astype(f32)
    after = shift(value, "z", -1).astype(f32)
    return (own + opposite) + (before + after)


def gather_over_z(value):
    ahead = [value, shift(value, "z", -1), shift(value, "z", 2), shift(value, "z", 1)]
    twice = jnp.stack(ahead + ahead[:3])
    start = lax.rem(4 - lax.axis_index("z"), 4)
    return lax.dynamic_slice_in_dim(twice, start, 4, 0)


def positions(route):
    chosen = route[:, 0]
    row = jnp.arange(chosen.shape[0], dtype=jnp.int32)
    earlier = (row[None, :] < row[:, None]) & (row[None, :] // SEQ == row[:, None] // SEQ)
    same = (chosen[None, :] == chosen[:, None]) & earlier
    return chosen, row // SEQ, jnp.sum(same.astype(jnp.int32), axis=1)


def table_first(route):
    chosen, sequence, position = positions(route)
    slot = chosen * 8 + sequence * 4 + position
    column = jnp.arange(1024, dtype=jnp.int32) % 256
    return (slot[:, None] == column[None, :]).astype(bf16)


def table_second(route):
    chosen, sequence, position = positions(route)
    slot = (chosen // 32) * 256 + (chosen % 32) * 8 + sequence * 2 + position
    column = jnp.arange(1024, dtype=jnp.int32)
    column = (column // 512) * 256 + column % 256
    rows = (slot[:, None] == column[None, :]).astype(bf16)
    grads = ((slot + 4)[:, None] == column[None, :]).astype(bf16)
    return jnp.concatenate([rows, grads], axis=0)


def exchange(rows):
    blocks = rows.reshape(128, 8, rows.shape[-1])
    moved = lax.all_to_all(blocks, ALL, split_axis=0, concat_axis=0, tiled=True)
    return moved.reshape(rows.shape)


def gelu_slope(widened, gradient):
    return jax.vjp(jax.nn.gelu, widened)[1](gradient)[0].astype(bf16)


def pack_attention(inner, outer, mixer, gain, regain):
    blank = jnp.zeros((inner.shape[0], 124), bf16)
    return jnp.concatenate([inner, outer, mixer, gain[:, None], regain[:, None], blank], axis=1)


def unpack_attention(packed):
    return (
        packed[:, :3072],
        packed[:, 3072:4096],
        packed[:, 4096:4098],
        packed[:, 4098].astype(f32),
        packed[:, 4099].astype(f32),
    )


def pack_feed(widen, narrow):
    z, c = lax.axis_index("z"), lax.axis_index("c")
    units = widen.reshape(32, 16, 2, 4, 32)
    units = lax.dynamic_index_in_dim(units, z, 3, keepdims=False)
    mine = lax.dynamic_index_in_dim(units, c, 2, keepdims=False).reshape(32, 512)
    other = lax.dynamic_index_in_dim(units, 1 - c, 2, keepdims=False).reshape(32, 512)
    columns = in_order(c, mine, swap(other), 1)
    rows = lax.dynamic_slice_in_dim(narrow, z * 32, 32, 0)
    return jnp.concatenate([columns, rows], axis=0)


def unpack_feed(packed):
    widen = packed[:, :32].reshape(16, 32, 2, 512).transpose(0, 2, 1, 3).reshape(1024, 512)
    return widen, packed[:, 32:].reshape(512, 1024)


def attention_forward(stream, weights):
    inner, outer, mixer, gain, regain = weights
    length = stream.shape[0]
    normed = layer_norm(stream, gain).astype(bf16)
    joint = dot(normed, inner).astype(bf16).reshape(length // SEQ, SEQ, 3, HEADS, HEAD)
    query, keys, values = joint[:, :, 0], joint[:, :, 1], joint[:, :, 2]
    scores = jnp.einsum("bqhd,bkhd->bhqk", query, keys, preferred_element_type=f32) * HEAD**-0.5
    causal = jnp.arange(SEQ)[:, None] >= jnp.arange(SEQ)[None, :]
    attention = softmax_rows(jnp.where(causal, scores, -1e30))
    mixed = (
        jnp.einsum("bhqk,bkhd->bqhd", attention.astype(bf16), values, preferred_element_type=f32)
        .astype(bf16)
        .reshape(length, HEADS * HEAD)
    )
    middle = stream + dot(mixed, outer)
    normed_two = layer_norm(middle, regain).astype(bf16)
    shares = softmax_rows(dot(normed_two, mixer))
    return normed, (query, keys, values), attention, mixed, middle, normed_two, shares


def feed_forward(rows, widen, narrow):
    widened = dot(rows, widen)
    active = jax.nn.gelu(widened).astype(bf16)
    return widened, active, dot(active, narrow)


def feed_backward(rows, widen, narrow, widened, active, incoming):
    grad_widened = gelu_slope(widened, dot_nt(incoming, narrow))
    grad_rows = dot_nt(grad_widened, widen)
    return grad_rows, dot_tn(rows, grad_widened), dot_tn(active, incoming)


def attention_backward(stream, weights, saved, upstream, dense, expert, from_feed, from_experts):
    inner, outer, mixer, gain, regain = weights
    normed, (query, keys, values), attention, mixed, middle, normed_two, shares = saved
    length = stream.shape[0]
    grad_shares = jnp.concatenate(
        [
            jnp.sum(upstream * dense, axis=1, keepdims=True),
            jnp.sum(upstream * expert, axis=1, keepdims=True),
        ],
        axis=1,
    )
    grad_logits = shares * (grad_shares - jnp.sum(shares * grad_shares, axis=1, keepdims=True))
    grad_mixer = jnp.einsum("sd,sk->kd", normed_two.astype(f32), grad_logits, precision=highest)
    from_mixer = (
        grad_logits[:, 0:1] * mixer[:, 0].astype(f32) + grad_logits[:, 1:2] * mixer[:, 1].astype(f32)
    )
    grad_normed_two = from_mixer + from_feed + from_experts
    from_norm, grad_regain = jax.vjp(layer_norm, middle, regain)[1](grad_normed_two)
    grad_middle = upstream + from_norm
    grad_attended = grad_middle.astype(bf16)
    grad_mixed = dot_nt(grad_attended, outer).astype(bf16).reshape(length // SEQ, SEQ, HEADS, HEAD)
    attention_low = attention.astype(bf16)
    grad_values = jnp.einsum(
        "bhqk,bqhd->bkhd", attention_low, grad_mixed, preferred_element_type=f32
    )
    grad_attention = jnp.einsum("bqhd,bkhd->bhqk", grad_mixed, values, preferred_element_type=f32)
    grad_scores = (
        attention * (grad_attention - jnp.sum(attention * grad_attention, axis=-1, keepdims=True))
    ).astype(bf16)
    grad_query = (
        jnp.einsum("bhqk,bkhd->bqhd", grad_scores, keys, preferred_element_type=f32) * HEAD**-0.5
    )
    grad_keys = (
        jnp.einsum("bhqk,bqhd->bkhd", grad_scores, query, preferred_element_type=f32) * HEAD**-0.5
    )
    grad_joint = (
        jnp.stack([grad_query, grad_keys, grad_values], axis=2)
        .astype(bf16)
        .reshape(length, 3 * HEADS * HEAD)
    )
    grad_normed = dot_nt(grad_joint, inner)
    from_first, grad_gain = jax.vjp(layer_norm, stream, gain)[1](grad_normed)
    small = jnp.stack([grad_mixer[0], grad_mixer[1], grad_gain, grad_regain])
    return grad_middle + from_first, grad_joint, grad_attended, small


def attention_weights(both, grad_joint, grad_attended):
    c = lax.axis_index("c")
    mine = jnp.concatenate([half_of(grad_joint, c, 1), half_of(grad_attended, c, 1)], axis=1)
    other = jnp.concatenate(
        [half_of(grad_joint, 1 - c, 1), half_of(grad_attended, 1 - c, 1)], axis=1
    )
    columns = jnp.concatenate([mine, swap(other)], axis=0)
    return jnp.concatenate(
        [
            dot_tn(both[:, :1024], columns[:, :1536]).astype(bf16),
            dot_tn(both[:, 1024:], columns[:, 1536:]).astype(bf16),
        ],
        axis=1,
    )


def reduce_gradients(attention, grad_widen, grad_narrow, small):
    c = lax.axis_index("c")
    stacked = grad_narrow.astype(bf16).reshape(16, 32, 2, 512).transpose(0, 2, 1, 3)
    few = jnp.pad(small.astype(bf16).T, ((0, 0), (0, 124)))
    packed = jnp.concatenate(
        [attention, grad_widen.astype(bf16), stacked.reshape(1024, 512), few], axis=1
    )
    summed = lax.psum_scatter(packed, PLANE, scatter_dimension=0, tiled=True)
    columns = summed.shape[1]
    rows = jnp.concatenate([summed[:, :2560], summed[:, 3072:]], axis=1)
    mine, got = half_of(rows, c, 0), swap(half_of(rows, 1 - c, 0))
    few = (mine[:, 2560:].astype(f32) + got[:, 2560:].astype(f32)).astype(bf16)
    inner = in_order(c, mine[:, :1536], got[:, :1536], 1)
    outer = in_order(c, mine[:, 1536:2048], got[:, 1536:2048], 1)
    total = sum_over_z(jnp.concatenate([inner, outer, few], axis=1))
    widen = in_order(c, mine[:, 2048:2560], got[:, 2048:2560], 1)
    narrow = summed[:, 2560:3072]
    narrow = jnp.concatenate([narrow[:32], narrow[32:]], axis=1)
    parts = gather_over_z(jnp.concatenate([widen, narrow], axis=0)).astype(f32)
    widen = parts[:, :32].reshape(4, 32, 2, 16, 32).transpose(1, 3, 2, 0, 4).reshape(32, 4096)
    narrow = parts[:, 32:].reshape(128, 1024)
    few = total[:, 4096:]
    return (
        total[:, :3072],
        total[:, 3072:4096],
        widen,
        narrow,
        few[:, 0:2],
        few[:, 2],
        few[:, 3],
    )


def on_device(
    tokens,
    cotangent,
    routes_first,
    routes_second,
    inner_first,
    outer_first,
    widen_first,
    narrow_first,
    mixer_first,
    gain_first,
    regain_first,
    inner_second,
    outer_second,
    widen_second,
    narrow_second,
    mixer_second,
    gain_second,
    regain_second,
    expand_first,
    reduce_first,
    expand_second,
    reduce_second,
):
    everyone = ("x", "y", "c")
    packed_first = pack_attention(inner_first, outer_first, mixer_first, gain_first, regain_first)
    packed_second = pack_attention(
        inner_second, outer_second, mixer_second, gain_second, regain_second
    )
    gathered_first = lax.all_gather(packed_first, everyone, axis=0, tiled=True)
    packed_feed = jnp.concatenate(
        [pack_feed(widen_first, narrow_first), pack_feed(widen_second, narrow_second)], axis=0
    )
    packed_feed, gathered_first = lax.optimization_barrier((packed_feed, gathered_first))
    gathered_feed = lax.all_gather(packed_feed, PLANE, axis=0)
    packed_second, gathered_feed = lax.optimization_barrier((packed_second, gathered_feed))
    gathered_second = lax.all_gather(packed_second, everyone, axis=0, tiled=True)
    weights_first = unpack_attention(gathered_first)
    weights_second = unpack_attention(gathered_second)
    widen_one, narrow_one = unpack_feed(gathered_feed[:, :64])
    widen_two, narrow_two = unpack_feed(gathered_feed[:, 64:])
    first_table = table_first(routes_first)
    second_table = table_second(routes_second)
    expander, reducer = expand_first[0], reduce_first[0]
    expander_two, reducer_two = expand_second[0], reduce_second[0]

    stream = tokens.astype(f32)
    saved = attention_forward(stream, weights_first)
    normed, _, _, mixed, middle, normed_two, shares = saved
    received = exchange(dot_tn(first_table, normed_two).astype(bf16))
    column = gather_column(normed_two)
    dense_widened, dense_active, dense_terms = feed_forward(column, widen_one, narrow_one)
    dense = scatter_column(dense_terms)
    widened, active, parts = feed_forward(received, expander, reducer)
    expert = dot(first_table, exchange(parts.astype(bf16)))
    own = jnp.concatenate([normed, mixed], axis=1)
    both_first = jnp.concatenate([own, swap(own)], axis=0)
    output = middle + shares[:, 0:1] * dense + shares[:, 1:2] * expert

    upstream = cotangent.astype(f32)
    saved_two = attention_forward(output, weights_second)
    normed, _, _, mixed, middle_two, normed_two, shares_two = saved_two
    grad_dense = (upstream * shares_two[:, 0:1]).astype(bf16)
    grad_expert = (upstream * shares_two[:, 1:2]).astype(bf16)
    arrived = exchange(
        dot_tn(second_table, jnp.concatenate([normed_two, grad_expert], axis=0)).astype(bf16)
    ).reshape(128, 2, 4, 1024)
    column_two = gather_column(jnp.concatenate([normed_two, grad_dense], axis=1))
    rows_two, incoming_two = column_two[:, :1024], column_two[:, 1024:]
    hidden, hidden_active, dense_terms = feed_forward(rows_two, widen_two, narrow_two)
    feed_terms, grad_widen_two, grad_narrow_two = feed_backward(
        rows_two, widen_two, narrow_two, hidden, hidden_active, incoming_two
    )
    summed = scatter_column(jnp.concatenate([dense_terms, feed_terms], axis=1))
    dense_two, from_feed = summed[:, :1024], summed[:, 1024:]
    rows = arrived[:, 0].reshape(512, 1024)
    incoming = arrived[:, 1].reshape(512, 1024)
    hidden, hidden_active, parts = feed_forward(rows, expander_two, reducer_two)
    grad_rows, grad_expand_two, grad_reduce_two = feed_backward(
        rows, expander_two, reducer_two, hidden, hidden_active, incoming
    )
    back = jnp.stack(
        [parts.astype(bf16).reshape(128, 4, 1024), grad_rows.astype(bf16).reshape(128, 4, 1024)],
        axis=1,
    )
    taken = dot(second_table, exchange(back.reshape(1024, 1024)))
    expert_two, from_experts = taken[:128], taken[128:]
    own = jnp.concatenate([normed, mixed], axis=1)
    both_second = jnp.concatenate([own, swap(own)], axis=0)
    output_two = middle_two + shares_two[:, 0:1] * dense_two + shares_two[:, 1:2] * expert_two
    upstream, grad_joint, grad_attended, small = attention_backward(
        output, weights_second, saved_two, upstream, dense_two, expert_two, from_feed, from_experts
    )

    grad_dense = (upstream * shares[:, 0:1]).astype(bf16)
    grad_expert = (upstream * shares[:, 1:2]).astype(bf16)
    incoming = exchange(dot_tn(first_table, grad_expert).astype(bf16))
    feed_incoming = gather_column(grad_dense)
    second_attention = attention_weights(both_second, grad_joint, grad_attended)
    finals_second = reduce_gradients(second_attention, grad_widen_two, grad_narrow_two, small)
    feed_terms, grad_widen_one, grad_narrow_one = feed_backward(
        column, widen_one, narrow_one, dense_widened, dense_active, feed_incoming
    )
    from_feed = scatter_column(feed_terms)
    grad_rows, grad_expand_one, grad_reduce_one = feed_backward(
        received, expander, reducer, widened, active, incoming
    )
    from_experts = dot(first_table, exchange(grad_rows.astype(bf16)))
    gradient_tokens, grad_joint, grad_attended, small = attention_backward(
        stream, weights_first, saved, upstream, dense, expert, from_feed, from_experts
    )
    first_attention = attention_weights(both_first, grad_joint, grad_attended)
    finals_first = reduce_gradients(first_attention, grad_widen_one, grad_narrow_one, small)
    return (
        (output.astype(bf16), output_two.astype(bf16), gradient_tokens)
        + finals_first
        + finals_second
        + (
            grad_expand_one[None],
            grad_reduce_one[None],
            grad_expand_two[None],
            grad_reduce_two[None],
        )
    )


def solution(mesh):
    fine = Mesh(mesh.devices.reshape(4, 4, 4, 2), ALL)
    owner = ("x", "y", "c")
    tokens = P(ALL, None)
    dense = (P(owner, None),) * 5 + (P(owner),) * 2
    experts = (
        P(owner, None, "z"),
        P(owner, "z", None),
        P(ALL, None, None),
        P(ALL, None, None),
    )
    return jax.shard_map(
        on_device,
        mesh=fine,
        in_specs=(tokens,) * 4 + dense + dense + experts,
        out_specs=(tokens,) * 3 + dense + dense + experts,
        check_vma=False,
    )
```

time: 1630 us -> 825 us (0.51)
  waiting for transfers between devices: 705 us -> 291 us
  matrix products: 371 us -> 171 us
  blocking collectives: 183 us -> 0 us
  starting transfers between devices: 131 us -> 98.4 us
  local copies, waits for them, and re-layouts: 145 us -> 175 us
    reduce_scatter x8 -> x2, waiting for transfers between devices: 545 us -> 18.2 us  [reduce_gradients(): summed = lax.psum_scatter(packed, PLANE, scatter_dimension=0, tiled=True)]
    dot_general x124 -> x58, matrix products: 371 us -> 171 us  [the longest x15 55.1 us: dot_tn(): lax.dot_general(a, b, (((0,), (0,)), ((), ())), preferred_element_type=f32)]
    unnamed x2 -> x0, blocking collectives: 133 us -> none
    ppermute x0 -> x44, waiting for transfers between devices: none -> 105 us  [shift(): lax.ppermute(value, axis, [(i, (i + step) % size) for i in range(size)])]
    all_to_all x16 -> x6, starting transfers between devices: 129 us -> 44.7 us  [exchange(): moved = lax.all_to_all(blocks, ALL, split_axis=0, concat_axis=0, tiled=True)]
    ppermute x0 -> x44, starting transfers between devices: none -> 53.2 us  [shift(): lax.ppermute(value, axis, [(i, (i + step) % size) for i in range(size)])]
    all_to_all x24 -> x0, local copies, waits for them, and re-layouts: 46.8 us -> none  [the longest x16 30.7 us: to_owners(): lax.all_to_all(spread, ('dp', 'expert'), split_axis=0, concat_axis=0, til...]
    all_gather x2 -> x0, blocking collectives: 39.1 us -> none  [gather_dense(): lax.all_gather(weights[4], 'expert', axis=0, tiled=True)]
  transfers between devices with their start and end apart: 35 -> 55, of which waited for: 21 -> 25; matrix products, arithmetic and copies ran while one was open for 30% -> 38% of each run, Pallas kernels for 0% -> 0%
where the time goes in v1:
time: 825 us; the launch traced here: 817 us
  waiting for transfers between devices  291 us (35%)
  local copies, waits for them, and re-layouts  175 us (21%)
  matrix products  171 us (21%)
  starting transfers between devices  98.4 us (12%)
  other arithmetic  65.5 us (8%)
  between operations  16.4 us (2%)
    ppermute x44, waiting for transfers between devices, shift(): lax.ppermute(value, axis, [(i, (i + step) % size) for i in range(size)])  105 us
    all_to_all x6, waiting for transfers between devices, exchange(): moved = lax.all_to_all(blocks, ALL, split_axis=0, concat_axis=0, tiled=True)  72 us
    dot_general x15, matrix products, dot_tn(): lax.dot_general(a, b, (((0,), (0,)), ((), ())), preferred_element_type=f32)  55.1 us
    ppermute x44, starting transfers between devices, shift(): lax.ppermute(value, axis, [(i, (i + step) % size) for i in range(size)])  53.2 us
    all_gather x1, waiting for transfers between devices, on_device(): gathered_feed = lax.all_gather(packed_feed, PLANE, axis=0)  52.3 us
    dot_general x17, matrix products, dot(): return jnp.dot(a, b, preferred_element_type=f32)  50.7 us
    dot_general x12, matrix products, dot_nt(): lax.dot_general(a, b, (((1,), (1,)), ((), ())), preferred_element_type=f32)  46.3 us
    all_to_all x6, starting transfers between devices, exchange(): moved = lax.all_to_all(blocks, ALL, split_axis=0, concat_axis=0, tiled=True)  44.7 us
  transfers between devices with their start and end apart: 55, of which 25 were waited for; matrix products, arithmetic and copies ran while one was open for 38% of the time, Pallas kernels for 0%

profile of v1, /device:TPU:0, one launch (start us, length us, event | category | flops | bytes accessed | tf_op | source)
XLA Modules:
  0.0 817.1 jit_solution(11296325411461405521)
XLA Ops:
  16.0 5.0 dynamic-slice_reduce_fusion.1
  24.0 43.4 %all-gather.5.cloned.1.call-done = bf16[1024,4224]{1,0:T(8,128)(2,1)} async-done(((bf16[32,4224]{1,0:T(8,128)(2,1)}), bf16[1024,4224]{1,0:T(8,128)(2,1)}) %all-gather.5.cloned.1.call-update) | async-done | bytes 8650768 | tf_op jit(solution)/shard_map/all_gather | solution.py:320
  69.0 52.3 %all-gather.9.cloned.1.call-done = bf16[2048,1024]{1,0:T(8,128)(2,1)} async-done(((bf16[128,1024]{1,0:T(8,128)(2,1)}), bf16[2048,1024]{1,0:T(8,128)(2,1)}) %all-gather.9.cloned.1.call-update) | async-done | bytes 4194320 | tf_op jit(solution)/shard_map/all_gather | solution.py:325
  149.4 8.8 %all-to-all-start = ((bf16[128,8,1024]{2,1,0:T(8,128)(2,1)}), bf16[128,8,1024]{2,1,0:T(8,128)(2,1)}, u32[]{:S(2)}, u32[]{:S(2)}) async-start(bf16[128,8,1024]{2,1,0:T(8,128)(2,1)} %convert_bitcast_fusion.4), calls=%async_computation | async-start | bytes 4194304 | tf_op jit(solution)/shard_map/all_to_all | solution.py:125
  163.1 14.4 %collective-permute-done.2 = bf16[128,1024]{1,0:T(8,128)(2,1)S(1)} collective-permute-done((bf16[128,1024]{1,0:T(8,128)(2,1)S(1)}, bf16[128,1024]{1,0:T(8,128)(2,1)S(1)}, u32[]{:S(2)}, u32[]{:S(2)}) %collective-permute-start.2) | collective-permute-done | bytes 262176 | tf_op jit(solution)/shard_map/ppermute | solution.py:20
  178.0 11.9 %collective-permute-done.4 = bf16[128,1024]{1,0:T(8,128)(2,1)S(1)} collective-permute-done((bf16[128,1024]{1,0:T(8,128)(2,1)S(1)}, bf16[128,1024]{1,0:T(8,128)(2,1)S(1)}, u32[]{:S(2)}, u32[]{:S(2)}) %collective-permute-start.4) | collective-permute-done | bytes 262176 | tf_op jit(solution)/shard_map/ppermute | solution.py:20
  194.2 8.5 %all-to-all-done = bf16[128,8,1024]{2,1,0:T(8,128)(2,1)} async-done(((bf16[128,8,1024]{2,1,0:T(8,128)(2,1)}), bf16[128,8,1024]{2,1,0:T(8,128)(2,1)}, u32[]{:S(2)}, u32[]{:S(2)}) %all-to-all-start) | async-done | bytes 2097184 | tf_op jit(solution)/shard_map/all_to_all | solution.py:125
  202.8 6.7 fusion.75
  227.8 5.8 all-to-all-start.1
  245.3 18.3 %all-to-all-done.1 = bf16[128,8,1024]{2,1,0:T(8,128)(2,1)} async-done(((bf16[128,8,1024]{2,1,0:T(8,128)(2,1)}), bf16[128,8,1024]{2,1,0:T(8,128)(2,1)}, u32[]{:S(2)}, u32[]{:S(2)}) %all-to-all-start.1) | async-done | bytes 2097184 | tf_op jit(solution)/shard_map/all_to_all | solution.py:125
  263.9 7.3 collective-permute-done.8
  304.2 7.0 all-to-all-start.2
  317.8 30.3 %collective-permute-done.10 = bf16[128,2048]{1,0:T(8,128)(2,1)S(1)} collective-permute-done((bf16[128,2048]{1,0:T(8,128)(2,1)S(1)}, bf16[128,2048]{1,0:T(8,128)(2,1)S(1)}, u32[]{:S(2)}, u32[]{:S(2)}) %collective-permute-start.10) | collective-permute-done | bytes 524320 | tf_op jit(solution)/shard_map/ppermute | solution.py:20
  348.2 11.2 %collective-permute-done.12 = bf16[128,2048]{1,0:T(8,128)(2,1)S(1)} collective-permute-done((bf16[128,2048]{1,0:T(8,128)(2,1)S(1)}, bf16[128,2048]{1,0:T(8,128)(2,1)S(1)}, u32[]{:S(2)}, u32[]{:S(2)}) %collective-permute-start.12) | collective-permute-done | bytes 524320 | tf_op jit(solution)/shard_map/ppermute | solution.py:20
  383.3 5.0 fusion.33
  427.8 7.8 all-to-all-start.3
  437.9 6.1 fusion.257
  457.6 8.0 all-to-all-done.3
  473.5 11.2 %collective-permute-done.17 = bf16[128,2048]{1,0:T(8,128)(2,1)} collective-permute-done((bf16[128,2048]{1,0:T(8,128)(2,1)}, bf16[128,2048]{1,0:T(8,128)(2,1)}, u32[]{:S(2)}, u32[]{:S(2)}) %collective-permute-start.17) | collective-permute-done | bytes 524320 | tf_op jit(solution)/shard_map/ppermute | solution.py:20
  509.3 6.6 multiply_reduce_fusion.3
  543.3 9.6 %all-to-all-start.4 = ((bf16[128,8,1024]{2,1,0:T(8,128)(2,1)}), bf16[128,8,1024]{2,1,0:T(8,128)(2,1)}, u32[]{:S(2)}, u32[]{:S(2)}) async-start(bf16[128,8,1024]{2,1,0:T(8,128)(2,1)} %convert_bitcast_fusion.1), calls=%async_computation.4 | async-start | bytes 4194304 | tf_op jit(solution)/shard_map/all_to_all | solution.py:125
  565.3 24.9 %all-to-all-done.4 = bf16[128,8,1024]{2,1,0:T(8,128)(2,1)} async-done(((bf16[128,8,1024]{2,1,0:T(8,128)(2,1)}), bf16[128,8,1024]{2,1,0:T(8,128)(2,1)}, u32[]{:S(2)}, u32[]{:S(2)}) %all-to-all-start.4) | async-done | bytes 2097184 | tf_op jit(solution)/shard_map/all_to_all | solution.py:125
  590.2 7.2 fusion.16
  602.4 5.8 all-to-all-start.5
  631.8 12.4 %all-to-all-done.5 = bf16[128,8,1024]{2,1,0:T(8,128)(2,1)} async-done(((bf16[128,8,1024]{2,1,0:T(8,128)(2,1)}), bf16[128,8,1024]{2,1,0:T(8,128)(2,1)}, u32[]{:S(2)}, u32[]{:S(2)}) %all-to-all-start.5) | async-done | bytes 2097184 | tf_op jit(solution)/shard_map/all_to_all | solution.py:125
  674.3 5.1 fusion.166
  693.9 7.8 convolution_bitcast_fusion.1
  701.7 6.3 convolution_bitcast_fusion
  708.0 6.1 convolution_bitcast_fusion.3
  714.2 7.0 convolution_bitcast_fusion.2
  754.4 18.2 %reduce-scatter.3.cloned.1.call-done = bf16[64,3200]{1,0:T(8,128)(2,1)} async-done(((bf16[1024,3200]{1,0:T(8,128)(2,1)}), bf16[64,3200]{1,0:T(8,128)(2,1)}) %reduce-scatter.3.cloned.1.call-update) | async-done | bytes 409616 | tf_op jit(solution)/shard_map/reduce_scatter | solution.py:265
  784.6 6.0 collective-permute-done.32
  (726 shorter events, 408.8 us)
Async XLA Ops:
  7.2 60.2 %all-gather.5.cloned.1.call-start = ((), (), s32[]{:S(2)}) async-start(), calls=%async_computation.8 | async-start | bytes 8921088 | tf_op jit(solution)/shard_map/all_gather | solution.py:320
  11.4 109.8 %all-gather.9.cloned.1.call-start = ((), (), s32[]{:S(2)}) async-start(), calls=%async_computation.12 | async-start | bytes 4456448 | tf_op jit(solution)/shard_map/all_gather | solution.py:325
  67.5 208.1 %all-gather.7.cloned.1.call-start = ((), (), s32[]{:S(2)}) async-start(), calls=%async_computation.9 | async-start | bytes 8921088 | tf_op jit(solution)/shard_map/all_gather | solution.py:327
  149.4 53.4 %all-to-all-start = ((bf16[128,8,1024]{2,1,0:T(8,128)(2,1)}), bf16[128,8,1024]{2,1,0:T(8,128)(2,1)}, u32[]{:S(2)}, u32[]{:S(2)}) async-start(bf16[128,8,1024]{2,1,0:T(8,128)(2,1)} %convert_bitcast_fusion.4), calls=%async_computation | async-start | bytes 4194304 | tf_op jit(solution)/shard_map/all_to_all | solution.py:125
  158.2 19.2 %collective-permute-start.2 = (bf16[128,1024]{1,0:T(8,128)(2,1)S(1)}, bf16[128,1024]{1,0:T(8,128)(2,1)S(1)}, u32[]{:S(2)}, u32[]{:S(2)}) collective-permute-start(bf16[128,1024]{1,0:T(8,128)(2,1)S(1)} %get-tuple-element.186), channel_id=1, source_target_pairs={{0,32},{32,64},{64,96},{96,0},{1,33},{33,65},{65,97},{97,1},{2,34}... | collective-permute-start | bytes 786440 | tf_op jit(solution)/shard_map/ppermute | solution.py:20
  159.3 18.7 %collective-permute-start.3 = (bf16[128,1024]{1,0:T(8,128)(2,1)S(1)}, bf16[128,1024]{1,0:T(8,128)(2,1)S(1)}, u32[]{:S(2)}, u32[]{:S(2)}) collective-permute-start(bf16[128,1024]{1,0:T(8,128)(2,1)S(1)} %get-tuple-element.186), channel_id=1, source_target_pairs={{0,96},{32,0},{64,32},{96,64},{1,97},{33,1},{65,33},{97,65},{2,98}... | collective-permute-start | bytes 786440 | tf_op jit(solution)/shard_map/ppermute | solution.py:20
  161.5 28.3 %collective-permute-start.4 = (bf16[128,1024]{1,0:T(8,128)(2,1)S(1)}, bf16[128,1024]{1,0:T(8,128)(2,1)S(1)}, u32[]{:S(2)}, u32[]{:S(2)}) collective-permute-start(bf16[128,1024]{1,0:T(8,128)(2,1)S(1)} %get-tuple-element.186), channel_id=1, source_target_pairs={{0,64},{32,96},{64,0},{96,32},{1,65},{33,97},{65,1},{97,33},{2,66}... | collective-permute-start | bytes 786440 | tf_op jit(solution)/shard_map/ppermute | solution.py:20
  227.8 35.8 %all-to-all-start.1 = ((bf16[128,8,1024]{2,1,0:T(8,128)(2,1)}), bf16[128,8,1024]{2,1,0:T(8,128)(2,1)}, u32[]{:S(2)}, u32[]{:S(2)}) async-start(bf16[128,8,1024]{2,1,0:T(8,128)(2,1)} %convert_bitcast_fusion.3), calls=%async_computation.1 | async-start | bytes 4194304 | tf_op jit(solution)/shard_map/all_to_all | solution.py:125
  240.3 23.6 %collective-permute-start.7 = (bf16[128,1024]{1,0:T(8,128)(2,1)}, bf16[128,1024]{1,0:T(8,128)(2,1)S(1)}, u32[]{:S(2)}, u32[]{:S(2)}) collective-permute-start(bf16[128,1024]{1,0:T(8,128)(2,1)} %get-tuple-element.210), channel_id=1, source_target_pairs={{0,96},{32,0},{64,32},{96,64},{1,97},{33,1},{65,33},{97,65},{2,98}... | collective-permute-start | bytes 786440 | tf_op jit(solution)/shard_map/ppermute | solution.py:20
  243.0 28.2 %collective-permute-start.8 = (bf16[128,1024]{1,0:T(8,128)(2,1)}, bf16[128,1024]{1,0:T(8,128)(2,1)S(1)}, u32[]{:S(2)}, u32[]{:S(2)}) collective-permute-start(bf16[128,1024]{1,0:T(8,128)(2,1)} %get-tuple-element.212), channel_id=1, source_target_pairs={{0,32},{32,64},{64,96},{96,0},{1,33},{33,65},{65,97},{97,1},{2,34}... | collective-permute-start | bytes 786440 | tf_op jit(solution)/shard_map/ppermute | solution.py:20
  243.0 28.2 %collective-permute-start.9 = (bf16[128,1024]{1,0:T(8,128)(2,1)}, bf16[128,1024]{1,0:T(8,128)(2,1)S(1)}, u32[]{:S(2)}, u32[]{:S(2)}) collective-permute-start(bf16[128,1024]{1,0:T(8,128)(2,1)} %get-tuple-element.211), channel_id=1, source_target_pairs={{0,64},{32,96},{64,0},{96,32},{1,65},{33,97},{65,1},{97,33},{2,66}... | collective-permute-start | bytes 786440 | tf_op jit(solution)/shard_map/ppermute | solution.py:20
  304.2 67.1 %all-to-all-start.2 = ((bf16[128,8,1024]{2,1,0:T(8,128)(2,1)}), bf16[128,8,1024]{2,1,0:T(8,128)(2,1)}, u32[]{:S(2)}, u32[]{:S(2)}) async-start(bf16[128,8,1024]{2,1,0:T(8,128)(2,1)} %convert_bitcast_fusion.2), calls=%async_computation.2 | async-start | bytes 4194304 | tf_op jit(solution)/shard_map/all_to_all | solution.py:125
  313.0 35.1 %collective-permute-start.10 = (bf16[128,2048]{1,0:T(8,128)(2,1)S(1)}, bf16[128,2048]{1,0:T(8,128)(2,1)S(1)}, u32[]{:S(2)}, u32[]{:S(2)}) collective-permute-start(bf16[128,2048]{1,0:T(8,128)(2,1)S(1)} %get-tuple-element.218), channel_id=1, source_target_pairs={{0,32},{32,64},{64,96},{96,0},{1,33},{33,65},{65,97},{97,1},{2,34}... | collective-permute-start | bytes 1572872 | tf_op jit(solution)/shard_map/ppermute | solution.py:20
  314.0 34.1 %collective-permute-start.11 = (bf16[128,2048]{1,0:T(8,128)(2,1)S(1)}, bf16[128,2048]{1,0:T(8,128)(2,1)S(1)}, u32[]{:S(2)}, u32[]{:S(2)}) collective-permute-start(bf16[128,2048]{1,0:T(8,128)(2,1)S(1)} %get-tuple-element.218), channel_id=1, source_target_pairs={{0,96},{32,0},{64,32},{96,64},{1,97},{33,1},{65,33},{97,65},{2,98}... | collective-permute-start | bytes 1572872 | tf_op jit(solution)/shard_map/ppermute | solution.py:20
  316.3 43.1 %collective-permute-start.12 = (bf16[128,2048]{1,0:T(8,128)(2,1)S(1)}, bf16[128,2048]{1,0:T(8,128)(2,1)S(1)}, u32[]{:S(2)}, u32[]{:S(2)}) collective-permute-start(bf16[128,2048]{1,0:T(8,128)(2,1)S(1)} %get-tuple-element.218), channel_id=1, source_target_pairs={{0,64},{32,96},{64,0},{96,32},{1,65},{33,97},{65,1},{97,33},{2,66}... | collective-permute-start | bytes 1572872 | tf_op jit(solution)/shard_map/ppermute | solution.py:20
  362.0 26.4 %collective-permute-start.13 = (bf16[512,2048]{1,0:T(8,128)(2,1)}, bf16[512,2048]{1,0:T(8,128)(2,1)}, u32[]{:S(2)}, u32[]{:S(2)}) collective-permute-start(bf16[512,2048]{1,0:T(8,128)(2,1)} %pad_maximum_fusion.1), channel_id=1, source_target_pairs={{0,1},{1,0},{2,3},{3,2},{4,5},{5,4},{6,7},{7,6},{8,9},{9,8},{10,11... | collective-permute-start | bytes 6291464 | tf_op jit(solution)/shard_map/ppermute | solution.py:20
  368.2 67.4 %collective-permute-start.35 = (bf16[128,2048]{1,0:T(8,128)(2,1)}, bf16[128,2048]{1,0:T(8,128)(2,1)}, u32[]{:S(2)}, u32[]{:S(2)}) collective-permute-start(bf16[128,2048]{1,0:T(8,128)(2,1)} %pad_maximum_fusion.14), channel_id=1, source_target_pairs={{0,1},{1,0},{2,3},{3,2},{4,5},{5,4},{6,7},{7,6},{8,9},{9,8},{10,11... | collective-permute-start | bytes 1572872 | tf_op jit(solution)/shard_map/ppermute | solution.py:20
  403.0 34.9 %collective-permute-start.14 = (bf16[512,2048]{1,0:T(8,128)(2,1)}, bf16[512,2048]{1,0:T(8,128)(2,1)}, u32[]{:S(2)}, u32[]{:S(2)}) collective-permute-start(bf16[512,2048]{1,0:T(8,128)(2,1)} %fusion.26), channel_id=1, source_target_pairs={{0,1},{1,0},{2,3},{3,2},{4,5},{5,4},{6,7},{7,6},{8,9},{9,8},{10,11... | collective-permute-start | bytes 6291464 | tf_op jit(solution)/shard_map/ppermute | solution.py:20
  427.8 37.7 %all-to-all-start.3 = ((bf16[128,8,1024]{2,1,0:T(8,128)(2,1)}), bf16[128,8,1024]{2,1,0:T(8,128)(2,1)}, u32[]{:S(2)}, u32[]{:S(2)}) async-start(bf16[128,8,1024]{2,1,0:T(8,128)(2,1)} %copy.336), calls=%async_computation.3 | async-start | bytes 4194304 | tf_op jit(solution)/shard_map/all_to_all | solution.py:125
  435.6 286.8 %reduce-scatter.5.cloned.1.call-start = ((), (), s32[]{:S(2)}) async-start(), calls=%async_computation.11 | async-start | bytes 6963200 | tf_op jit(solution)/shard_map/reduce_scatter | solution.py:265
  445.2 26.5 %collective-permute-start.15 = (bf16[128,2048]{1,0:T(8,128)(2,1)}, bf16[128,2048]{1,0:T(8,128)(2,1)}, u32[]{:S(2)}, u32[]{:S(2)}) collective-permute-start(bf16[128,2048]{1,0:T(8,128)(2,1)} %get-tuple-element.192), channel_id=1, source_target_pairs={{0,96},{32,0},{64,32},{96,64},{1,97},{33,1},{65,33},{97,65},{2,98}... | collective-permute-start | bytes 1572872 | tf_op jit(solution)/shard_map/ppermute | solution.py:20
  448.0 25.5 %collective-permute-start.16 = (bf16[128,2048]{1,0:T(8,128)(2,1)}, bf16[128,2048]{1,0:T(8,128)(2,1)}, u32[]{:S(2)}, u32[]{:S(2)}) collective-permute-start(bf16[128,2048]{1,0:T(8,128)(2,1)} %get-tuple-element.194), channel_id=1, source_target_pairs={{0,32},{32,64},{64,96},{96,0},{1,33},{33,65},{65,97},{97,1},{2,34}... | collective-permute-start | bytes 1572872 | tf_op jit(solution)/shard_map/ppermute | solution.py:20
  448.0 36.7 %collective-permute-start.17 = (bf16[128,2048]{1,0:T(8,128)(2,1)}, bf16[128,2048]{1,0:T(8,128)(2,1)}, u32[]{:S(2)}, u32[]{:S(2)}) collective-permute-start(bf16[128,2048]{1,0:T(8,128)(2,1)} %get-tuple-element.193), channel_id=1, source_target_pairs={{0,64},{32,96},{64,0},{96,32},{1,65},{33,97},{65,1},{97,33},{2,66}... | collective-permute-start | bytes 1572872 | tf_op jit(solution)/shard_map/ppermute | solution.py:20
  543.3 46.9 %all-to-all-start.4 = ((bf16[128,8,1024]{2,1,0:T(8,128)(2,1)}), bf16[128,8,1024]{2,1,0:T(8,128)(2,1)}, u32[]{:S(2)}, u32[]{:S(2)}) async-start(bf16[128,8,1024]{2,1,0:T(8,128)(2,1)} %convert_bitcast_fusion.1), calls=%async_computation.4 | async-start | bytes 4194304 | tf_op jit(solution)/shard_map/all_to_all | solution.py:125
  602.4 41.8 %all-to-all-start.5 = ((bf16[128,8,1024]{2,1,0:T(8,128)(2,1)}), bf16[128,8,1024]{2,1,0:T(8,128)(2,1)}, u32[]{:S(2)}, u32[]{:S(2)}) async-start(bf16[128,8,1024]{2,1,0:T(8,128)(2,1)} %convert_bitcast_fusion), calls=%async_computation.5 | async-start | bytes 4194304 | tf_op jit(solution)/shard_map/all_to_all | solution.py:125
  608.2 164.4 %reduce-scatter.3.cloned.1.call-start = ((), (), s32[]{:S(2)}) async-start(), calls=%async_computation.10 | async-start | bytes 6963200 | tf_op jit(solution)/shard_map/reduce_scatter | solution.py:265
  626.8 19.8 %collective-permute-start.23 = (bf16[128,1024]{1,0:T(8,128)(2,1)}, bf16[128,1024]{1,0:T(8,128)(2,1)S(1)}, u32[]{:S(2)}, u32[]{:S(2)}) collective-permute-start(bf16[128,1024]{1,0:T(8,128)(2,1)} %get-tuple-element.207), channel_id=1, source_target_pairs={{0,96},{32,0},{64,32},{96,64},{1,97},{33,1},{65,33},{97,65},{2,98}... | collective-permute-start | bytes 786440 | tf_op jit(solution)/shard_map/ppermute | solution.py:20
  629.6 20.7 %collective-permute-start.24 = (bf16[128,1024]{1,0:T(8,128)(2,1)}, bf16[128,1024]{1,0:T(8,128)(2,1)}, u32[]{:S(2)}, u32[]{:S(2)}) collective-permute-start(bf16[128,1024]{1,0:T(8,128)(2,1)} %get-tuple-element.209), channel_id=1, source_target_pairs={{0,32},{32,64},{64,96},{96,0},{1,33},{33,65},{65,97},{97,1},{2,34}... | collective-permute-start | bytes 786440 | tf_op jit(solution)/shard_map/ppermute | solution.py:20
  629.8 20.5 %collective-permute-start.25 = (bf16[128,1024]{1,0:T(8,128)(2,1)}, bf16[128,1024]{1,0:T(8,128)(2,1)}, u32[]{:S(2)}, u32[]{:S(2)}) collective-permute-start(bf16[128,1024]{1,0:T(8,128)(2,1)} %get-tuple-element.208), channel_id=1, source_target_pairs={{0,64},{32,96},{64,0},{96,32},{1,65},{33,97},{65,1},{97,33},{2,66}... | collective-permute-start | bytes 786440 | tf_op jit(solution)/shard_map/ppermute | solution.py:20
  728.7 20.3 %collective-permute-start.38 = (bf16[32,4224]{1,0:T(8,128)(2,1)}, bf16[32,4224]{1,0:T(8,128)(2,1)S(1)}, u32[]{:S(2)}, u32[]{:S(2)}) collective-permute-start(bf16[32,4224]{1,0:T(8,128)(2,1)} %pad_maximum_fusion.17), channel_id=1, source_target_pairs={{0,64},{32,96},{64,0},{96,32},{1,65},{33,97},{65,1},{97,33},{2,66}... | collective-permute-start | bytes 811016 | tf_op jit(solution)/shard_map/ppermute | solution.py:20
  781.3 25.1 %collective-permute-start.29 = (bf16[32,4224]{1,0:T(8,128)(2,1)}, bf16[32,4224]{1,0:T(8,128)(2,1)S(1)}, u32[]{:S(2)}, u32[]{:S(2)}) collective-permute-start(bf16[32,4224]{1,0:T(8,128)(2,1)} %pad_maximum_fusion.16), channel_id=1, source_target_pairs={{0,64},{32,96},{64,0},{96,32},{1,65},{33,97},{65,1},{97,33},{2,66}... | collective-permute-start | bytes 811016 | tf_op jit(solution)/shard_map/ppermute | solution.py:20
  783.2 23.3 %collective-permute-start.30 = (bf16[32,4224]{1,0:T(8,128)(2,1)}, bf16[32,4224]{1,0:T(8,128)(2,1)S(1)}, u32[]{:S(2)}, u32[]{:S(2)}) collective-permute-start(bf16[32,4224]{1,0:T(8,128)(2,1)} %pad_maximum_fusion.16), channel_id=1, source_target_pairs={{0,32},{32,64},{64,96},{96,0},{1,33},{33,65},{65,97},{97,1},{2,34}... | collective-permute-start | bytes 811016 | tf_op jit(solution)/shard_map/ppermute | solution.py:20
  (197 other events, 1974.3 us)
Sparse Core Ops, SparseCore 0:
  11.6 55.8 all-gather.4
  70.2 51.0 all-gather.8
  124.1 75.2 all-gather.6
  534.0 106.5 reduce-scatter.4
  694.0 78.5 reduce-scatter.2

commit v2 on v1

v2 whole, which is shorter than its diff:
```python
import jax
import jax.numpy as jnp
from jax import lax
from jax.experimental import pallas as pl
from jax.experimental.pallas import tpu as pltpu
from jax.sharding import Mesh, PartitionSpec as P

HEADS = 16
HEAD = 64
SEQ = 64
ROWS = 128
D = 1024
PACKED = 4224
SCALE = HEAD**-0.5
ALL = ("z", "x", "y", "c")
PLANE = ("x", "y")
COLUMN = ("z", "c")
SIZES = {"z": 4, "x": 4, "y": 4, "c": 2}
epsilon = 1e-05
bf16 = jnp.bfloat16
f32 = jnp.float32
LIMIT = 56 * 1024 * 1024


def shift(value, axis, step):
    size = SIZES[axis]
    return lax.ppermute(value, axis, [(i, (i + step) % size) for i in range(size)])


def swap(value):
    return shift(value, "c", 1)


def flip(value):
    return lax.ppermute(value, "z", [(0, 1), (1, 0), (2, 3), (3, 2)])


def dot(a, b):
    return jnp.dot(a, b, preferred_element_type=f32)


def dot_tn(a, b):
    return lax.dot_general(a, b, (((0,), (0,)), ((), ())), preferred_element_type=f32)


def dot_nt(a, b):
    return lax.dot_general(a, b, (((1,), (1,)), ((), ())), preferred_element_type=f32)


def in_order(core, mine, twin, axis):
    return jnp.where(
        core == 0,
        jnp.concatenate([mine, twin], axis=axis),
        jnp.concatenate([twin, mine], axis=axis),
    )


def half_of(value, which, axis):
    size = value.shape[axis] // 2
    return lax.dynamic_slice_in_dim(value, which * size, size, axis)


def shape(*dims, dtype=bf16):
    return jax.ShapeDtypeStruct(dims, dtype)


def whole():
    return pl.BlockSpec(memory_space=pltpu.VMEM)


def space_of(value):
    if value.dtype == jnp.int32 and value.ndim == 1:
        return pl.BlockSpec(memory_space=pltpu.SMEM)
    return whole()


def call(body, outs, args, flops, moved, far=(), scratch=(), name=None):
    return pl.pallas_call(
        body,
        out_shape=outs,
        in_specs=[
            pl.BlockSpec(memory_space=pl.ANY) if i in far else space_of(arg)
            for i, arg in enumerate(args)
        ],
        out_specs=[whole()] * len(outs),
        scratch_shapes=list(scratch),
        compiler_params=pltpu.CompilerParams(vmem_limit_bytes=LIMIT),
        cost_estimate=pl.CostEstimate(flops=flops, bytes_accessed=moved, transcendentals=0),
        name=name,
    )(*args)


def start_weights(far, near, sems, base):
    copies = []
    for i, low, high in ((4, 4096, 4224), (0, 0, D), (1, D, 2 * D), (2, 2 * D, 3 * D), (3, 3 * D, 4096)):
        copy = pltpu.make_async_copy(
            far.at[:, base + low : base + high], near.at[:, low:high], sems.at[i]
        )
        copy.start()
        copies.append(copy)
    return copies


WEIGHTS = (pltpu.VMEM((D, PACKED), bf16), pltpu.SemaphoreType.DMA((5,)))


def vector_rows(near):
    pick = lax.broadcasted_iota(jnp.int32, (8, 128), 0) == lax.broadcasted_iota(
        jnp.int32, (8, 128), 1
    )
    return dot_nt(pick.astype(bf16), near[:, 4096:4224])


def normalize(values):
    center = values - jnp.mean(values, axis=-1, keepdims=True)
    spread = jnp.mean(center * center, axis=-1, keepdims=True)
    inverse = lax.rsqrt(spread + epsilon)
    return center * inverse, inverse


def normalize_backward(hat, inverse, gradient):
    return inverse * (
        gradient
        - jnp.mean(gradient, axis=-1, keepdims=True)
        - hat * jnp.mean(gradient * hat, axis=-1, keepdims=True)
    )


def lane_half(rows=ROWS):
    return lax.broadcasted_iota(jnp.int32, (rows, 128), 1) < HEAD


def split_heads(pair):
    first = lane_half()
    blank = jnp.zeros_like(pair)
    return jnp.concatenate([jnp.where(first, pair, blank), jnp.where(first, blank, pair)], axis=0)


def own_sequence(table):
    first = lane_half(SEQ)
    return [
        jnp.where(first, table[low : low + SEQ], table[low + SEQ : low + 2 * SEQ])
        for low in (0, ROWS)
    ]


def spread_sequences(blocks):
    first = lane_half(SEQ)
    parts = []
    for block in blocks:
        parts += [jnp.where(first, block, 0.0), jnp.where(first, 0.0, block)]
    return jnp.concatenate(parts, axis=0).astype(bf16)


def attention_of(query, keys):
    key = lax.broadcasted_iota(jnp.int32, (SEQ, ROWS), 0)
    place = jnp.bitwise_and(lax.broadcasted_iota(jnp.int32, (SEQ, ROWS), 1), SEQ - 1)
    result = []
    for scores in own_sequence(dot_nt(split_heads(keys), query) * SCALE):
        scores = jnp.where(key <= place, scores, -1e30)
        raised = jnp.exp(scores - jnp.max(scores, axis=0, keepdims=True))
        result.append(raised / jnp.sum(raised, axis=0, keepdims=True))
    return result


def pair_of(ref, part, pair):
    return ref[:, pl.ds(pl.multiple_of(part * D + pair * 128, 128), 128)]


def front(stream, near, copies, normed_out, joint_out, mixed_out, middle_out, two_out, share_out):
    copies[0].wait()
    vectors = vector_rows(near)
    hat, _ = normalize(stream)
    normed = (hat * vectors[2:3]).astype(bf16)
    normed_out[...] = normed
    for part in range(3):
        copies[part + 1].wait()
        for low in range(part * D, part * D + D, 512):
            joint_out[:, low : low + 512] = dot(normed, near[:, low : low + 512]).astype(bf16)

    @pl.loop(0, HEADS // 2, unroll=True)
    def _(pair):
        query, keys, values = (pair_of(joint_out, part, pair) for part in range(3))
        table = spread_sequences(attention_of(query, keys))
        one = dot_tn(table[0:ROWS], values)
        two = dot_tn(table[ROWS : 2 * ROWS], values)
        column = pl.ds(pl.multiple_of(pair * 128, 128), 128)
        mixed_out[:, column] = jnp.where(lane_half(), one, two).astype(bf16)

    mixed = mixed_out[...]
    copies[4].wait()
    for low in range(0, D, 512):
        middle_out[:, low : low + 512] = stream[:, low : low + 512] + dot(
            mixed, near[:, 3072 + low : 3072 + low + 512]
        )
    hat, _ = normalize(middle_out[...])
    normed_two = (hat * vectors[3:4]).astype(bf16)
    two_out[...] = normed_two
    logits = dot(normed_two, near[:, 4096:4224])
    one, two = logits[:, 0:1], logits[:, 1:2]
    top = jnp.maximum(one, two)
    one, two = jnp.exp(one - top), jnp.exp(two - top)
    total = one + two
    one, two = one / total, two / total
    lane = lax.broadcasted_iota(jnp.int32, (ROWS, 128), 1)
    share_out[...] = jnp.where(lane == 0, one, two)
    return normed_two, one, two


def send_first(rows, slot_row, out):
    slots = lax.broadcasted_iota(jnp.int32, (256, ROWS), 0)
    table = (slots == slot_row[...]).astype(bf16)
    buffer = dot(table, rows).astype(bf16)
    for z in range(4):
        out[z * 256 : (z + 1) * 256, :] = buffer


def send_second(rows, grads, slot_row, out):
    slots = lax.broadcasted_iota(jnp.int32, (256, ROWS), 0)
    for group in range(2):
        wanted = slot_row[...] - group * 256
        buffer = dot((slots == wanted).astype(bf16), rows) + dot(
            (slots == wanted + 4).astype(bf16), grads
        )
        buffer = buffer.astype(bf16)
        for z in (2 * group, 2 * group + 1):
            out[z * 256 : (z + 1) * 256, :] = buffer


def take_first(back, slot_column):
    column = lax.broadcasted_iota(jnp.int32, (ROWS, 1024), 1)
    table = (slot_column[...] == jnp.bitwise_and(column, 255)).astype(bf16)
    return dot(table, back[...])


def take_second(back, slot_column):
    column = lax.broadcasted_iota(jnp.int32, (ROWS, 1024), 1)
    place = jnp.where(column >= 512, 256, 0) + jnp.bitwise_and(column, 255)
    rows = dot((slot_column[...] == place).astype(bf16), back[...])
    grads = dot((slot_column[...] + 4 == place).astype(bf16), back[...])
    return rows, grads


def backward(
    stream,
    near,
    copies,
    joint_ref,
    middle,
    normed_two,
    one,
    two,
    upstream,
    dense,
    expert,
    incoming,
    joint_out,
    attended_out,
    small_out,
    mixed_ref,
):
    copies[0].wait()
    vectors = vector_rows(near)
    first = jnp.sum(upstream * dense, axis=1, keepdims=True)
    second = jnp.sum(upstream * expert, axis=1, keepdims=True)
    both = one * first + two * second
    first, second = one * (first - both), two * (second - both)
    normed_two = normed_two.astype(f32)
    gradient = first * vectors[0:1] + second * vectors[1:2] + incoming
    hat, inverse = normalize(middle)
    small_out[0:1, :] = jnp.sum(normed_two * first, axis=0, keepdims=True)
    small_out[1:2, :] = jnp.sum(normed_two * second, axis=0, keepdims=True)
    small_out[3:4, :] = jnp.sum(gradient * hat, axis=0, keepdims=True)
    small_out[4:8, :] = jnp.zeros((4, D), f32)
    grad_middle = upstream + normalize_backward(hat, inverse, gradient * vectors[3:4])
    attended = grad_middle.astype(bf16)
    attended_out[...] = attended
    copies[4].wait()
    for low in range(0, D, 512):
        mixed_ref[:, low : low + 512] = dot_nt(attended, near[low : low + 512, 3072:4096]).astype(
            bf16
        )

    @pl.loop(0, HEADS // 2, unroll=True)
    def _(pair):
        query, keys, values = (pair_of(joint_ref, part, pair) for part in range(3))
        column = pl.ds(pl.multiple_of(pair * 128, 128), 128)
        grad_mixed = mixed_ref[:, column]
        attention = attention_of(query, keys)
        grad_attention = own_sequence(dot_nt(split_heads(values), grad_mixed))
        grad_scores = [
            weight * (grad - jnp.sum(weight * grad, axis=0, keepdims=True))
            for weight, grad in zip(attention, grad_attention)
        ]
        grad_scores = spread_sequences(grad_scores)
        grad_keys = dot(grad_scores, query) * SCALE
        grad_values = dot(spread_sequences(attention), grad_mixed)
        halves = (
            (
                dot_tn(grad_scores[0:ROWS], keys) * SCALE,
                dot_tn(grad_scores[ROWS : 2 * ROWS], keys) * SCALE,
            ),
            (grad_keys[0:ROWS], grad_keys[ROWS : 2 * ROWS]),
            (grad_values[0:ROWS], grad_values[ROWS : 2 * ROWS]),
        )
        for part in range(3):
            place = pl.ds(pl.multiple_of(part * D + pair * 128, 128), 128)
            joint_out[:, place] = jnp.where(lane_half(), *halves[part]).astype(bf16)

    for copy in copies[1:4]:
        copy.wait()
    parts = []
    for low in range(0, D, 256):
        parts.append(dot_nt(joint_out[...], near[low : low + 256, 0:3072]))
    grad_normed = jnp.concatenate(parts, axis=1)
    hat, inverse = normalize(stream)
    small_out[2:3, :] = jnp.sum(grad_normed * hat, axis=0, keepdims=True)
    return grad_middle + normalize_backward(hat, inverse, grad_normed * vectors[2:3])


def halves_of(pair):
    return pair.at[:, 0:D], pair.at[:, D : 2 * D]


def first_front(tokens, weights, slot_row):
    def body(tokens, far, slot_row, pair, joint, middle, two, shares, send, near, sems):
        copies = start_weights(far, near, sems, 0)
        normed, mixed = halves_of(pair)
        rows, _, _ = front(
            tokens[...].astype(f32), near, copies, normed, joint, mixed, middle, two, shares
        )
        send_first(rows, slot_row, send)

    outs = (
        shape(ROWS, 2 * D),
        shape(ROWS, 3 * D),
        shape(ROWS, D, dtype=f32),
        shape(ROWS, D),
        shape(ROWS, 128, dtype=f32),
        shape(1024, D),
    )
    args = (tokens, weights, slot_row)
    return call(body, outs, args, 1300000000, 14000000, far=(1,), scratch=WEIGHTS, name="front")


def second_front(back, slot_column, middle, shares, own, parts, cotangent, weights, slot_row):
    def body(
        back,
        slot_column,
        middle,
        shares,
        own,
        part_a,
        part_b,
        part_c,
        cotangent,
        far,
        slot_row,
        low_out,
        stream_out,
        dense_out,
        expert_out,
        pair,
        joint,
        middle_out,
        feed,
        shares_out,
        send,
        near,
        sems,
    ):
        copies = start_weights(far, near, sems, PACKED)
        expert = take_first(back, slot_column)
        dense = own[...] + part_a[...].astype(f32) + part_b[...].astype(f32) + part_c[...].astype(f32)
        dense_out[...] = dense
        expert_out[...] = expert
        stream = middle[...] + shares[:, 0:1] * dense + shares[:, 1:2] * expert
        stream_out[...] = stream
        low_out[...] = stream.astype(bf16)
        normed, mixed = halves_of(pair)
        two, grad_dense = halves_of(feed)
        rows, one, other = front(
            stream, near, copies, normed, joint, mixed, middle_out, two, shares_out
        )
        upstream = cotangent[...].astype(f32)
        grad_dense[...] = (upstream * one).astype(bf16)
        send_second(rows, (upstream * other).astype(bf16), slot_row, send)

    outs = (
        shape(ROWS, D),
        shape(ROWS, D, dtype=f32),
        shape(ROWS, D, dtype=f32),
        shape(ROWS, D, dtype=f32),
        shape(ROWS, 2 * D),
        shape(ROWS, 3 * D),
        shape(ROWS, D, dtype=f32),
        shape(ROWS, 2 * D),
        shape(ROWS, 128, dtype=f32),
        shape(1024, D),
    )
    args = (back, slot_column, middle, shares, own, *parts, cotangent, weights, slot_row)
    return call(body, outs, args, 1800000000, 20000000, far=(9,), scratch=WEIGHTS, name="between")


BACK = WEIGHTS + (
    pltpu.VMEM((ROWS, D), bf16),
    pltpu.VMEM((ROWS, 3 * D), bf16),
    pltpu.VMEM((ROWS, D), bf16),
)


def second_back(
    place,
    back,
    slot_column,
    cotangent,
    middle,
    shares,
    own,
    got,
    flipped,
    feed,
    joint,
    stream,
    weights,
    first_shares,
    slot_row,
):
    def body(
        place,
        back,
        slot_column,
        cotangent,
        middle,
        shares,
        own,
        got,
        flipped,
        feed,
        joint,
        stream,
        far,
        first_shares,
        slot_row,
        low_out,
        grad_out,
        mine,
        other,
        small_out,
        grad_dense,
        send,
        near,
        sems,
        mixed,
        joint_grad,
        attended,
    ):
        copies = start_weights(far, near, sems, PACKED)
        expert, from_experts = take_second(back, slot_column)
        total = own[0:ROWS, :] + got[0:ROWS, :].astype(f32) + flipped[...].astype(f32)
        dense, from_feed = total[:, 0:D], total[:, D : 2 * D]
        one, two = shares[:, 0:1], shares[:, 1:2]
        low_out[...] = (middle[...] + one * dense + two * expert).astype(bf16)
        gradient = backward(
            stream[...],
            near,
            copies,
            joint,
            middle[...],
            feed[:, 0:D],
            one,
            two,
            cotangent[...].astype(f32),
            dense,
            expert,
            from_feed + from_experts,
            joint_grad,
            attended,
            small_out,
            mixed,
        )
        grad_out[...] = gradient
        grad_dense[...] = (gradient * first_shares[:, 0:1]).astype(bf16)
        send_first((gradient * first_shares[:, 1:2]).astype(bf16), slot_row, send)
        for out, core in ((mine, place[1]), (other, 1 - place[1])):
            wide = pl.multiple_of(core * 1536, 128)
            out[:, 0:1536] = joint_grad[:, pl.ds(wide, 1536)]
            out[:, 1536:2048] = attended[:, pl.ds(pl.multiple_of(core * 512, 128), 512)]

    outs = (
        shape(ROWS, D),
        shape(ROWS, D, dtype=f32),
        shape(ROWS, 2048),
        shape(ROWS, 2048),
        shape(8, D, dtype=f32),
        shape(ROWS, D),
        shape(1024, D),
    )
    args = (
        place,
        back,
        slot_column,
        cotangent,
        middle,
        shares,
        own,
        got,
        flipped,
        feed,
        joint,
        stream,
        weights,
        first_shares,
        slot_row,
    )
    return call(body, outs, args, 2200000000, 22000000, far=(12,), scratch=BACK, name="turn")


def first_back(
    place, back, slot_column, upstream, middle, shares, dense, expert, own, parts, normed_two, joint, tokens, weights
):
    def body(
        place,
        back,
        slot_column,
        upstream,
        middle,
        shares,
        dense,
        expert,
        own,
        part_a,
        part_b,
        part_c,
        normed_two,
        joint,
        tokens,
        far,
        grad_out,
        mine,
        other,
        small_out,
        near,
        sems,
        mixed,
        joint_grad,
        attended,
    ):
        copies = start_weights(far, near, sems, 0)
        incoming = take_first(back, slot_column)
        incoming = (
            own[...]
            + part_a[...].astype(f32)
            + part_b[...].astype(f32)
            + part_c[...].astype(f32)
            + incoming
        )
        grad_out[...] = backward(
            tokens[...].astype(f32),
            near,
            copies,
            joint,
            middle[...],
            normed_two[...],
            shares[:, 0:1],
            shares[:, 1:2],
            upstream[...],
            dense[...],
            expert[...],
            incoming,
            joint_grad,
            attended,
            small_out,
            mixed,
        )
        for out, core in ((mine, place[1]), (other, 1 - place[1])):
            for i, step in enumerate((0, 1, 3, 2)):
                index = lax.rem(place[0] + step, 4) * 2 + core
                wide = pl.ds(pl.multiple_of(index * 384, 128), 384)
                out[i, :, 0:384] = joint_grad[:, wide]
                out[i, :, 384:512] = attended[:, pl.ds(pl.multiple_of(index * 128, 128), 128)]

    outs = (
        shape(ROWS, D, dtype=f32),
        shape(4, ROWS, 512),
        shape(4, ROWS, 512),
        shape(8, D, dtype=f32),
    )
    args = (
        place,
        back,
        slot_column,
        upstream,
        middle,
        shares,
        dense,
        expert,
        own,
        *parts,
        normed_two,
        joint,
        tokens,
        weights,
    )
    return call(body, outs, args, 2000000000, 20000000, far=(15,), scratch=BACK, name="back")


def few_columns(small):
    pick = lax.broadcasted_iota(jnp.int32, (8, 128), 0) == lax.broadcasted_iota(
        jnp.int32, (8, 128), 1
    )
    return dot_tn(small[...].astype(bf16), pick.astype(bf16)).astype(bf16)


def weights_first(place, line, mine, got, parts, small):
    def body(place, line, mine, got, part_a, part_b, part_c, small, out, ordered):
        def put(step, core, value):
            index = lax.rem(place[0] + step, 4) * 2 + core
            ordered[pl.ds(pl.multiple_of(index * ROWS, ROWS), ROWS), :] = value

        own, other = place[1], 1 - place[1]
        put(0, own, mine[0])
        put(0, other, got[0])
        for step, part in ((3, part_a), (1, part_b), (2, part_c)):
            put(step, own, part[0:ROWS, :])
            put(step, other, part[ROWS : 2 * ROWS, :])
        for low in range(0, D, 256):
            rows = slice(low, low + 256)
            for left, first, last in ((low, 0, 384), (D + low, 384, 512)):
                out[rows, first:last] = dot_tn(
                    line[:, left : left + 256], ordered[:, first:last]
                ).astype(bf16)
        out[:, 512:640] = few_columns(small)

    args = (place, line, mine, got, *parts, small)
    return call(
        body,
        (shape(D, 640),),
        args,
        1100000000,
        7000000,
        scratch=(pltpu.VMEM((1024, 512), bf16),),
        name="first_weights",
    )[0]


def weights_second(packed, pair, pair_twin, mine, got, small):
    def body(packed, pair, pair_twin, mine, got, small, out, near, sem):
        for low in range(0, D, 256):
            rows = slice(low, low + 256)
            for left, first, last in ((low, 0, 1536), (D + low, 1536, 2048)):
                near[rows, first:last] = (
                    dot_tn(pair[:, left : left + 256], mine[:, first:last])
                    + dot_tn(pair_twin[:, left : left + 256], got[:, first:last])
                ).astype(bf16)
        near[:, 2048:2176] = few_columns(small)
        copy = pltpu.make_async_copy(near, out.at[:, 2048:4224], sem)
        copy.start()
        copy.wait()

    args = (packed, pair, pair_twin, mine, got, small)
    return pl.pallas_call(
        body,
        out_shape=shape(D, 4224),
        in_specs=[pl.BlockSpec(memory_space=pl.ANY)] + [whole()] * 5,
        out_specs=pl.BlockSpec(memory_space=pl.ANY),
        scratch_shapes=[pltpu.VMEM((D, 2176), bf16), pltpu.SemaphoreType.DMA(())],
        input_output_aliases={0: 0},
        compiler_params=pltpu.CompilerParams(vmem_limit_bytes=LIMIT),
        cost_estimate=pl.CostEstimate(flops=1000000, bytes_accessed=1000000, transcendentals=0),
        name="second_weights",
    )(*args)


def weights_feed(group, group_twin, grad_hidden, active, inc, inc_twin):
    def body(group, group_twin, grad_hidden, active, inc, inc_twin, out):
        for low in range(0, D, 256):
            rows = slice(low, low + 256)
            out[rows, 0:512] = (
                dot_tn(group[:, rows], grad_hidden[0:512, :])
                + dot_tn(group_twin[:, rows], grad_hidden[512:1024, :])
            ).astype(bf16)
        for low in range(0, 512, 256):
            units = slice(low, low + 256)
            narrow = (
                dot_tn(active[0:512, units], inc[...]) + dot_tn(active[512:1024, units], inc_twin[...])
            ).astype(bf16)
            for i in range(8):
                place = low * 2 + i * 64
                part = narrow[i * 32 : (i + 1) * 32, :]
                out[place : place + 32, 512:1024] = part[:, 0:512]
                out[place + 32 : place + 64, 512:1024] = part[:, 512:1024]

    args = (group, group_twin, grad_hidden, active, inc, inc_twin)
    return call(body, (shape(D, 1024),), args, 1000000, 1000000, name="feed_weights")[0]


def feed_forward(group, twin, packed):
    def body(group, twin, far, other, own, active_out, slope_out, widen, narrow, near, sem):
        copy = pltpu.make_async_copy(far, near, sem)
        copy.start()
        copy.wait()
        for i in range(16):
            rows = near[i * 64 : i * 64 + 32, :]
            widen[i * 64 : i * 64 + 32, :] = rows[:, 0:512]
            widen[i * 64 + 32 : i * 64 + 64, :] = rows[:, 512:1024]
            narrow[i * 32 : i * 32 + 32, :] = near[i * 64 + 32 : i * 64 + 64, :]
        for i, source in ((1, twin), (0, group)):
            for low in range(0, 512, 256):
                active, slope = gelu_pieces(dot(source[low : low + 256, :], widen[...]))
                active = active.astype(bf16)
                place = slice(i * 512 + low, i * 512 + low + 256)
                active_out[place, :] = active
                slope_out[place, :] = slope.astype(bf16)
                terms = dot(active, narrow[...])
                if i == 1:
                    other[low : low + 256, :] = terms.astype(bf16)
                else:
                    own[low : low + 256, :] = terms

    outs = (
        shape(512, D),
        shape(512, D, dtype=f32),
        shape(1024, 512),
        shape(1024, 512),
        shape(D, 512),
        shape(512, D),
    )
    scratch = (pltpu.VMEM((D, D), bf16), pltpu.SemaphoreType.DMA(()))
    args = (group, twin, packed)
    return call(body, outs, args, 1000000, 1000000, far=(2,), scratch=scratch, name="feed_one")


def feed_backward(group, twin, slope, widen, narrow):
    def body(group, twin, slope, widen, narrow, other, own, grad_out):
        for i, source in ((1, twin), (0, group)):
            for low in range(0, 512, 256):
                place = slice(i * 512 + low, i * 512 + low + 256)
                grad = dot_nt(source[low : low + 256, :], narrow[...]) * slope[place, :].astype(f32)
                grad = grad.astype(bf16)
                grad_out[place, :] = grad
                terms = dot_nt(grad, widen[...])
                if i == 1:
                    other[low : low + 256, :] = terms.astype(bf16)
                else:
                    own[low : low + 256, :] = terms

    outs = (shape(512, D), shape(512, D, dtype=f32), shape(1024, 512))
    args = (group, twin, slope, widen, narrow)
    return call(body, outs, args, 1000000, 1000000, name="feed_one_back")


def gelu_pieces(x):
    k = 0.7978845608028654
    square = x * x
    bend = jnp.tanh(k * (x + 0.044715 * (square * x)))
    half = 0.5 * (1.0 + bend)
    slope = half + x * (0.5 * (1.0 - bend * bend)) * (k * (1.0 + 3 * 0.044715 * square))
    return x * half, slope


def grid_call(body, grid, in_specs, outs, out_specs, scratch, args, flops, moved, name):
    return pl.pallas_call(
        body,
        grid=grid,
        in_specs=in_specs,
        out_shape=outs,
        out_specs=out_specs,
        scratch_shapes=scratch,
        compiler_params=pltpu.CompilerParams(
            vmem_limit_bytes=LIMIT, dimension_semantics=("arbitrary",)
        ),
        cost_estimate=pl.CostEstimate(flops=flops, bytes_accessed=moved, transcendentals=0),
        name=name,
    )(*args)


def fixed(rows, columns):
    return pl.BlockSpec(
        (rows, columns), lambda i: (0, 0), pipeline_mode=pl.Buffered(buffer_count=1)
    )


def rows_of(rows, columns):
    return pl.BlockSpec((rows, columns), lambda i: (i, 0))


def owner_forward(rows, expander, reducer):
    def body(rows, expander, reducer, active_out, slope_out, parts_out):
        active, slope = gelu_pieces(dot(rows[...], expander[...]))
        active = active.astype(bf16)
        active_out[...] = active
        slope_out[...] = slope.astype(bf16)
        parts_out[...] = dot(active, reducer[...]).astype(bf16)

    block = rows_of(512, D)
    return grid_call(
        body,
        (2,),
        [block, fixed(D, D), fixed(D, D)],
        (shape(1024, D),) * 3,
        [block] * 3,
        [],
        (rows, expander, reducer),
        4300000000,
        12000000,
        "owner",
    )


def owner_backward(incoming, slope, expander, reducer):
    def body(incoming, slope, expander, reducer, grad_out, rows_out):
        grad = (dot_nt(incoming[...], reducer[...]) * slope[...].astype(f32)).astype(bf16)
        grad_out[...] = grad
        rows_out[...] = dot_nt(grad, expander[...]).astype(bf16)

    block = rows_of(256, D)
    return grid_call(
        body,
        (4,),
        [block, block, fixed(D, D), fixed(D, D)],
        (shape(1024, D),) * 2,
        [block] * 2,
        [],
        (incoming, slope, expander, reducer),
        4300000000,
        12000000,
        "owner_back",
    )


def places(kind):
    row = lax.broadcasted_iota(jnp.int32, (128, 256), 0)
    column = lax.broadcasted_iota(jnp.int32, (128, 256), 1)
    return (column == (row // 4) * 8 + kind * 4 + row % 4).astype(bf16)


def owner_both(arrived, expander, reducer):
    def body(arrived, expander, reducer, rows, grads, active_out, grad_out, sent):
        for block in range(2):
            packed = arrived[block * 256 : (block + 1) * 256, :]
            place = slice(block * 128, (block + 1) * 128)
            rows[place, :] = dot(places(0), packed).astype(bf16)
            grads[place, :] = dot(places(1), packed).astype(bf16)
        for low in range(0, 2048, 512):
            units = slice(low, low + 512)
            active, slope = gelu_pieces(dot(rows[...], expander[:, units]))
            active_out[:, units] = active.astype(bf16)
            grad_out[:, units] = (dot_nt(grads[...], reducer[units, :]) * slope).astype(bf16)
        parts = dot(active_out[...], reducer[...]).astype(bf16)
        returned = dot_nt(grad_out[...], expander[...]).astype(bf16)
        for block in range(2):
            place = slice(block * 128, (block + 1) * 128)
            sent[block * 256 : (block + 1) * 256, :] = (
                dot_tn(places(0), parts[place]) + dot_tn(places(1), returned[place])
            ).astype(bf16)

    return grid_call(
        body,
        (2,),
        [rows_of(512, D), fixed(D, 2048), fixed(2048, D)],
        (shape(512, D), shape(512, D), shape(512, 2048), shape(512, 2048), shape(1024, D)),
        [rows_of(256, D), rows_of(256, D), rows_of(256, 2048), rows_of(256, 2048), rows_of(512, D)],
        [],
        (arrived, expander, reducer),
        9000000000,
        20000000,
        "owner_both",
    )


def feed_both(blocks, weights):
    def body(
        block_a, block_b, block_c, block_d, weights, own, other, gradient, rows, active, grad
    ):
        part = pl.program_id(0)

        @pl.when(part == 0)
        def _():
            for i, block in enumerate((block_a, block_b, block_c, block_d)):
                rows[i * ROWS : (i + 1) * ROWS, :] = block[...]
            value, slope = gelu_pieces(dot(rows[:, 0:D], weights[:, 0:D]))
            active[...] = value.astype(bf16)
            back = dot_nt(rows[:, D : 2 * D], weights[:, D : 2 * D]) * slope
            grad[...] = back.astype(bf16)
            gradient[...] = dot_tn(rows[:, 0:D], grad[...]).astype(bf16)

        @pl.when(part == 1)
        def _():
            gradient[...] = dot_tn(active[...], rows[:, D : 2 * D]).astype(bf16)
            mine, twin = slice(0, 2 * ROWS), slice(2 * ROWS, 4 * ROWS)
            for place, out in ((twin, other), (mine, own)):
                out[:, 0:D] = dot(active[place, :], weights[:, D : 2 * D]).astype(out.dtype)
                out[:, D : 2 * D] = dot_nt(grad[place, :], weights[:, 0:D]).astype(out.dtype)

    full = fixed(ROWS, 2 * D)
    return pl.pallas_call(
        body,
        grid=(2,),
        in_specs=[full] * 4 + [fixed(D, 2 * D)],
        out_shape=(shape(2 * ROWS, 2 * D, dtype=f32), shape(2 * ROWS, 2 * D), shape(D, 4224)),
        out_specs=[
            pl.BlockSpec((2 * ROWS, 2 * D), lambda i: (0, 0)),
            pl.BlockSpec((2 * ROWS, 2 * D), lambda i: (0, 0)),
            pl.BlockSpec((D, D), lambda i: (0, i)),
        ],
        scratch_shapes=[
            pltpu.VMEM((4 * ROWS, 2 * D), bf16),
            pltpu.VMEM((4 * ROWS, D), bf16),
            pltpu.VMEM((4 * ROWS, D), bf16),
        ],
        compiler_params=pltpu.CompilerParams(
            vmem_limit_bytes=LIMIT, dimension_semantics=("arbitrary",)
        ),
        cost_estimate=pl.CostEstimate(
            flops=1000000, bytes_accessed=1000000, transcendentals=0
        ),
        name="feed",
    )(*blocks, weights)


def after(value, *others):
    return lax.optimization_barrier((value, *others))[0]


def gather_line(value):
    return jnp.concatenate(around(value), axis=0)


def scatter_column(other, own):
    got = swap(other)
    low = (own[ROWS:] + got[ROWS:].astype(f32)).astype(bf16)
    parts = (
        shift(low[:ROWS], "z", -1),
        shift(low[ROWS : 2 * ROWS], "z", 1),
        shift(low[2 * ROWS :], "z", 2),
    )
    return own[:ROWS] + got[:ROWS].astype(f32), parts


def around(value):
    return value, shift(value, "z", 1), shift(value, "z", -1), shift(value, "z", 2)


def positions(route):
    chosen = route[:, 0]
    row = jnp.arange(ROWS, dtype=jnp.int32)
    earlier = (row[None, :] < row[:, None]) & (row[None, :] // SEQ == row[:, None] // SEQ)
    same = (chosen[None, :] == chosen[:, None]) & earlier
    return chosen, row // SEQ, jnp.sum(same.astype(jnp.int32), axis=1)


def slots_first(route):
    chosen, sequence, position = positions(route)
    slot = chosen * 8 + sequence * 4 + position
    return slot[:, None], slot[None, :]


def slots_second(route):
    chosen, sequence, position = positions(route)
    slot = (chosen // 32) * 256 + (chosen % 32) * 8 + sequence * 2 + position
    return slot[:, None], slot[None, :]


def exchange(rows):
    blocks = rows.reshape(128, 8, rows.shape[-1])
    moved = lax.all_to_all(blocks, ALL, split_axis=0, concat_axis=0, tiled=True)
    return moved.reshape(rows.shape)


def exchange_plane(packed):
    blocks = packed.reshape(16, 64, packed.shape[1])
    return lax.all_to_all(blocks, PLANE, split_axis=0, concat_axis=0, tiled=True)


def add_blocks(blocks):
    return jnp.sum(blocks.astype(f32), axis=0).astype(bf16)


def pack_attention(inner, outer, mixer, gain, regain):
    blank = jnp.zeros((inner.shape[0], 124), bf16)
    return jnp.concatenate([inner, outer, mixer, gain[:, None], regain[:, None], blank], axis=1)


def pack_feed_first(widen, narrow):
    z, c = lax.axis_index("z"), lax.axis_index("c")
    units = widen.reshape(32, 16, 2, 4, 32)
    units = lax.dynamic_index_in_dim(units, z, 3, keepdims=False)
    mine = lax.dynamic_index_in_dim(units, c, 2, keepdims=False).reshape(32, 512)
    other = lax.dynamic_index_in_dim(units, 1 - c, 2, keepdims=False).reshape(32, 512)
    columns = in_order(c, mine, swap(other), 1)
    rows = lax.dynamic_slice_in_dim(narrow, z * 32, 32, 0)
    return jnp.concatenate([columns, rows], axis=0)


def pack_feed_second(widen, narrow):
    z, c = lax.axis_index("z"), lax.axis_index("c")
    half = lax.rem(z, 2)
    units = widen.reshape(32, 16, 2, 2, 64)
    units = lax.dynamic_index_in_dim(units, half, 3, keepdims=False)
    mine = lax.dynamic_index_in_dim(units, c, 2, keepdims=False).reshape(32, 1024)
    other = lax.dynamic_index_in_dim(units, 1 - c, 2, keepdims=False).reshape(32, 1024)
    columns = in_order(c, mine, swap(other), 0)
    return jnp.concatenate([columns, half_of(narrow, half, 0)], axis=1)


def quarter(place, i):
    return lax.rem(place[0] + (0, 3, 1, 2)[i], 4)


def finish_second(place, summed):
    c = lax.axis_index("c")
    rows = lax.dynamic_slice_in_dim(summed, 32 * (1 - c), 32, 1)
    got = swap(jnp.concatenate([rows[:, :, :1024], rows[:, :, 2048:]], axis=2))

    def body(place, summed, got, widen, narrow, inner, outer, few):
        first = lax.broadcasted_iota(jnp.int32, (32, 128), 1) < 64
        rows = pl.ds(pl.multiple_of(place[1] * 32, 32), 32)

        def mine(z, low, size):
            return summed[z, rows, low : low + size].astype(f32)

        def twin(z, low, size):
            low = low if low < 1024 else low - 1024
            return got[z, :, low : low + size].astype(f32)

        for core, term in ((place[1], mine), (1 - place[1], twin)):
            for low in range(0, 1024, 128):
                one = term(0, low, 128) + term(2, low, 128)
                two = term(1, low, 128) + term(3, low, 128)
                even = jnp.where(first, one, pltpu.roll(two, 64, 1))
                odd = jnp.where(first, pltpu.roll(one, 64, 1), two)
                for i, value in ((0, even), (1, odd)):
                    column = pl.multiple_of((low // 64 + i) * 256 + core * 128, 128)
                    widen[:, pl.ds(column, 128)] = value
            for out, low, size in ((inner, 2048, 1536), (outer, 3584, 512)):
                total = (term(0, low, size) + term(1, low, size)) + (
                    term(2, low, size) + term(3, low, size)
                )
                out[:, pl.ds(pl.multiple_of(core * size, 128), size)] = total
        total = jnp.zeros((32, 128), f32)
        for z in range(4):
            total += mine(z, 4096, 128) + twin(z, 4096, 128)
        few[...] = total
        for half in range(2):
            narrow[half * 64 : half * 64 + 64, :] = summed[half, :, 1024:2048].astype(f32) + summed[
                half + 2, :, 1024:2048
            ].astype(f32)

    outs = (
        shape(32, 4096, dtype=f32),
        shape(ROWS, D, dtype=f32),
        shape(32, 3072, dtype=f32),
        shape(32, D, dtype=f32),
        shape(32, 128, dtype=f32),
    )
    widen, narrow, inner, outer, few = call(
        body, outs, (place, summed, got), 1000000, 1000000, name="second_out"
    )
    return (widen, narrow), (inner, outer), (few[:, 0:2], few[:, 2], few[:, 3])


def finish_feed_first(place, blocks):
    c = lax.axis_index("c")
    summed = add_blocks(blocks)
    widen = summed[:, :512]
    widen = in_order(c, half_of(widen, c, 0), swap(half_of(widen, 1 - c, 0)), 1)
    narrow = jnp.concatenate([summed[:32, 512:], summed[32:, 512:]], axis=1)
    pieces = around(jnp.concatenate([widen, narrow], axis=0))

    def body(place, own, before, later, opposite, widen, narrow):
        lane = lax.broadcasted_iota(jnp.int32, (32, 128), 1) // 32
        for i, source in enumerate((own, before, later, opposite)):
            z = quarter(place, i)
            narrow[pl.ds(pl.multiple_of(z * 32, 32), 32), :] = source[32:64, :].astype(f32)
            for core in range(2):
                for four in range(4):
                    column = core * 512 + four * 128
                    value = source[0:32, column : column + 128].astype(f32)
                    for k in range(4):
                        moved = pltpu.roll(value, lax.rem(z * 32 + (128 - k * 32), 128), 1)
                        low = (four * 4 + k) * 256 + core * 128
                        out = widen.at[:, low : low + 128]
                        if i == 0:
                            out[...] = moved
                        else:
                            out[...] = jnp.where(lane == z, moved, out[...])

    outs = (shape(32, 4096, dtype=f32), shape(ROWS, D, dtype=f32))
    return call(body, outs, (place, *pieces), 1000000, 1000000, name="feed_one_out")


def finish_attention_first(place, blocks):
    c = lax.axis_index("c")
    summed = add_blocks(blocks)
    mine, got = half_of(summed, c, 0), swap(half_of(summed, 1 - c, 0))
    pieces = around(in_order(c, mine, got, 1))

    def body(place, own, before, later, opposite, inner, outer, few):
        total = (own[:, 512:640].astype(f32) + opposite[:, 512:640].astype(f32)) + (
            before[:, 512:640].astype(f32) + later[:, 512:640].astype(f32)
        )
        twin = (own[:, 1152:1280].astype(f32) + opposite[:, 1152:1280].astype(f32)) + (
            before[:, 1152:1280].astype(f32) + later[:, 1152:1280].astype(f32)
        )
        few[...] = total + twin
        for i, source in enumerate((own, before, later, opposite)):
            z = quarter(place, i)
            for core in range(2):
                low = core * 640
                index = z * 2 + core
                inner[:, pl.ds(pl.multiple_of(index * 384, 128), 384)] = source[
                    :, low : low + 384
                ].astype(f32)
                outer[:, pl.ds(pl.multiple_of(index * 128, 128), 128)] = source[
                    :, low + 384 : low + 512
                ].astype(f32)

    outs = (shape(32, 3072, dtype=f32), shape(32, D, dtype=f32), shape(32, 128, dtype=f32))
    inner, outer, few = call(body, outs, (place, *pieces), 1000000, 1000000, name="attention_out")
    return inner, outer, few[:, 0:2], few[:, 2], few[:, 3]


def on_device(
    tokens,
    cotangent,
    routes_first,
    routes_second,
    inner_first,
    outer_first,
    widen_first,
    narrow_first,
    mixer_first,
    gain_first,
    regain_first,
    inner_second,
    outer_second,
    widen_second,
    narrow_second,
    mixer_second,
    gain_second,
    regain_second,
    expand_first,
    reduce_first,
    expand_second,
    reduce_second,
):
    place = jnp.stack([lax.axis_index("z"), lax.axis_index("c")]).astype(jnp.int32)
    gathered = lax.all_gather(
        jnp.concatenate(
            [
                pack_attention(inner_first, outer_first, mixer_first, gain_first, regain_first),
                pack_attention(inner_second, outer_second, mixer_second, gain_second, regain_second),
            ],
            axis=1,
        ),
        ("x", "y", "c"),
        axis=0,
        tiled=True,
    )
    gathered_feed_first = lax.all_gather(
        pack_feed_first(widen_first, narrow_first), PLANE, axis=0, tiled=True
    )
    gathered_feed = lax.all_gather(
        pack_feed_second(widen_second, narrow_second), PLANE, axis=0, tiled=True
    )
    column_first, row_first = slots_first(routes_first)
    column_second, row_second = slots_second(routes_second)
    expander, reducer = expand_first[0], reduce_first[0]

    pair, joint, middle, normed_two, shares, send = first_front(tokens, gathered, row_first)
    received = exchange(send)
    group = gather_line(normed_two)
    received = after(received, group)
    active, slope, parts = owner_forward(received, expander, reducer)
    back = exchange(parts)
    group_twin = swap(group)
    other, own, active_feed, slope_feed, widen_one, narrow_one = feed_forward(
        group, group_twin, gathered_feed_first
    )
    dense_own, dense_parts = scatter_column(other, own)

    output, stream, dense, expert, pair_s, joint_s, middle_s, feed_s, shares_s, send = second_front(
        back,
        column_first,
        middle,
        shares,
        dense_own,
        dense_parts,
        cotangent,
        gathered,
        row_second,
    )
    arrived = exchange(send)
    feed_flipped = flip(feed_s)
    feed_blocks = (feed_s, feed_flipped, swap(feed_s), swap(feed_flipped))
    arrived = after(arrived, *feed_blocks)
    line = lax.all_gather(after(pair, arrived), COLUMN, axis=0, tiled=True)
    rows, incoming_s, active_s, grad_s, sent = owner_both(
        arrived, expand_second[0], reduce_second[0]
    )
    back = exchange(sent)
    feed_blocks = lax.optimization_barrier((*feed_blocks, sent))[:4]
    terms, terms_twin, feed_gradient = feed_both(feed_blocks, gathered_feed)
    got = swap(terms_twin)
    flipped = flip((terms[ROWS:] + got[ROWS:].astype(f32)).astype(bf16))
    pair_twin = swap(pair_s)
    back = after(back, line, pair_twin)
    output_two, upstream, mine, other, small, grad_dense, send = second_back(
        place,
        back,
        column_second,
        cotangent,
        middle_s,
        shares_s,
        terms,
        got,
        flipped,
        feed_s,
        joint_s,
        stream,
        gathered,
        shares,
        row_first,
    )
    grad_s = after(grad_s, send)
    grad_expand_two = dot_tn(rows, grad_s)
    grad_reduce_two = dot_tn(active_s, after(incoming_s, send))

    incoming = after(exchange(send), grad_expand_two, grad_reduce_two)
    grad_group = gather_line(grad_dense)
    grad_group_twin = swap(grad_group)
    feed_other, feed_own, grad_hidden = feed_backward(
        grad_group, grad_group_twin, slope_feed, widen_one, narrow_one
    )
    packed = weights_second(feed_gradient, pair_s, pair_twin, mine, swap(other), small)
    packed = lax.psum_scatter(packed, PLANE, scatter_dimension=0, tiled=True)
    grad_first, grad_rows = owner_backward(incoming, slope, expander, reducer)
    back = exchange(grad_rows)
    feed_own, feed_parts = scatter_column(feed_other, feed_own)
    feed_packed = weights_feed(
        group, group_twin, grad_hidden, active_feed, grad_group, grad_group_twin
    )
    back = after(back, feed_packed)
    feed_sums = exchange_plane(after(feed_packed, back))
    gradient_tokens, mine, other, small = first_back(
        place,
        back,
        column_first,
        upstream,
        middle,
        shares,
        dense,
        expert,
        feed_own,
        feed_parts,
        normed_two,
        joint,
        tokens,
        gathered,
    )
    got = swap(other)
    ahead = [jnp.concatenate([mine[i], got[i]], axis=0) for i in (1, 2, 3)]
    parts = (shift(ahead[0], "z", 1), shift(ahead[1], "z", -1), shift(ahead[2], "z", 2))
    packed = lax.all_gather(after(packed, mine), "z", axis=0)
    grad_first = after(grad_first, mine)
    grad_expand_one = dot_tn(received, grad_first)
    grad_reduce_one = dot_tn(active, after(incoming, mine))
    first_packed = weights_first(place, line, mine, got, parts, small)
    first_packed = after(first_packed, feed_sums)
    blocks = exchange_plane(first_packed)
    feed_finals = finish_feed_first(place, feed_sums)
    feed_finals_second, finals_second, few_second = finish_second(place, packed)
    blocks = after(
        blocks, feed_finals, feed_finals_second, finals_second, grad_expand_one, grad_reduce_one
    )
    inner, outer, *few_first = finish_attention_first(place, blocks)
    return (
        (output, output_two, gradient_tokens)
        + (inner, outer)
        + tuple(feed_finals)
        + tuple(few_first)
        + finals_second
        + tuple(feed_finals_second)
        + few_second
        + (
            grad_expand_one[None],
            grad_reduce_one[None],
            grad_expand_two[None],
            grad_reduce_two[None],
        )
    )


def solution(mesh):
    fine = Mesh(mesh.devices.reshape(4, 4, 4, 2), ALL)
    owner = ("x", "y", "c")
    tokens = P(ALL, None)
    dense = (P(owner, None),) * 5 + (P(owner),) * 2
    experts = (
        P(owner, None, "z"),
        P(owner, "z", None),
        P(ALL, None, None),
        P(ALL, None, None),
    )
    return jax.shard_map(
        on_device,
        mesh=fine,
        in_specs=(tokens,) * 4 + dense + dense + experts,
        out_specs=(tokens,) * 3 + dense + dense + experts,
        check_vma=False,
    )
```

time: 825 us -> 604 us (0.73)
  matrix products: 171 us -> 25.3 us
  local copies, waits for them, and re-layouts: 175 us -> 34.5 us
  Pallas kernels: 0 us -> 135 us
  other arithmetic: 65.5 us -> 15 us
  waiting for transfers between devices: 291 us -> 266 us
    pallas_call x0 -> x16, Pallas kernels: none -> 135 us  [the longest x11 80.5 us: call(): pl.pallas_call(body, out_shape=outs, in_specs=[pl.BlockSpec(memory_space=...]
    dot_general x43 -> x0, matrix products: 116 us -> none  [the longest x17 50.7 us: dot(): return jnp.dot(a, b, preferred_element_type=f32)]
    reshape x28 -> x6, local copies, waits for them, and re-layouts: 44.1 us -> 2.84 us  [the longest x1 1.71 us: pack_feed_first(): units = widen.reshape(32, 16, 2, 4, 32)]
    ppermute x0 -> x2, waiting for transfers between devices: none -> 39.3 us  [flip(): return lax.ppermute(value, 'z', [(0, 1), (1, 0), (2, 3), (3, 2)])]
    dot_general x15 -> x4, matrix products: 55.1 us -> 25.3 us  [dot_tn(): lax.dot_general(a, b, (((0,), (0,)), ((), ())), preferred_element_type=f32)]
    all_to_all x6, waiting for transfers between devices: 72 us -> 42.2 us  [exchange(): moved = lax.all_to_all(blocks, ALL, split_axis=0, concat_axis=0, tiled=True)]
    all_gather x3 -> x5, waiting for transfers between devices: 95.8 us -> 69 us  [the longest x1 64.5 us: on_device(): lax.all_gather(jnp.concatenate([pack_attention(inner_first, outer_first,...]
    another operation x15 -> x1, local copies, waits for them, and re-layouts: 25.7 us -> 0.01 us  [the longest x4 8.68 us: on_device(): jnp.stack([parts.astype(bf16).reshape(128, 4, 1024), grad_rows.astype(bf1...]
  transfers between devices with their start and end apart: 55 -> 52, of which waited for: 25 -> 25; matrix products, arithmetic and copies ran while one was open for 38% -> 9% of each run, Pallas kernels for 0% -> 19%
where the time goes in v2:
time: 604 us; the launch traced here: 595 us
  waiting for transfers between devices  266 us (44%)
  Pallas kernels  135 us (22%)
  starting transfers between devices  104 us (17%)
  local copies, waits for them, and re-layouts  34.5 us (6%)
  matrix products  25.3 us (4%)
  between operations  15.4 us (3%)
  other arithmetic  15 us (2%)
    ppermute x36, waiting for transfers between devices, shift(): lax.ppermute(value, axis, [(i, (i + step) % size) for i in range(size)])  115 us
    pallas_call x11, Pallas kernels, call(): pl.pallas_call(body, out_shape=outs, in_specs=[pl.BlockSpec(memory_space=...  80.5 us
    all_gather x1, waiting for transfers between devices, on_device(): lax.all_gather(jnp.concatenate([pack_attention(inner_first, outer_first,...  64.5 us
    all_to_all x6, starting transfers between devices, exchange(): moved = lax.all_to_all(blocks, ALL, split_axis=0, concat_axis=0, tiled=True)  50 us
    all_to_all x6, waiting for transfers between devices, exchange(): moved = lax.all_to_all(blocks, ALL, split_axis=0, concat_axis=0, tiled=True)  42.2 us
    ppermute x2, waiting for transfers between devices, flip(): return lax.ppermute(value, 'z', [(0, 1), (1, 0), (2, 3), (3, 2)])  39.3 us
    ppermute x36, starting transfers between devices, shift(): lax.ppermute(value, axis, [(i, (i + step) % size) for i in range(size)])  38.9 us
    pallas_call x3, Pallas kernels, grid_call(): pl.pallas_call(body, grid=grid, in_specs=in_specs, out_shape=outs, out_sp...  35.6 us
  transfers between devices with their start and end apart: 52, of which 25 were waited for; matrix products, arithmetic and copies ran while one was open for 9% of the time, Pallas kernels for 19%

profile of v2, /device:TPU:0, one launch (start us, length us, event | category | flops | bytes accessed | tf_op | source)
XLA Modules:
  0.0 594.9 jit_solution(2718873995696766829)
XLA Ops:
  25.6 64.5 %all-gather.7.cloned.1.call-done.far = bf16[1024,8448]{1,0:T(8,128)(2,1)} async-done(((bf16[32,8448]{1,0:T(8,128)(2,1)}), bf16[1024,8448]{1,0:T(8,128)(2,1)}) %all-gather.7.cloned.1.call-update) | async-done | bytes 17301520 | tf_op jit(solution)/shard_map/all_gather | solution.py:1149
  90.1 7.5 %front.1 = (bf16[128,2048]{1,0:T(8,128)(2,1)}, bf16[128,3072]{1,0:T(8,128)(2,1)}, f32[128,1024]{1,0:T(8,128)}, bf16[128,1024]{1,0:T(8,128)(2,1)}, f32[128,128]{1,0:T(8,128)}, /*index=5*/bf16[1024,1024]{1,0:T(8,128)(2,1)}) custom-call(bf16[128,1024]{1,0:T(8,128)(2,1)} %tokens.3, bf16[1024,8448]{1,0:T(8,128)(2,1)} %all-gather.7.cloned.1.call-done.far, ...), custom_call_target="tpu_custom_call" | custom-call | flops 1300000000 | bytes 14000000 | tf_op jit(solution)/shard_map/front/pallas_call | solution.py:78
  97.6 8.7 %all-to-all-start = ((bf16[128,8,1024]{2,1,0:T(8,128)(2,1)}), bf16[128,8,1024]{2,1,0:T(8,128)(2,1)}, u32[]{:S(2)}, u32[]{:S(2)}) async-start(bf16[128,8,1024]{2,1,0:T(8,128)(2,1)} %bitcast.89), calls=%async_computation | async-start | bytes 4194304 | tf_op jit(solution)/shard_map/all_to_all | solution.py:967
  111.2 25.5 %collective-permute-done = bf16[128,1024]{1,0:T(8,128)(2,1)S(1)} collective-permute-done((bf16[128,1024]{1,0:T(8,128)(2,1)S(1)}, bf16[128,1024]{1,0:T(8,128)(2,1)S(1)}, u32[]{:S(2)}, u32[]{:S(2)}) %collective-permute-start) | collective-permute-done | bytes 262176 | tf_op jit(solution)/shard_map/ppermute | solution.py:27
  136.7 6.4 %collective-permute-done.2 = bf16[128,1024]{1,0:T(8,128)(2,1)S(1)} collective-permute-done((bf16[128,1024]{1,0:T(8,128)(2,1)S(1)}, bf16[128,1024]{1,0:T(8,128)(2,1)S(1)}, u32[]{:S(2)}, u32[]{:S(2)}) %collective-permute-start.2) | collective-permute-done | bytes 262176 | tf_op jit(solution)/shard_map/ppermute | solution.py:27
  148.8 8.7 %feed_one.1 = (bf16[512,1024]{1,0:T(8,128)(2,1)}, f32[512,1024]{1,0:T(8,128)}, bf16[1024,512]{1,0:T(8,128)(2,1)}, bf16[1024,512]{1,0:T(8,128)(2,1)}, bf16[1024,5...) custom-call(bf16[512,1024]{1,0:T(8,128)(2,1)} %copy-done.6, bf16[512,1024]{1,0:T(8,128)(2,1)} %copy-done.7, ...), custom_call_target="tpu_custom_call" | custom-call | flops 1000000 | bytes 1000000 | tf_op jit(solution)/shard_map/feed_one/pallas_call | solution.py:78
  157.7 9.3 %owner.1 = (bf16[1024,1024]{1,0:T(8,128)(2,1)}, bf16[1024,1024]{1,0:T(8,128)(2,1)}, bf16[1024,1024]{1,0:T(8,128)(2,1)}) custom-call(bf16[1024,1024]{1,0:T(8,128)(2,1)} %bitcast.7.rows, bf16[1024,1024]{1,0:T(8,128)(2,1)} %bitcast.107, bf16[1024,1024]{1,0:T(8,128)(2,1)} %bitcast.109), custom_call_target="tpu_custom_call" | custom-call | flops 4300000256 | bytes 12000000 | tf_op jit(solution)/shard_map/owner/pallas_call | solution.py:763
  166.9 8.0 %all-to-all-start.1 = ((bf16[128,8,1024]{2,1,0:T(8,128)(2,1)}), bf16[128,8,1024]{2,1,0:T(8,128)(2,1)S(1)}, u32[]{:S(2)}, u32[]{:S(2)}) async-start(bf16[128,8,1024]{2,1,0:T(8,128)(2,1)} %bitcast.92), calls=%async_computation.1 | async-start | bytes 4194304 | tf_op jit(solution)/shard_map/all_to_all | solution.py:967
  185.2 14.1 %collective-permute-done.8.part_c = bf16[128,1024]{1,0:T(8,128)(2,1)S(1)} collective-permute-done((bf16[128,1024]{1,0:T(8,128)(2,1)S(1)}, bf16[128,1024]{1,0:T(8,128)(2,1)S(1)}, u32[]{:S(2)}, u32[]{:S(2)}) %collective-permute-start.8) | collective-permute-done | bytes 262176 | tf_op jit(solution)/shard_map/ppermute | solution.py:27
  199.3 9.7 %collective-permute-done.7.part_b = bf16[128,1024]{1,0:T(8,128)(2,1)S(1)} collective-permute-done((bf16[128,1024]{1,0:T(8,128)(2,1)S(1)}, bf16[128,1024]{1,0:T(8,128)(2,1)S(1)}, u32[]{:S(2)}, u32[]{:S(2)}) %collective-permute-start.7) | collective-permute-done | bytes 262176 | tf_op jit(solution)/shard_map/ppermute | solution.py:27
  209.7 11.5 %all-to-all-done.1 = bf16[128,8,1024]{2,1,0:T(8,128)(2,1)S(1)} async-done(((bf16[128,8,1024]{2,1,0:T(8,128)(2,1)}), bf16[128,8,1024]{2,1,0:T(8,128)(2,1)S(1)}, u32[]{:S(2)}, u32[]{:S(2)}) %all-to-all-start.1) | async-done | bytes 2097184 | tf_op jit(solution)/shard_map/all_to_all | solution.py:967
  222.5 9.5 %between.1 = (bf16[128,1024]{1,0:T(8,128)(2,1)}, f32[128,1024]{1,0:T(8,128)}, f32[128,1024]{1,0:T(8,128)}, f32[128,1024]{1,0:T(8,128)}, bf16[128,2048]{1,0:T(8,1...) custom-call(bf16[1024,1024]{1,0:T(8,128)(2,1)} %bitcast.79, ...), custom_call_target="tpu_custom_call" | custom-call | flops 1800000000 | bytes 20000000 | tf_op jit(solution)/shard_map/between/pallas_call | solution.py:78
  238.2 33.8 %collective-permute-done.9.block_b = bf16[128,2048]{1,0:T(8,128)(2,1)S(1)} collective-permute-done((bf16[128,2048]{1,0:T(8,128)(2,1)S(1)}, bf16[128,2048]{1,0:T(8,128)(2,1)S(1)}, u32[]{:S(2)}, u32[]{:S(2)}) %collective-permute-start.9) | collective-permute-done | bytes 524320 | tf_op jit(solution)/shard_map/ppermute | solution.py:35
  275.5 17.3 %owner_both.1 = (bf16[512,1024]{1,0:T(8,128)(2,1)}, bf16[512,1024]{1,0:T(8,128)(2,1)}, bf16[512,2048]{1,0:T(8,128)(2,1)}, bf16[512,2048]{1,0:T(8,128)(2,1)}, bf16[1024,1024]{1,0:T(8,128)(2,1)}) custom-call(bf16[1024,1024]{1,0:T(8,128)(2,1)} %bitcast.93, bf16[1024,2048]{1,0:T(8,128)(2,1)} %bitcast.105, bf16[2048,1024]{1,0:T(8,128)(2,1)} %bitcast.106), custom_call_target="tpu_custom_call" | custom-call | flops 8999999488 | bytes 20000000 | tf_op jit(solution)/shard_map/owner_both/pallas_call | solution.py:763
  292.8 12.5 %feed.1 = (f32[256,2048]{1,0:T(8,128)}, bf16[256,2048]{1,0:T(8,128)(2,1)}, bf16[1024,4224]{1,0:T(8,128)(2,1)}) custom-call(bf16[128,2048]{1,0:T(8,128)(2,1)} %get-tuple-element.117.block_a.feed, bf16[128,2048]{1,0:T(8,128)(2,1)} %copy-done.17, bf16[128,2048]{1,0:T(8,128)(2,1)} %copy-done.18, bf16[128,2048]{1,0:T(8,128)(2,1)} %collective-permute-done.11.block_d, ...), custom_call_target="tpu_custom_call" | custom-call | flops 1000000 | bytes 1000000 | tf_op jit(solution)/shard_map/feed/pallas_call | solution.py:897
  305.8 10.1 %all-to-all-start.3 = ((bf16[128,8,1024]{2,1,0:T(8,128)(2,1)}), bf16[128,8,1024]{2,1,0:T(8,128)(2,1)S(1)}, u32[]{:S(2)}, u32[]{:S(2)}) async-start(bf16[128,8,1024]{2,1,0:T(8,128)(2,1)} %bitcast.91), calls=%async_computation.3 | async-start | bytes 4194304 | tf_op jit(solution)/shard_map/all_to_all | solution.py:967
  321.4 24.8 %all-to-all-done.3 = bf16[128,8,1024]{2,1,0:T(8,128)(2,1)S(1)} async-done(((bf16[128,8,1024]{2,1,0:T(8,128)(2,1)}), bf16[128,8,1024]{2,1,0:T(8,128)(2,1)S(1)}, u32[]{:S(2)}, u32[]{:S(2)}) %all-to-all-start.3) | async-done | bytes 2097184 | tf_op jit(solution)/shard_map/all_to_all | solution.py:967
  351.7 14.6 %turn.1 = (bf16[128,1024]{1,0:T(8,128)(2,1)}, f32[128,1024]{1,0:T(8,128)}, bf16[128,2048]{1,0:T(8,128)(2,1)}, bf16[128,2048]{1,0:T(8,128)(2,1)}, f32[8,1024]{1,0...) custom-call(s32[2]{0:T(128)} %pad_add_fusion.place, bf16[1024,1024]{1,0:T(8,128)(2,1)} %bitcast.78, ...), custom_call_target="tpu_custom_call" | custom-call | flops 2200000000 | bytes 22000000 | tf_op jit(solution)/shard_map/turn/pallas_call | solution.py:78
  369.2 6.1 %second_weights.1 = bf16[1024,4224]{1,0:T(8,128)(2,1)} custom-call(bf16[1024,4224]{1,0:T(8,128)(2,1)} %get-tuple-element.157.packed, bf16[128,2048]{1,0:T(8,128)(2,1)} %get-tuple-element.113.pair, bf16[128,2048]{1,0:T(8,128)(2,1)} %collective-permute-done.12.pair_twin, bf16[128,2048]{1,0:T(8,128)(2,1)} %get-tuple-element.158.mine, ...), custom_call_target="tpu_custom_call", output_to_operand_aliasing={{}: (0, {})} | custom-call | flops 1000000 | bytes 1000000 | tf_op jit(solution)/shard_map/second_weights/pallas_call | solution.py:662
  375.4 9.6 %all-to-all-start.4 = ((bf16[128,8,1024]{2,1,0:T(8,128)(2,1)}), bf16[128,8,1024]{2,1,0:T(8,128)(2,1)S(1)}, u32[]{:S(2)}, u32[]{:S(2)}) async-start(bf16[128,8,1024]{2,1,0:T(8,128)(2,1)} %bitcast.88), calls=%async_computation.4 | async-start | bytes 4194304 | tf_op jit(solution)/shard_map/all_to_all | solution.py:967
  390.1 7.5 %fusion.24 = f32[1024,2048]{1,0:T(8,128)} fusion(bf16[512,1024]{1,0:T(8,128)(2,1)S(1)} %copy-done.42, bf16[512,2048]{1,0:T(8,128)(2,1)} %get-tuple-element.129), kind=kOutput, calls=%fused_computation.102 | convolution fusion | flops 2147483648 | bytes 11534336 | tf_op jit(solution)/shard_map/dot_general | solution.py:43
  397.6 23.6 %collective-permute-done.16 = bf16[128,1024]{1,0:T(8,128)(2,1)S(1)} collective-permute-done((bf16[128,1024]{1,0:T(8,128)(2,1)S(1)}, bf16[128,1024]{1,0:T(8,128)(2,1)S(1)}, u32[]{:S(2)}, u32[]{:S(2)}) %collective-permute-start.16) | collective-permute-done | bytes 262176 | tf_op jit(solution)/shard_map/ppermute | solution.py:27
  428.8 9.1 %owner_back.1 = (bf16[1024,1024]{1,0:T(8,128)(2,1)}, bf16[1024,1024]{1,0:T(8,128)(2,1)}) custom-call(bf16[1024,1024]{1,0:T(8,128)(2,1)} %bitcast.86, bf16[1024,1024]{1,0:T(8,128)(2,1)} %get-tuple-element.134.slope, bf16[1024,1024]{1,0:T(8,128)(2,1)} %bitcast.108, bf16[1024,1024]{1,0:T(8,128)(2,1)} %bitcast.110), custom_call_target="tpu_custom_call" | custom-call | flops 4300000256 | bytes 12000000 | tf_op jit(solution)/shard_map/owner_back/pallas_call | solution.py:763
  437.8 8.8 %all-to-all-start.5 = ((bf16[128,8,1024]{2,1,0:T(8,128)(2,1)}), bf16[128,8,1024]{2,1,0:T(8,128)(2,1)S(1)}, u32[]{:S(2)}, u32[]{:S(2)}) async-start(bf16[128,8,1024]{2,1,0:T(8,128)(2,1)} %bitcast.90), calls=%async_computation.5 | async-start | bytes 4194304 | tf_op jit(solution)/shard_map/all_to_all | solution.py:967
  446.7 7.0 %feed_one_back.1 = (bf16[512,1024]{1,0:T(8,128)(2,1)}, f32[512,1024]{1,0:T(8,128)}, bf16[1024,512]{1,0:T(8,128)(2,1)}) custom-call(bf16[512,1024]{1,0:T(8,128)(2,1)} %copy-done.5, bf16[512,1024]{1,0:T(8,128)(2,1)} %collective-permute-done.19.twin.inc_twin, bf16[1024,512]{1,0:T(8,128)(2,1)} %get-tuple-element.137.slope, ...), custom_call_target="tpu_custom_call" | custom-call | flops 1000000 | bytes 1000000 | tf_op jit(solution)/shard_map/feed_one_back/pallas_call | solution.py:78
  465.3 6.5 %feed_weights.1 = bf16[1024,1024]{1,0:T(8,128)(2,1)} custom-call(bf16[512,1024]{1,0:T(8,128)(2,1)} %copy-done.6, bf16[512,1024]{1,0:T(8,128)(2,1)} %copy-done.7, bf16[1024,512]{1,0:T(8,128)(2,1)} %get-tuple-element.140.grad_hidden, bf16[1024,512]{1,0:T(8,128)(2,1)} %get-tuple-element.141.active, bf16[512,1024]{1,0:T(8,128)(2,1)} %copy-done.5, ...), custom_call_target="tpu_custom_call" | custom-call | flops 1000000 | bytes 1000000 | tf_op jit(solution)/shard_map/feed_weights/pallas_call | solution.py:78
  487.7 13.6 %back.1 = (f32[128,1024]{1,0:T(8,128)}, bf16[4,128,512]{2,1,0:T(8,128)(2,1)}, bf16[4,128,512]{2,1,0:T(8,128)(2,1)}, f32[8,1024]{1,0:T(8,128)}) custom-call(s32[2]{0:T(128)} %pad_add_fusion.place, bf16[1024,1024]{1,0:T(8,128)(2,1)} %bitcast.81, s32[128,1]{1,0:T(8,128)} %get-tuple-element.287.slot_column, f32[128,1024]{1,0:T(8,128)} %get-tuple-element.143.upstream, ...), custom_call_target="tpu_custom_call" | custom-call | flops 2000000000 | bytes 20000000 | tf_op jit(solution)/shard_map/back/pallas_call | solution.py:78
  512.5 6.0 %fusion.26 = f32[1024,1024]{1,0:T(8,128)} fusion(bf16[1024,1024]{1,0:T(8,128)(2,1)} %bitcast.7.rows, bf16[1024,1024]{1,0:T(8,128)(2,1)S(1)} %copy-done.43), kind=kOutput, calls=%fused_computation.104 | convolution fusion | flops 2147483648 | bytes 8388608 | tf_op jit(solution)/shard_map/dot_general | solution.py:43
  518.5 8.5 %collective-permute-done.25.part_a = bf16[256,512]{1,0:T(8,128)(2,1)S(1)} collective-permute-done((bf16[256,512]{1,0:T(8,128)(2,1)S(1)}, bf16[256,512]{1,0:T(8,128)(2,1)S(1)}, u32[]{:S(2)}, u32[]{:S(2)}) %collective-permute-start.25) | collective-permute-done | bytes 262176 | tf_op jit(solution)/shard_map/ppermute | solution.py:27
  527.0 6.4 %collective-permute-done.27.part_c = bf16[256,512]{1,0:T(8,128)(2,1)S(1)} collective-permute-done((bf16[256,512]{1,0:T(8,128)(2,1)S(1)}, bf16[256,512]{1,0:T(8,128)(2,1)S(1)}, u32[]{:S(2)}, u32[]{:S(2)}) %collective-permute-start.27) | collective-permute-done | bytes 262176 | tf_op jit(solution)/shard_map/ppermute | solution.py:27
  540.4 7.5 %all-to-all-start.7 = ((bf16[16,64,640]{2,1,0:T(8,128)(2,1)}), bf16[16,64,640]{2,1,0:T(8,128)(2,1)S(1)}, u32[]{:S(2)}, u32[]{:S(2)}) async-start(bf16[16,64,640]{2,1,0:T(8,128)(2,1)} %bitcast.82), calls=%async_computation.7 | async-start | bytes 2621440 | tf_op jit(solution)/shard_map/all_to_all | solution.py:973
  556.0 6.0 %fusion.27 = f32[1024,1024]{1,0:T(8,128)} fusion(bf16[1024,1024]{1,0:T(8,128)(2,1)} %get-tuple-element.168, bf16[1024,1024]{1,0:T(8,128)(2,1)S(1)} %bitcast.87), kind=kOutput, calls=%fused_computation.105 | convolution fusion | flops 2147483648 | bytes 8388608 | tf_op jit(solution)/shard_map/dot_general | solution.py:43
  (257 shorter events, 156.9 us)
Async XLA Ops:
  7.2 82.9 %all-gather.7.cloned.1.call-start = ((), (), s32[]{:S(2)}) async-start(), calls=%async_computation.9 | async-start | bytes 17842176 | tf_op jit(solution)/shard_map/all_gather | solution.py:1149
  13.7 134.1 %all-gather.9.cloned.1.call-start = ((), (), s32[]{:S(2)}) async-start(), calls=%async_computation.10 | async-start | bytes 2228224 | tf_op jit(solution)/shard_map/all_gather | solution.py:1161
  19.3 273.4 %all-gather.13.cloned.1.call-start = ((), (), s32[]{:S(2)}) async-start(), calls=%async_computation.12 | async-start | bytes 4456448 | tf_op jit(solution)/shard_map/all_gather | solution.py:1164
  97.6 60.1 %all-to-all-start = ((bf16[128,8,1024]{2,1,0:T(8,128)(2,1)}), bf16[128,8,1024]{2,1,0:T(8,128)(2,1)}, u32[]{:S(2)}, u32[]{:S(2)}) async-start(bf16[128,8,1024]{2,1,0:T(8,128)(2,1)} %bitcast.89), calls=%async_computation | async-start | bytes 4194304 | tf_op jit(solution)/shard_map/all_to_all | solution.py:967
  106.3 30.4 %collective-permute-start = (bf16[128,1024]{1,0:T(8,128)(2,1)S(1)}, bf16[128,1024]{1,0:T(8,128)(2,1)S(1)}, u32[]{:S(2)}, u32[]{:S(2)}) collective-permute-start(bf16[128,1024]{1,0:T(8,128)(2,1)S(1)} %copy-done.15), channel_id=1, source_target_pairs={{0,32},{32,64},{64,96},{96,0},{1,33},{33,65},{65,97},{97,1},{2,34}... | collective-permute-start | bytes 786440 | tf_op jit(solution)/shard_map/ppermute | solution.py:27
  107.4 29.3 %collective-permute-start.1 = (bf16[128,1024]{1,0:T(8,128)(2,1)S(1)}, bf16[128,1024]{1,0:T(8,128)(2,1)S(1)}, u32[]{:S(2)}, u32[]{:S(2)}) collective-permute-start(bf16[128,1024]{1,0:T(8,128)(2,1)S(1)} %copy-done.15), channel_id=1, source_target_pairs={{0,96},{32,0},{64,32},{96,64},{1,97},{33,1},{65,33},{97,65},{2,98}... | collective-permute-start | bytes 786440 | tf_op jit(solution)/shard_map/ppermute | solution.py:27
  109.6 33.5 %collective-permute-start.2 = (bf16[128,1024]{1,0:T(8,128)(2,1)S(1)}, bf16[128,1024]{1,0:T(8,128)(2,1)S(1)}, u32[]{:S(2)}, u32[]{:S(2)}) collective-permute-start(bf16[128,1024]{1,0:T(8,128)(2,1)S(1)} %copy-done.15), channel_id=1, source_target_pairs={{0,64},{32,96},{64,0},{96,32},{1,65},{33,97},{65,1},{97,33},{2,66}... | collective-permute-start | bytes 786440 | tf_op jit(solution)/shard_map/ppermute | solution.py:27
  166.9 54.3 %all-to-all-start.1 = ((bf16[128,8,1024]{2,1,0:T(8,128)(2,1)}), bf16[128,8,1024]{2,1,0:T(8,128)(2,1)S(1)}, u32[]{:S(2)}, u32[]{:S(2)}) async-start(bf16[128,8,1024]{2,1,0:T(8,128)(2,1)} %bitcast.92), calls=%async_computation.1 | async-start | bytes 4194304 | tf_op jit(solution)/shard_map/all_to_all | solution.py:967
  176.7 22.7 %collective-permute-start.8 = (bf16[128,1024]{1,0:T(8,128)(2,1)S(1)}, bf16[128,1024]{1,0:T(8,128)(2,1)S(1)}, u32[]{:S(2)}, u32[]{:S(2)}) collective-permute-start(bf16[128,1024]{1,0:T(8,128)(2,1)S(1)} %get-tuple-element.272), channel_id=1, source_target_pairs={{0,64},{32,96},{64,0},{96,32},{1,65},{33,97},{65,1},{97,33},{2,66}... | collective-permute-start | bytes 786440 | tf_op jit(solution)/shard_map/ppermute | solution.py:27
  179.6 29.4 %collective-permute-start.7 = (bf16[128,1024]{1,0:T(8,128)(2,1)S(1)}, bf16[128,1024]{1,0:T(8,128)(2,1)S(1)}, u32[]{:S(2)}, u32[]{:S(2)}) collective-permute-start(bf16[128,1024]{1,0:T(8,128)(2,1)S(1)} %get-tuple-element.273), channel_id=1, source_target_pairs={{0,32},{32,64},{64,96},{96,0},{1,33},{33,65},{65,97},{97,1},{2,34}... | collective-permute-start | bytes 786440 | tf_op jit(solution)/shard_map/ppermute | solution.py:27
  180.4 29.3 %collective-permute-start.6 = (bf16[128,1024]{1,0:T(8,128)(2,1)S(1)}, bf16[128,1024]{1,0:T(8,128)(2,1)}, u32[]{:S(2)}, u32[]{:S(2)}) collective-permute-start(bf16[128,1024]{1,0:T(8,128)(2,1)S(1)} %get-tuple-element.274), channel_id=1, source_target_pairs={{0,96},{32,0},{64,32},{96,64},{1,97},{33,1},{65,33},{97,65},{2,98}... | collective-permute-start | bytes 786440 | tf_op jit(solution)/shard_map/ppermute | solution.py:27
  232.0 42.1 %all-to-all-start.2 = ((bf16[128,8,1024]{2,1,0:T(8,128)(2,1)}), bf16[128,8,1024]{2,1,0:T(8,128)(2,1)S(1)}, u32[]{:S(2)}, u32[]{:S(2)}) async-start(bf16[128,8,1024]{2,1,0:T(8,128)(2,1)} %bitcast.94), calls=%async_computation.2 | async-start | bytes 4194304 | tf_op jit(solution)/shard_map/all_to_all | solution.py:967
  236.8 109.4 %all-gather.11.cloned.1.call-start = ((), (), s32[]{:S(2)}) async-start(), calls=%async_computation.11 | async-start | bytes 4718592 | tf_op jit(solution)/shard_map/all_gather | solution.py:1198
  236.9 35.2 %collective-permute-start.9 = (bf16[128,2048]{1,0:T(8,128)(2,1)S(1)}, bf16[128,2048]{1,0:T(8,128)(2,1)S(1)}, u32[]{:S(2)}, u32[]{:S(2)}) collective-permute-start(bf16[128,2048]{1,0:T(8,128)(2,1)S(1)} %copy-done.9), channel_id=1, source_target_pairs={{0,32},{32,0},{64,96},{96,64},{1,33},{33,1},{65,97},{97,65},{2,34}... | collective-permute-start | bytes 1572872 | tf_op jit(solution)/shard_map/ppermute | solution.py:35
  238.2 33.9 %collective-permute-start.10 = (bf16[128,2048]{1,0:T(8,128)(2,1)S(1)}, bf16[128,2048]{1,0:T(8,128)(2,1)S(1)}, u32[]{:S(2)}, u32[]{:S(2)}) collective-permute-start(bf16[128,2048]{1,0:T(8,128)(2,1)S(1)} %copy-done.9), channel_id=1, source_target_pairs={{0,1},{1,0},{2,3},{3,2},{4,5},{5,4},{6,7},{7,6},{8,9},{9,8},{10,11... | collective-permute-start | bytes 1572872 | tf_op jit(solution)/shard_map/ppermute | solution.py:27
  305.8 40.5 %all-to-all-start.3 = ((bf16[128,8,1024]{2,1,0:T(8,128)(2,1)}), bf16[128,8,1024]{2,1,0:T(8,128)(2,1)S(1)}, u32[]{:S(2)}, u32[]{:S(2)}) async-start(bf16[128,8,1024]{2,1,0:T(8,128)(2,1)} %bitcast.91), calls=%async_computation.3 | async-start | bytes 4194304 | tf_op jit(solution)/shard_map/all_to_all | solution.py:967
  315.8 185.5 %reduce-scatter.2.cloned.1.call-start = ((), (), s32[]{:S(2)}) async-start(), calls=%async_computation.13 | async-start | bytes 9191424 | tf_op jit(solution)/shard_map/reduce_scatter | solution.py:1237
  318.6 33.0 %collective-permute-start.15 = (bf16[128,2048]{1,0:T(8,128)(2,1)}, bf16[128,2048]{1,0:T(8,128)(2,1)}, u32[]{:S(2)}, u32[]{:S(2)}) collective-permute-start(bf16[128,2048]{1,0:T(8,128)(2,1)} %add_convert_fusion.2), channel_id=1, source_target_pairs={{0,32},{32,0},{64,96},{96,64},{1,33},{33,1},{65,97},{97,65},{2,34}... | collective-permute-start | bytes 1572872 | tf_op jit(solution)/shard_map/ppermute | solution.py:35
  375.4 52.0 %all-to-all-start.4 = ((bf16[128,8,1024]{2,1,0:T(8,128)(2,1)}), bf16[128,8,1024]{2,1,0:T(8,128)(2,1)S(1)}, u32[]{:S(2)}, u32[]{:S(2)}) async-start(bf16[128,8,1024]{2,1,0:T(8,128)(2,1)} %bitcast.88), calls=%async_computation.4 | async-start | bytes 4194304 | tf_op jit(solution)/shard_map/all_to_all | solution.py:967
  385.0 36.3 %collective-permute-start.18 = (bf16[128,1024]{1,0:T(8,128)(2,1)S(1)}, bf16[128,1024]{1,0:T(8,128)(2,1)S(1)}, u32[]{:S(2)}, u32[]{:S(2)}) collective-permute-start(bf16[128,1024]{1,0:T(8,128)(2,1)S(1)} %copy-done.28), channel_id=1, source_target_pairs={{0,64},{32,96},{64,0},{96,32},{1,65},{33,97},{65,1},{97,33},{2,66}... | collective-permute-start | bytes 786440 | tf_op jit(solution)/shard_map/ppermute | solution.py:27
  388.0 33.3 %collective-permute-start.17 = (bf16[128,1024]{1,0:T(8,128)(2,1)S(1)}, bf16[128,1024]{1,0:T(8,128)(2,1)S(1)}, u32[]{:S(2)}, u32[]{:S(2)}) collective-permute-start(bf16[128,1024]{1,0:T(8,128)(2,1)S(1)} %copy-done.28), channel_id=1, source_target_pairs={{0,96},{32,0},{64,32},{96,64},{1,97},{33,1},{65,33},{97,65},{2,98}... | collective-permute-start | bytes 786440 | tf_op jit(solution)/shard_map/ppermute | solution.py:27
  388.9 32.4 %collective-permute-start.16 = (bf16[128,1024]{1,0:T(8,128)(2,1)S(1)}, bf16[128,1024]{1,0:T(8,128)(2,1)S(1)}, u32[]{:S(2)}, u32[]{:S(2)}) collective-permute-start(bf16[128,1024]{1,0:T(8,128)(2,1)S(1)} %copy-done.28), channel_id=1, source_target_pairs={{0,32},{32,64},{64,96},{96,0},{1,33},{33,65},{65,97},{97,1},{2,34}... | collective-permute-start | bytes 786440 | tf_op jit(solution)/shard_map/ppermute | solution.py:27
  421.4 25.3 %collective-permute-start.19 = (bf16[512,1024]{1,0:T(8,128)(2,1)S(1)}, bf16[512,1024]{1,0:T(8,128)(2,1)}, u32[]{:S(2)}, u32[]{:S(2)}) collective-permute-start(bf16[512,1024]{1,0:T(8,128)(2,1)S(1)} %constant_dynamic-update-slice_fusion.4.group.inc), channel_id=1, source_target_pairs={{0,1},{1,0},{2,3},{3,2},{4,5},{5,4},{6,7},{7,6},{8,9},{9,8},{10,11... | collective-permute-start | bytes 3145736 | tf_op jit(solution)/shard_map/ppermute | solution.py:27
  437.8 41.7 %all-to-all-start.5 = ((bf16[128,8,1024]{2,1,0:T(8,128)(2,1)}), bf16[128,8,1024]{2,1,0:T(8,128)(2,1)S(1)}, u32[]{:S(2)}, u32[]{:S(2)}) async-start(bf16[128,8,1024]{2,1,0:T(8,128)(2,1)} %bitcast.90), calls=%async_computation.5 | async-start | bytes 4194304 | tf_op jit(solution)/shard_map/all_to_all | solution.py:967
  446.7 101.3 %all-gather.15.cloned.1.call-start = ((), (), s32[]{:S(2)}) async-start(), calls=%async_computation.14 | async-start | bytes 2703360 | tf_op jit(solution)/shard_map/all_gather | solution.py:1265
  459.0 22.7 %collective-permute-start.23 = (bf16[128,1024]{1,0:T(8,128)(2,1)}, bf16[128,1024]{1,0:T(8,128)(2,1)S(1)}, u32[]{:S(2)}, u32[]{:S(2)}) collective-permute-start(bf16[128,1024]{1,0:T(8,128)(2,1)} %get-tuple-element.269), channel_id=1, source_target_pairs={{0,64},{32,96},{64,0},{96,32},{1,65},{33,97},{65,1},{97,33},{2,66}... | collective-permute-start | bytes 786440 | tf_op jit(solution)/shard_map/ppermute | solution.py:27
  461.9 25.1 %collective-permute-start.22 = (bf16[128,1024]{1,0:T(8,128)(2,1)S(1)}, bf16[128,1024]{1,0:T(8,128)(2,1)S(1)}, u32[]{:S(2)}, u32[]{:S(2)}) collective-permute-start(bf16[128,1024]{1,0:T(8,128)(2,1)S(1)} %get-tuple-element.270), channel_id=1, source_target_pairs={{0,32},{32,64},{64,96},{96,0},{1,33},{33,65},{65,97},{97,1},{2,34}... | collective-permute-start | bytes 786440 | tf_op jit(solution)/shard_map/ppermute | solution.py:27
  462.7 24.3 %collective-permute-start.21 = (bf16[128,1024]{1,0:T(8,128)(2,1)S(1)}, bf16[128,1024]{1,0:T(8,128)(2,1)S(1)}, u32[]{:S(2)}, u32[]{:S(2)}) collective-permute-start(bf16[128,1024]{1,0:T(8,128)(2,1)S(1)} %get-tuple-element.271), channel_id=1, source_target_pairs={{0,96},{32,0},{64,32},{96,64},{1,97},{33,1},{65,33},{97,65},{2,98}... | collective-permute-start | bytes 786440 | tf_op jit(solution)/shard_map/ppermute | solution.py:27
  501.4 38.5 %all-to-all-start.6 = ((bf16[16,64,1024]{2,1,0:T(8,128)(2,1)}), bf16[16,64,1024]{2,1,0:T(8,128)(2,1)S(1)}, u32[]{:S(2)}, u32[]{:S(2)}) async-start(bf16[16,64,1024]{2,1,0:T(8,128)(2,1)} %bitcast.80), calls=%async_computation.6 | async-start | bytes 4194304 | tf_op jit(solution)/shard_map/all_to_all | solution.py:973
  508.8 18.2 %collective-permute-start.25 = (bf16[256,512]{1,0:T(8,128)(2,1)S(1)}, bf16[256,512]{1,0:T(8,128)(2,1)S(1)}, u32[]{:S(2)}, u32[]{:S(2)}) collective-permute-start(bf16[256,512]{1,0:T(8,128)(2,1)S(1)} %pad_maximum_fusion.2), channel_id=1, source_target_pairs={{0,32},{32,64},{64,96},{96,0},{1,33},{33,65},{65,97},{97,1},{2,34}... | collective-permute-start | bytes 786440 | tf_op jit(solution)/shard_map/ppermute | solution.py:27
  512.2 21.3 %collective-permute-start.27 = (bf16[256,512]{1,0:T(8,128)(2,1)S(1)}, bf16[256,512]{1,0:T(8,128)(2,1)S(1)}, u32[]{:S(2)}, u32[]{:S(2)}) collective-permute-start(bf16[256,512]{1,0:T(8,128)(2,1)S(1)} %pad_maximum_fusion.4), channel_id=1, source_target_pairs={{0,64},{32,96},{64,0},{96,32},{1,65},{33,97},{65,1},{97,33},{2,66}... | collective-permute-start | bytes 786440 | tf_op jit(solution)/shard_map/ppermute | solution.py:27
  540.4 29.5 %all-to-all-start.7 = ((bf16[16,64,640]{2,1,0:T(8,128)(2,1)}), bf16[16,64,640]{2,1,0:T(8,128)(2,1)S(1)}, u32[]{:S(2)}, u32[]{:S(2)}) async-start(bf16[16,64,640]{2,1,0:T(8,128)(2,1)} %bitcast.82), calls=%async_computation.7 | async-start | bytes 2621440 | tf_op jit(solution)/shard_map/all_to_all | solution.py:973
  (64 other events, 483.7 us)
Sparse Core Ops, SparseCore 0:
  13.8 76.1 all-gather.6
  92.8 54.9 all-gather.8
  150.0 67.2 all-gather.12
  274.3 34.3 all-gather.10
  375.5 121.7 reduce-scatter.1
  501.5 39.9 all-gather.14

commit v3 on v2

--- a/solution.py
+++ b/solution.py
@@ -90,11 +90,11 @@
     )(*args)
 
 
-def start_weights(far, near, sems, base):
+def start_weights(far, near, sems):
     copies = []
     for i, low, high in ((4, 4096, 4224), (0, 0, D), (1, D, 2 * D), (2, 2 * D, 3 * D), (3, 3 * D, 4096)):
         copy = pltpu.make_async_copy(
-            far.at[:, base + low : base + high], near.at[:, low:high], sems.at[i]
+            far.at[:, low:high], near.at[:, low:high], sems.at[i]
         )
         copy.start()
         copies.append(copy)
@@ -324,7 +324,7 @@
 
 def first_front(tokens, weights, slot_row):
     def body(tokens, far, slot_row, pair, joint, middle, two, shares, send, near, sems):
-        copies = start_weights(far, near, sems, 0)
+        copies = start_weights(far, near, sems)
         normed, mixed = halves_of(pair)
         rows, _, _ = front(
             tokens[...].astype(f32), near, copies, normed, joint, mixed, middle, two, shares
@@ -369,7 +369,7 @@
         near,
         sems,
     ):
-        copies = start_weights(far, near, sems, PACKED)
+        copies = start_weights(far, near, sems)
         expert = take_first(back, slot_column)
         dense = own[...] + part_a[...].astype(f32) + part_b[...].astype(f32) + part_c[...].astype(f32)
         dense_out[...] = dense
@@ -417,7 +417,6 @@
     middle,
     shares,
     own,
-    got,
     flipped,
     feed,
     joint,
@@ -434,7 +433,6 @@
         middle,
         shares,
         own,
-        got,
         flipped,
         feed,
         joint,
@@ -455,9 +453,9 @@
         joint_grad,
         attended,
     ):
-        copies = start_weights(far, near, sems, PACKED)
+        copies = start_weights(far, near, sems)
         expert, from_experts = take_second(back, slot_column)
-        total = own[0:ROWS, :] + got[0:ROWS, :].astype(f32) + flipped[...].astype(f32)
+        total = own[...] + flipped[...].astype(f32)
         dense, from_feed = total[:, 0:D], total[:, D : 2 * D]
         one, two = shares[:, 0:1], shares[:, 1:2]
         low_out[...] = (middle[...] + one * dense + two * expert).astype(bf16)
@@ -504,7 +502,6 @@
         middle,
         shares,
         own,
-        got,
         flipped,
         feed,
         joint,
@@ -513,7 +510,7 @@
         first_shares,
         slot_row,
     )
-    return call(body, outs, args, 2200000000, 22000000, far=(12,), scratch=BACK, name="turn")
+    return call(body, outs, args, 1000000, 1000000, far=(11,), scratch=BACK, name="turn")
 
 
 def first_back(
@@ -546,7 +543,7 @@
         joint_grad,
         attended,
     ):
-        copies = start_weights(far, near, sems, 0)
+        copies = start_weights(far, near, sems)
         incoming = take_first(back, slot_column)
         incoming = (
             own[...]
@@ -602,7 +599,7 @@
         tokens,
         weights,
     )
-    return call(body, outs, args, 2000000000, 20000000, far=(15,), scratch=BACK, name="back")
+    return call(body, outs, args, 1000000, 1000000, far=(15,), scratch=BACK, name="back")
 
 
 def few_columns(small):
@@ -637,8 +634,8 @@
         body,
         (shape(D, 640),),
         args,
-        1100000000,
-        7000000,
+        1000000,
+        1000000,
         scratch=(pltpu.VMEM((1024, 512), bf16),),
         name="first_weights",
     )[0]
@@ -672,82 +669,103 @@
     )(*args)
 
 
-def weights_feed(group, group_twin, grad_hidden, active, inc, inc_twin):
-    def body(group, group_twin, grad_hidden, active, inc, inc_twin, out):
+def weights_feed(place, group, group_twin, grad_hidden, active, got, inc, inc_twin):
+    def body(place, group, group_twin, grad_hidden, active, got, inc, inc_twin, out):
+        base = place[1] * 512
+        grad = grad_hidden[:, pl.ds(pl.multiple_of(base, 128), 512)]
         for low in range(0, D, 256):
             rows = slice(low, low + 256)
             out[rows, 0:512] = (
-                dot_tn(group[:, rows], grad_hidden[0:512, :])
-                + dot_tn(group_twin[:, rows], grad_hidden[512:1024, :])
+                dot_tn(group[:, rows], grad) + dot_tn(group_twin[:, rows], got[:, 0:512])
             ).astype(bf16)
         for low in range(0, 512, 256):
-            units = slice(low, low + 256)
+            units = active[:, pl.ds(pl.multiple_of(base + low, 128), 256)]
             narrow = (
-                dot_tn(active[0:512, units], inc[...]) + dot_tn(active[512:1024, units], inc_twin[...])
+                dot_tn(units, inc[...]) + dot_tn(got[:, 512 + low : 768 + low], inc_twin[...])
             ).astype(bf16)
             for i in range(8):
-                place = low * 2 + i * 64
+                start = low * 2 + i * 64
                 part = narrow[i * 32 : (i + 1) * 32, :]
-                out[place : place + 32, 512:1024] = part[:, 0:512]
-                out[place + 32 : place + 64, 512:1024] = part[:, 512:1024]
-
-    args = (group, group_twin, grad_hidden, active, inc, inc_twin)
+                out[start : start + 32, 512:1024] = part[:, 0:512]
+                out[start + 32 : start + 64, 512:1024] = part[:, 512:1024]
+
+    args = (place, group, group_twin, grad_hidden, active, got, inc, inc_twin)
     return call(body, (shape(D, 1024),), args, 1000000, 1000000, name="feed_weights")[0]
 
 
-def feed_forward(group, twin, packed):
-    def body(group, twin, far, other, own, active_out, slope_out, widen, narrow, near, sem):
-        copy = pltpu.make_async_copy(far, near, sem)
+def feed_forward(group, packed):
+    def body(group, far, own, part_a, part_b, part_c, active_out, slope_out, narrow, near, sem):
+        copy = pltpu.make_async_copy(far.at[:, PACKED : PACKED + 2 * D], near, sem)
         copy.start()
         copy.wait()
         for i in range(16):
-            rows = near[i * 64 : i * 64 + 32, :]
-            widen[i * 64 : i * 64 + 32, :] = rows[:, 0:512]
-            widen[i * 64 + 32 : i * 64 + 64, :] = rows[:, 512:1024]
-            narrow[i * 32 : i * 32 + 32, :] = near[i * 64 + 32 : i * 64 + 64, :]
-        for i, source in ((1, twin), (0, group)):
-            for low in range(0, 512, 256):
-                active, slope = gelu_pieces(dot(source[low : low + 256, :], widen[...]))
-                active = active.astype(bf16)
-                place = slice(i * 512 + low, i * 512 + low + 256)
-                active_out[place, :] = active
-                slope_out[place, :] = slope.astype(bf16)
-                terms = dot(active, narrow[...])
-                if i == 1:
-                    other[low : low + 256, :] = terms.astype(bf16)
-                else:
-                    own[low : low + 256, :] = terms
+            for core in range(2):
+                source = (i * 2 + core) * 32
+                target = core * 512 + i * 32
+                narrow[target : target + 32, :] = near[source : source + 32, D : 2 * D]
+        for low in range(0, 512, 256):
+            place = slice(low, low + 256)
+            active, slope = gelu_pieces(dot(group[place, :], near[:, 0:D]))
+            active = active.astype(bf16)
+            active_out[place, :] = active
+            slope_out[place, :] = slope.astype(bf16)
+            terms = dot(active, narrow[...])
+            first, second = ((own, part_a), (part_b, part_c))[low // 256]
+            first[...] = terms[0:ROWS].astype(first.dtype)
+            second[...] = terms[ROWS : 2 * ROWS].astype(bf16)
 
     outs = (
+        shape(ROWS, D, dtype=f32),
+        shape(ROWS, D),
+        shape(ROWS, D),
+        shape(ROWS, D),
         shape(512, D),
-        shape(512, D, dtype=f32),
-        shape(1024, 512),
-        shape(1024, 512),
-        shape(D, 512),
         shape(512, D),
+        shape(D, D),
+    )
+    scratch = (pltpu.VMEM((D, 2 * D), bf16), pltpu.SemaphoreType.DMA(()))
+    args = (group, packed)
+    own, *parts, active, slope, narrow = call(
+        body, outs, args, 1000000, 1000000, far=(1,), scratch=scratch, name="feed_one"
+    )
+    return own, return_parts(parts), active, slope, narrow
+
+
+def feed_backward(place, group, active, slope, narrow, packed):
+    def body(
+        place, group, active, slope, narrow, far, own, part_a, part_b, part_c, grad_out, sent, near, sem
+    ):
+        copy = pltpu.make_async_copy(far.at[:, PACKED : PACKED + D], near, sem)
+        copy.start()
+        other = pl.ds(pl.multiple_of((1 - place[1]) * 512, 128), 512)
+        sent[:, 512:1024] = active[:, other]
+        for low in range(0, 512, 256):
+            rows = slice(low, low + 256)
+            grad = dot_nt(group[rows, :], narrow[...]) * slope[rows, :].astype(f32)
+            grad = grad.astype(bf16)
+            grad_out[rows, :] = grad
+            if low == 0:
+                copy.wait()
+            terms = dot_nt(grad, near[...])
+            first, second = ((own, part_a), (part_b, part_c))[low // 256]
+            first[...] = terms[0:ROWS].astype(first.dtype)
+            second[...] = terms[ROWS : 2 * ROWS].astype(bf16)
+        sent[:, 0:512] = grad_out[:, other]
+
+    outs = (
+        shape(ROWS, D, dtype=f32),
+        shape(ROWS, D),
+        shape(ROWS, D),
+        shape(ROWS, D),
+        shape(512, D),
+        shape(512, D),
     )
     scratch = (pltpu.VMEM((D, D), bf16), pltpu.SemaphoreType.DMA(()))
-    args = (group, twin, packed)
-    return call(body, outs, args, 1000000, 1000000, far=(2,), scratch=scratch, name="feed_one")
-
-
-def feed_backward(group, twin, slope, widen, narrow):
-    def body(group, twin, slope, widen, narrow, other, own, grad_out):
-        for i, source in ((1, twin), (0, group)):
-            for low in range(0, 512, 256):
-                place = slice(i * 512 + low, i * 512 + low + 256)
-                grad = dot_nt(source[low : low + 256, :], narrow[...]) * slope[place, :].astype(f32)
-                grad = grad.astype(bf16)
-                grad_out[place, :] = grad
-                terms = dot_nt(grad, widen[...])
-                if i == 1:
-                    other[low : low + 256, :] = terms.astype(bf16)
-                else:
-                    own[low : low + 256, :] = terms
-
-    outs = (shape(512, D), shape(512, D, dtype=f32), shape(1024, 512))
-    args = (group, twin, slope, widen, narrow)
-    return call(body, outs, args, 1000000, 1000000, name="feed_one_back")
+    args = (place, group, active, slope, narrow, packed)
+    own, *parts, grad, sent = call(
+        body, outs, args, 1000000, 1000000, far=(5,), scratch=scratch, name="feed_one_back"
+    )
+    return own, return_parts(parts), grad, sent
 
 
 def gelu_pieces(x):
@@ -869,54 +887,87 @@
     )
 
 
-def feed_both(blocks, weights):
-    def body(
-        block_a, block_b, block_c, block_d, weights, own, other, gradient, rows, active, grad
-    ):
-        part = pl.program_id(0)
-
-        @pl.when(part == 0)
-        def _():
-            for i, block in enumerate((block_a, block_b, block_c, block_d)):
-                rows[i * ROWS : (i + 1) * ROWS, :] = block[...]
-            value, slope = gelu_pieces(dot(rows[:, 0:D], weights[:, 0:D]))
-            active[...] = value.astype(bf16)
-            back = dot_nt(rows[:, D : 2 * D], weights[:, D : 2 * D]) * slope
-            grad[...] = back.astype(bf16)
-            gradient[...] = dot_tn(rows[:, 0:D], grad[...]).astype(bf16)
-
-        @pl.when(part == 1)
-        def _():
-            gradient[...] = dot_tn(active[...], rows[:, D : 2 * D]).astype(bf16)
-            mine, twin = slice(0, 2 * ROWS), slice(2 * ROWS, 4 * ROWS)
-            for place, out in ((twin, other), (mine, own)):
-                out[:, 0:D] = dot(active[place, :], weights[:, D : 2 * D]).astype(out.dtype)
-                out[:, D : 2 * D] = dot_nt(grad[place, :], weights[:, 0:D]).astype(out.dtype)
-
-    full = fixed(ROWS, 2 * D)
+def feed_both(place, mine, partner, weights):
+    def body(place, mine, partner, far, own, other, active, grad, sent, rows, near, sems):
+        copies = []
+        for i, low in enumerate((0, 2 * D, D, 3 * D)):
+            copy = pltpu.make_async_copy(
+                far.at[:, low : low + D], near.at[:, low : low + D], sems.at[i]
+            )
+            copy.start()
+            copies.append(copy)
+        rows[0:ROWS, :] = mine[...]
+        rows[ROWS : 2 * ROWS, :] = partner[...]
+        for part in range(2):
+            units = slice(part * D, part * D + D)
+            narrow = slice(2 * D + part * D, 3 * D + part * D)
+            copies[2 * part].wait()
+            value, slope = gelu_pieces(dot(rows[:, 0:D], near[:, units]))
+            active[:, units] = value.astype(bf16)
+            copies[2 * part + 1].wait()
+            back = dot_nt(rows[:, D : 2 * D], near[:, narrow]) * slope
+            grad[:, units] = back.astype(bf16)
+        dense = dot(active[:, 0:D], near[:, 2 * D : 3 * D]) + dot(
+            active[:, D : 2 * D], near[:, 3 * D : 4 * D]
+        )
+        own[:, 0:D] = dense[0:ROWS]
+        other[:, 0:D] = dense[ROWS : 2 * ROWS].astype(bf16)
+        back = dot_nt(grad[...], near[:, 0 : 2 * D])
+        own[:, D : 2 * D] = back[0:ROWS]
+        other[:, D : 2 * D] = back[ROWS : 2 * ROWS].astype(bf16)
+        twin = pl.ds(pl.multiple_of((1 - place[1]) * D, 128), D)
+        sent[:, 0:D] = active[:, twin]
+        sent[:, D : 2 * D] = grad[:, twin]
+
+    outs = (
+        shape(ROWS, 2 * D, dtype=f32),
+        shape(ROWS, 2 * D),
+        shape(2 * ROWS, 2 * D),
+        shape(2 * ROWS, 2 * D),
+        shape(2 * ROWS, 2 * D),
+    )
+    scratch = (
+        pltpu.VMEM((2 * ROWS, 2 * D), bf16),
+        pltpu.VMEM((D, 4 * D), bf16),
+        pltpu.SemaphoreType.DMA((4,)),
+    )
+    args = (place, mine, partner, weights)
+    return call(body, outs, args, 1000000, 1000000, far=(3,), scratch=scratch, name="feed")
+
+
+def feed_gradients(place, mine, partner, twins, active, grad, got):
+    def body(place, mine, partner, twins, active, grad, got, out):
+        base = place[1] * D
+
+        for low in range(0, D, 256):
+            column = slice(low, low + 256)
+            units = pl.ds(pl.multiple_of(base + low, 128), 256)
+            normed = slice(low, low + 256)
+            values = grad[:, pl.ds(pl.multiple_of(base, 128), D)]
+            out[column, 0:D] = (
+                dot_tn(mine[:, normed], values[0:ROWS])
+                + dot_tn(partner[:, normed], values[ROWS : 2 * ROWS])
+                + dot_tn(twins[:, normed], got[:, D : 2 * D])
+            ).astype(bf16)
+            out[column, D : 2 * D] = (
+                dot_tn(active[0:ROWS, units], mine[:, D : 2 * D])
+                + dot_tn(active[ROWS : 2 * ROWS, units], partner[:, D : 2 * D])
+                + dot_tn(got[:, column], twins[:, D : 2 * D])
+            ).astype(bf16)
+
+    args = (place, mine, partner, twins, active, grad, got)
+    outs = (shape(D, 4224),)
     return pl.pallas_call(
         body,
-        grid=(2,),
-        in_specs=[full] * 4 + [fixed(D, 2 * D)],
-        out_shape=(shape(2 * ROWS, 2 * D, dtype=f32), shape(2 * ROWS, 2 * D), shape(D, 4224)),
-        out_specs=[
-            pl.BlockSpec((2 * ROWS, 2 * D), lambda i: (0, 0)),
-            pl.BlockSpec((2 * ROWS, 2 * D), lambda i: (0, 0)),
-            pl.BlockSpec((D, D), lambda i: (0, i)),
-        ],
-        scratch_shapes=[
-            pltpu.VMEM((4 * ROWS, 2 * D), bf16),
-            pltpu.VMEM((4 * ROWS, D), bf16),
-            pltpu.VMEM((4 * ROWS, D), bf16),
-        ],
-        compiler_params=pltpu.CompilerParams(
-            vmem_limit_bytes=LIMIT, dimension_semantics=("arbitrary",)
-        ),
-        cost_estimate=pl.CostEstimate(
-            flops=1000000, bytes_accessed=1000000, transcendentals=0
-        ),
-        name="feed",
-    )(*blocks, weights)
+        grid=(1,),
+        in_specs=[pl.BlockSpec(memory_space=pltpu.SMEM)]
+        + [pl.BlockSpec(arg.shape, lambda i: (0, 0)) for arg in args[1:]],
+        out_shape=outs,
+        out_specs=[pl.BlockSpec((D, 2 * D), lambda i: (0, 0))],
+        compiler_params=pltpu.CompilerParams(vmem_limit_bytes=LIMIT),
+        cost_estimate=pl.CostEstimate(flops=1000000, bytes_accessed=1000000, transcendentals=0),
+        name="feed_gradients",
+    )(*args)[0]
 
 
 def after(value, *others):
@@ -927,15 +978,8 @@
     return jnp.concatenate(around(value), axis=0)
 
 
-def scatter_column(other, own):
-    got = swap(other)
-    low = (own[ROWS:] + got[ROWS:].astype(f32)).astype(bf16)
-    parts = (
-        shift(low[:ROWS], "z", -1),
-        shift(low[ROWS : 2 * ROWS], "z", 1),
-        shift(low[2 * ROWS :], "z", 2),
-    )
-    return own[:ROWS] + got[:ROWS].astype(f32), parts
+def return_parts(parts):
+    return shift(parts[0], "z", -1), shift(parts[1], "z", 1), shift(parts[2], "z", 2)
 
 
 def around(value):
@@ -973,6 +1017,33 @@
     return lax.all_to_all(blocks, PLANE, split_axis=0, concat_axis=0, tiled=True)
 
 
+def few_rows(few):
+    pick = lax.broadcasted_iota(jnp.int32, (8, 128), 0) == lax.broadcasted_iota(
+        jnp.int32, (8, 128), 1
+    )
+    return lax.dot_general(
+        pick.astype(f32),
+        few,
+        (((1,), (1,)), ((), ())),
+        precision=lax.Precision.HIGHEST,
+        preferred_element_type=f32,
+    )
+
+
+def write_few(total, mixer, gain, regain):
+    rows = few_rows(total)
+    mixer[...] = rows[0:2]
+    gain[...] = rows[2:3]
+    regain[...] = rows[3:4]
+
+
+FEW = (
+    jax.ShapeDtypeStruct((2, 32), f32),
+    jax.ShapeDtypeStruct((1, 32), f32),
+    jax.ShapeDtypeStruct((1, 32), f32),
+)
+
+
 def add_blocks(blocks):
     return jnp.sum(blocks.astype(f32), axis=0).astype(bf16)
 
@@ -983,25 +1054,20 @@
 
 
 def pack_feed_first(widen, narrow):
-    z, c = lax.axis_index("z"), lax.axis_index("c")
+    z = lax.axis_index("z")
     units = widen.reshape(32, 16, 2, 4, 32)
     units = lax.dynamic_index_in_dim(units, z, 3, keepdims=False)
-    mine = lax.dynamic_index_in_dim(units, c, 2, keepdims=False).reshape(32, 512)
-    other = lax.dynamic_index_in_dim(units, 1 - c, 2, keepdims=False).reshape(32, 512)
-    columns = in_order(c, mine, swap(other), 1)
-    rows = lax.dynamic_slice_in_dim(narrow, z * 32, 32, 0)
-    return jnp.concatenate([columns, rows], axis=0)
+    columns = units.transpose(0, 2, 1, 3).reshape(32, 1024)
+    return jnp.concatenate([columns, lax.dynamic_slice_in_dim(narrow, z * 32, 32, 0)], axis=1)
 
 
 def pack_feed_second(widen, narrow):
-    z, c = lax.axis_index("z"), lax.axis_index("c")
-    half = lax.rem(z, 2)
-    units = widen.reshape(32, 16, 2, 2, 64)
+    half = lax.rem(lax.axis_index("z"), 2)
+    units = widen.reshape(32, 16, 2, 2, 2, 32)
     units = lax.dynamic_index_in_dim(units, half, 3, keepdims=False)
-    mine = lax.dynamic_index_in_dim(units, c, 2, keepdims=False).reshape(32, 1024)
-    other = lax.dynamic_index_in_dim(units, 1 - c, 2, keepdims=False).reshape(32, 1024)
-    columns = in_order(c, mine, swap(other), 0)
-    return jnp.concatenate([columns, half_of(narrow, half, 0)], axis=1)
+    columns = units.transpose(0, 3, 1, 2, 4).reshape(32, 2048)
+    rows = half_of(narrow, half, 0)
+    return jnp.concatenate([columns, rows[:32], rows[32:]], axis=1)
 
 
 def quarter(place, i):
@@ -1010,29 +1076,34 @@
 
 def finish_second(place, summed):
     c = lax.axis_index("c")
-    rows = lax.dynamic_slice_in_dim(summed, 32 * (1 - c), 32, 1)
-    got = swap(jnp.concatenate([rows[:, :, :1024], rows[:, :, 2048:]], axis=2))
-
-    def body(place, summed, got, widen, narrow, inner, outer, few):
-        first = lax.broadcasted_iota(jnp.int32, (32, 128), 1) < 64
+    got = swap(lax.dynamic_slice_in_dim(summed, 32 * (1 - c), 32, 1))
+
+    def body(place, summed, got, widen, narrow, inner, outer, mixer, gain, regain):
+        lane = lax.broadcasted_iota(jnp.int32, (32, 128), 1) // 32
         rows = pl.ds(pl.multiple_of(place[1] * 32, 32), 32)
 
         def mine(z, low, size):
             return summed[z, rows, low : low + size].astype(f32)
 
         def twin(z, low, size):
-            low = low if low < 1024 else low - 1024
             return got[z, :, low : low + size].astype(f32)
 
-        for core, term in ((place[1], mine), (1 - place[1], twin)):
+        for index, (core, term) in enumerate(((place[1], mine), (1 - place[1], twin))):
             for low in range(0, 1024, 128):
-                one = term(0, low, 128) + term(2, low, 128)
-                two = term(1, low, 128) + term(3, low, 128)
-                even = jnp.where(first, one, pltpu.roll(two, 64, 1))
-                odd = jnp.where(first, pltpu.roll(one, 64, 1), two)
-                for i, value in ((0, even), (1, odd)):
-                    column = pl.multiple_of((low // 64 + i) * 256 + core * 128, 128)
-                    widen[:, pl.ds(column, 128)] = value
+                for half in range(2):
+                    value = term(half, low, 128) + term(half + 2, low, 128)
+                    target = half * 2 + core
+                    for k in range(4):
+                        moved = pltpu.roll(value, lax.rem(target * 32 + (128 - k * 32), 128), 1)
+                        column = (low // 32 + k) * 128
+                        out = widen.at[:, column : column + 128]
+                        if index == 0 and half == 0:
+                            out[...] = moved
+                        else:
+                            out[...] = jnp.where(lane == target, moved, out[...])
+            for half in range(2):
+                place_in = pl.multiple_of(half * 64 + core * 32, 32)
+                narrow[pl.ds(place_in, 32), :] = term(half, 1024, 1024) + term(half + 2, 1024, 1024)
             for out, low, size in ((inner, 2048, 1536), (outer, 3584, 512)):
                 total = (term(0, low, size) + term(1, low, size)) + (
                     term(2, low, size) + term(3, low, size)
@@ -1041,23 +1112,19 @@
         total = jnp.zeros((32, 128), f32)
         for z in range(4):
             total += mine(z, 4096, 128) + twin(z, 4096, 128)
-        few[...] = total
-        for half in range(2):
-            narrow[half * 64 : half * 64 + 64, :] = summed[half, :, 1024:2048].astype(f32) + summed[
-                half + 2, :, 1024:2048
-            ].astype(f32)
+        write_few(total, mixer, gain, regain)
 
     outs = (
         shape(32, 4096, dtype=f32),
         shape(ROWS, D, dtype=f32),
         shape(32, 3072, dtype=f32),
         shape(32, D, dtype=f32),
-        shape(32, 128, dtype=f32),
-    )
-    widen, narrow, inner, outer, few = call(
+        *FEW,
+    )
+    widen, narrow, inner, outer, mixer, gain, regain = call(
         body, outs, (place, summed, got), 1000000, 1000000, name="second_out"
     )
-    return (widen, narrow), (inner, outer), (few[:, 0:2], few[:, 2], few[:, 3])
+    return (widen, narrow), (inner, outer), (mixer.T, gain.reshape(32), regain.reshape(32))
 
 
 def finish_feed_first(place, blocks):
@@ -1090,35 +1157,33 @@
     return call(body, outs, (place, *pieces), 1000000, 1000000, name="feed_one_out")
 
 
-def finish_attention_first(place, blocks):
-    c = lax.axis_index("c")
-    summed = add_blocks(blocks)
-    mine, got = half_of(summed, c, 0), swap(half_of(summed, 1 - c, 0))
-    pieces = around(in_order(c, mine, got, 1))
-
-    def body(place, own, before, later, opposite, inner, outer, few):
-        total = (own[:, 512:640].astype(f32) + opposite[:, 512:640].astype(f32)) + (
-            before[:, 512:640].astype(f32) + later[:, 512:640].astype(f32)
-        )
-        twin = (own[:, 1152:1280].astype(f32) + opposite[:, 1152:1280].astype(f32)) + (
-            before[:, 1152:1280].astype(f32) + later[:, 1152:1280].astype(f32)
-        )
-        few[...] = total + twin
-        for i, source in enumerate((own, before, later, opposite)):
+def finish_attention_first(place, blocks, earlier):
+    summed = jnp.sum(blocks.reshape(16, 2, 32, 640).astype(f32), axis=0).astype(bf16)
+    pieces = lax.optimization_barrier((*around(summed), earlier))[:4]
+
+    def body(place, own, before, later, opposite, inner, outer, mixer, gain, regain):
+        sources = (own, before, later, opposite)
+        halves = []
+        for core in range(2):
+            one, two, three, four = (x[core, :, 512:640].astype(f32) for x in sources)
+            halves.append((one + four) + (two + three))
+        write_few(halves[0] + halves[1], mixer, gain, regain)
+        for i, source in enumerate(sources):
             z = quarter(place, i)
             for core in range(2):
-                low = core * 640
                 index = z * 2 + core
                 inner[:, pl.ds(pl.multiple_of(index * 384, 128), 384)] = source[
-                    :, low : low + 384
+                    core, :, 0:384
                 ].astype(f32)
                 outer[:, pl.ds(pl.multiple_of(index * 128, 128), 128)] = source[
-                    :, low + 384 : low + 512
+                    core, :, 384:512
                 ].astype(f32)
 
-    outs = (shape(32, 3072, dtype=f32), shape(32, D, dtype=f32), shape(32, 128, dtype=f32))
-    inner, outer, few = call(body, outs, (place, *pieces), 1000000, 1000000, name="attention_out")
-    return inner, outer, few[:, 0:2], few[:, 2], few[:, 3]
+    outs = (shape(32, 3072, dtype=f32), shape(32, D, dtype=f32), *FEW)
+    inner, outer, mixer, gain, regain = call(
+        body, outs, (place, *pieces), 1000000, 1000000, name="attention_out"
+    )
+    return inner, outer, mixer.T, gain.reshape(32), regain.reshape(32)
 
 
 def on_device(
@@ -1146,11 +1211,11 @@
     reduce_second,
 ):
     place = jnp.stack([lax.axis_index("z"), lax.axis_index("c")]).astype(jnp.int32)
-    gathered = lax.all_gather(
+    gathered_first = lax.all_gather(
         jnp.concatenate(
             [
                 pack_attention(inner_first, outer_first, mixer_first, gain_first, regain_first),
-                pack_attention(inner_second, outer_second, mixer_second, gain_second, regain_second),
+                pack_feed_first(widen_first, narrow_first),
             ],
             axis=1,
         ),
@@ -1158,27 +1223,28 @@
         axis=0,
         tiled=True,
     )
-    gathered_feed_first = lax.all_gather(
-        pack_feed_first(widen_first, narrow_first), PLANE, axis=0, tiled=True
+    gathered_second = lax.all_gather(
+        pack_attention(inner_second, outer_second, mixer_second, gain_second, regain_second),
+        ("x", "y", "c"),
+        axis=0,
+        tiled=True,
     )
     gathered_feed = lax.all_gather(
-        pack_feed_second(widen_second, narrow_second), PLANE, axis=0, tiled=True
+        pack_feed_second(widen_second, narrow_second), ("x", "y", "c"), axis=0, tiled=True
     )
     column_first, row_first = slots_first(routes_first)
     column_second, row_second = slots_second(routes_second)
     expander, reducer = expand_first[0], reduce_first[0]
 
-    pair, joint, middle, normed_two, shares, send = first_front(tokens, gathered, row_first)
+    pair, joint, middle, normed_two, shares, send = first_front(tokens, gathered_first, row_first)
     received = exchange(send)
     group = gather_line(normed_two)
     received = after(received, group)
     active, slope, parts = owner_forward(received, expander, reducer)
     back = exchange(parts)
-    group_twin = swap(group)
-    other, own, active_feed, slope_feed, widen_one, narrow_one = feed_forward(
-        group, group_twin, gathered_feed_first
-    )
-    dense_own, dense_parts = scatter_column(other, own)
+    dense_own, dense_parts, active_feed, slope_feed, narrow_one = feed_forward(
+        after(group, parts), gathered_first
+    )
 
     output, stream, dense, expert, pair_s, joint_s, middle_s, feed_s, shares_s, send = second_front(
         back,
@@ -1188,22 +1254,31 @@
         dense_own,
         dense_parts,
         cotangent,
-        gathered,
+        gathered_second,
         row_second,
     )
     arrived = exchange(send)
     feed_flipped = flip(feed_s)
-    feed_blocks = (feed_s, feed_flipped, swap(feed_s), swap(feed_flipped))
-    arrived = after(arrived, *feed_blocks)
+    arrived = after(arrived, feed_flipped)
     line = lax.all_gather(after(pair, arrived), COLUMN, axis=0, tiled=True)
     rows, incoming_s, active_s, grad_s, sent = owner_both(
         arrived, expand_second[0], reduce_second[0]
     )
     back = exchange(sent)
-    feed_blocks = lax.optimization_barrier((*feed_blocks, sent))[:4]
-    terms, terms_twin, feed_gradient = feed_both(feed_blocks, gathered_feed)
-    got = swap(terms_twin)
-    flipped = flip((terms[ROWS:] + got[ROWS:].astype(f32)).astype(bf16))
+    terms, terms_partner, active_second, grad_second, feed_sent = feed_both(
+        place, feed_s, after(feed_flipped, sent), gathered_feed
+    )
+    flipped = flip(terms_partner)
+    feed_gradient = feed_gradients(
+        place,
+        feed_s,
+        feed_flipped,
+        swap(jnp.concatenate([feed_s, feed_flipped], axis=0)),
+        active_second,
+        grad_second,
+        swap(feed_sent),
+    )
+    back = after(back, feed_gradient)
     pair_twin = swap(pair_s)
     back = after(back, line, pair_twin)
     output_two, upstream, mine, other, small, grad_dense, send = second_back(
@@ -1214,12 +1289,11 @@
         middle_s,
         shares_s,
         terms,
-        got,
         flipped,
         feed_s,
         joint_s,
         stream,
-        gathered,
+        gathered_second,
         shares,
         row_first,
     )
@@ -1227,20 +1301,33 @@
     grad_expand_two = dot_tn(rows, grad_s)
     grad_reduce_two = dot_tn(active_s, after(incoming_s, send))
 
-    incoming = after(exchange(send), grad_expand_two, grad_reduce_two)
     grad_group = gather_line(grad_dense)
-    grad_group_twin = swap(grad_group)
-    feed_other, feed_own, grad_hidden = feed_backward(
-        grad_group, grad_group_twin, slope_feed, widen_one, narrow_one
+    incoming = after(exchange(send), grad_expand_two, grad_reduce_two, grad_group)
+    grad_first, grad_rows = owner_backward(incoming, slope, expander, reducer)
+    feed_own, feed_parts, grad_hidden, feed_sent = feed_backward(
+        place,
+        after(grad_group, grad_rows),
+        active_feed,
+        slope_feed,
+        narrow_one,
+        gathered_first,
     )
     packed = weights_second(feed_gradient, pair_s, pair_twin, mine, swap(other), small)
     packed = lax.psum_scatter(packed, PLANE, scatter_dimension=0, tiled=True)
-    grad_first, grad_rows = owner_backward(incoming, slope, expander, reducer)
     back = exchange(grad_rows)
-    feed_own, feed_parts = scatter_column(feed_other, feed_own)
     feed_packed = weights_feed(
-        group, group_twin, grad_hidden, active_feed, grad_group, grad_group_twin
-    )
+        place,
+        group,
+        swap(group),
+        grad_hidden,
+        active_feed,
+        swap(feed_sent),
+        grad_group,
+        swap(grad_group),
+    )
+    grad_expand_one = dot_tn(received, grad_first)
+    grad_reduce_one = dot_tn(active, incoming)
+    back = after(back, grad_expand_one, grad_reduce_one, *feed_parts)
     back = after(back, feed_packed)
     feed_sums = exchange_plane(after(feed_packed, back))
     gradient_tokens, mine, other, small = first_back(
@@ -1257,24 +1344,23 @@
         normed_two,
         joint,
         tokens,
-        gathered,
+        gathered_first,
     )
     got = swap(other)
     ahead = [jnp.concatenate([mine[i], got[i]], axis=0) for i in (1, 2, 3)]
     parts = (shift(ahead[0], "z", 1), shift(ahead[1], "z", -1), shift(ahead[2], "z", 2))
-    packed = lax.all_gather(after(packed, mine), "z", axis=0)
-    grad_first = after(grad_first, mine)
-    grad_expand_one = dot_tn(received, grad_first)
-    grad_reduce_one = dot_tn(active, after(incoming, mine))
     first_packed = weights_first(place, line, mine, got, parts, small)
     first_packed = after(first_packed, feed_sums)
-    blocks = exchange_plane(first_packed)
+    packed = lax.all_gather(after(packed, first_packed), "z", axis=0)
+    blocks = lax.all_to_all(
+        first_packed.reshape(32, 32, 640), ("x", "y", "c"), split_axis=0, concat_axis=0, tiled=True
+    )
     feed_finals = finish_feed_first(place, feed_sums)
+    packed = after(packed, feed_finals)
     feed_finals_second, finals_second, few_second = finish_second(place, packed)
-    blocks = after(
-        blocks, feed_finals, feed_finals_second, finals_second, grad_expand_one, grad_reduce_one
-    )
-    inner, outer, *few_first = finish_attention_first(place, blocks)
+    inner, outer, *few_first = finish_attention_first(
+        place, blocks, (feed_finals, feed_finals_second, finals_second)
+    )
     return (
         (output, output_two, gradient_tokens)
         + (inner, outer)

time: 604 us -> 541 us (0.90)
  waiting for transfers between devices: 266 us -> 224 us
  local copies, waits for them, and re-layouts: 34.5 us -> 24.8 us
  other arithmetic: 15 us -> 5.62 us
  starting transfers between devices: 104 us -> 96.4 us
    all_to_all x6, waiting for transfers between devices: 42.2 us -> 8.59 us  [exchange(): moved = lax.all_to_all(blocks, ALL, split_axis=0, concat_axis=0, tiled=True)]
    ppermute x36 -> x31, waiting for transfers between devices: 115 us -> 99.7 us  [shift(): lax.ppermute(value, axis, [(i, (i + step) % size) for i in range(size)])]
    pallas_call x11 -> x12, Pallas kernels: 80.5 us -> 91.7 us  [call(): pl.pallas_call(body, out_shape=outs, in_specs=[pl.BlockSpec(memory_space=...]
    all_gather x3, waiting for transfers between devices: 4.47 us -> 15.2 us  [the longest x1 15.2 us: on_device(): packed = lax.all_gather(after(packed, first_packed), 'z', axis=0)]
    all_to_all x2 -> x1, starting transfers between devices: 12.6 us -> 4.55 us  [exchange_plane(): lax.all_to_all(blocks, PLANE, split_axis=0, concat_axis=0, tiled=True)]
    all_to_all x0 -> x1, starting transfers between devices: none -> 7.48 us  [on_device(): lax.all_to_all(first_packed.reshape(32, 32, 640), ('x', 'y', 'c'), split_...]
    ppermute x36 -> x31, starting transfers between devices: 38.9 us -> 34.2 us  [shift(): lax.ppermute(value, axis, [(i, (i + step) % size) for i in range(size)])]
    unnamed x100 -> x120, local copies, waits for them, and re-layouts: 15.9 us -> 14.3 us
  transfers between devices with their start and end apart: 52 -> 47, of which waited for: 25 -> 22; matrix products, arithmetic and copies ran while one was open for 9% -> 7% of each run, Pallas kernels for 19% -> 22%
where the time goes in v3:
time: 541 us; the launch traced here: 531 us
  waiting for transfers between devices  224 us (41%)
  Pallas kernels  141 us (26%)
  starting transfers between devices  96.4 us (18%)
  local copies, waits for them, and re-layouts  24.8 us (5%)
  matrix products  23.9 us (4%)
  between operations  15.5 us (3%)
  other arithmetic  5.62 us (1%)
    ppermute x31, waiting for transfers between devices, shift(): lax.ppermute(value, axis, [(i, (i + step) % size) for i in range(size)])  99.7 us
    pallas_call x12, Pallas kernels, call(): pl.pallas_call(body, out_shape=outs, in_specs=[pl.BlockSpec(memory_space=...  91.7 us
    all_gather x1, waiting for transfers between devices, on_device(): lax.all_gather(jnp.concatenate([pack_attention(inner_first, outer_first,...  60 us
    all_to_all x6, starting transfers between devices, exchange(): moved = lax.all_to_all(blocks, ALL, split_axis=0, concat_axis=0, tiled=True)  47.5 us
    ppermute x2, waiting for transfers between devices, flip(): return lax.ppermute(value, 'z', [(0, 1), (1, 0), (2, 3), (3, 2)])  40.1 us
    pallas_call x3, Pallas kernels, grid_call(): pl.pallas_call(body, grid=grid, in_specs=in_specs, out_shape=outs, out_sp...  35.1 us
    ppermute x31, starting transfers between devices, shift(): lax.ppermute(value, axis, [(i, (i + step) % size) for i in range(size)])  34.2 us
    dot_general x4, matrix products, dot_tn(): lax.dot_general(a, b, (((0,), (0,)), ((), ())), preferred_element_type=f32)  23.9 us
  transfers between devices with their start and end apart: 47, of which 22 were waited for; matrix products, arithmetic and copies ran while one was open for 7% of the time, Pallas kernels for 22%

profile of v3, /device:TPU:0, one launch (start us, length us, event | category | flops | bytes accessed | tf_op | source)
XLA Modules:
  0.0 530.9 jit_solution(14782083756120938252)
XLA Ops:
  17.3 60.0 %all-gather.7.cloned.1.call-done.far = bf16[1024,6272]{1,0:T(8,128)(2,1)} async-done(((bf16[32,6272]{1,0:T(8,128)(2,1)}), bf16[1024,6272]{1,0:T(8,128)(2,1)}) %all-gather.7.cloned.1.call-update) | async-done | bytes 12845072 | tf_op jit(solution)/shard_map/all_gather | solution.py:1214
  77.3 7.5 %front.1 = (bf16[128,2048]{1,0:T(8,128)(2,1)}, bf16[128,3072]{1,0:T(8,128)(2,1)}, f32[128,1024]{1,0:T(8,128)}, bf16[128,1024]{1,0:T(8,128)(2,1)}, f32[128,128]{1,0:T(8,128)}, /*index=5*/bf16[1024,1024]{1,0:T(8,128)(2,1)}) custom-call(bf16[128,1024]{1,0:T(8,128)(2,1)} %tokens.3, bf16[1024,6272]{1,0:T(8,128)(2,1)} %all-gather.7.cloned.1.call-done.far, ...), custom_call_target="tpu_custom_call" | custom-call | flops 1300000000 | bytes 14000000 | tf_op jit(solution)/shard_map/front/pallas_call | solution.py:78
  84.8 8.3 %all-to-all-start = ((bf16[128,8,1024]{2,1,0:T(8,128)(2,1)}), bf16[128,8,1024]{2,1,0:T(8,128)(2,1)S(1)}, u32[]{:S(2)}, u32[]{:S(2)}) async-start(bf16[128,8,1024]{2,1,0:T(8,128)(2,1)} %bitcast.112), calls=%async_computation | async-start | bytes 4194304 | tf_op jit(solution)/shard_map/all_to_all | solution.py:1011
  98.0 26.2 %collective-permute-done = bf16[128,1024]{1,0:T(8,128)(2,1)S(1)} collective-permute-done((bf16[128,1024]{1,0:T(8,128)(2,1)S(1)}, bf16[128,1024]{1,0:T(8,128)(2,1)S(1)}, u32[]{:S(2)}, u32[]{:S(2)}) %collective-permute-start) | collective-permute-done | bytes 262176 | tf_op jit(solution)/shard_map/ppermute | solution.py:27
  131.5 9.1 %owner.1 = (bf16[1024,1024]{1,0:T(8,128)(2,1)}, bf16[1024,1024]{1,0:T(8,128)(2,1)}, bf16[1024,1024]{1,0:T(8,128)(2,1)}) custom-call(bf16[1024,1024]{1,0:T(8,128)(2,1)} %bitcast.104, bf16[1024,1024]{1,0:T(8,128)(2,1)} %bitcast.126, bf16[1024,1024]{1,0:T(8,128)(2,1)} %bitcast.128), custom_call_target="tpu_custom_call" | custom-call | flops 4300000256 | bytes 12000000 | tf_op jit(solution)/shard_map/owner/pallas_call | solution.py:781
  140.6 7.9 %all-to-all-start.1 = ((bf16[128,8,1024]{2,1,0:T(8,128)(2,1)}), bf16[128,8,1024]{2,1,0:T(8,128)(2,1)S(1)}, u32[]{:S(2)}, u32[]{:S(2)}) async-start(bf16[128,8,1024]{2,1,0:T(8,128)(2,1)} %bitcast.111), calls=%async_computation.1 | async-start | bytes 4194304 | tf_op jit(solution)/shard_map/all_to_all | solution.py:1011
  148.5 8.3 %feed_one.1 = (f32[128,1024]{1,0:T(8,128)}, bf16[128,1024]{1,0:T(8,128)(2,1)}, bf16[128,1024]{1,0:T(8,128)(2,1)}, bf16[128,1024]{1,0:T(8,128)(2,1)}, bf16[512,10...) custom-call(bf16[512,1024]{1,0:T(8,128)(2,1)} %copy-done.6, ...), custom_call_target="tpu_custom_call" | custom-call | flops 1000000 | bytes 1000000 | tf_op jit(solution)/shard_map/feed_one/pallas_call | solution.py:78
  162.5 16.8 %collective-permute-done.3.part_a = bf16[128,1024]{1,0:T(8,128)(2,1)S(1)} collective-permute-done((bf16[128,1024]{1,0:T(8,128)(2,1)}, bf16[128,1024]{1,0:T(8,128)(2,1)S(1)}, u32[]{:S(2)}, u32[]{:S(2)}) %collective-permute-start.3) | collective-permute-done | bytes 262176 | tf_op jit(solution)/shard_map/ppermute | solution.py:27
  180.7 6.2 %collective-permute-done.5.part_c = bf16[128,1024]{1,0:T(8,128)(2,1)S(1)} collective-permute-done((bf16[128,1024]{1,0:T(8,128)(2,1)}, bf16[128,1024]{1,0:T(8,128)(2,1)S(1)}, u32[]{:S(2)}, u32[]{:S(2)}) %collective-permute-start.5) | collective-permute-done | bytes 262176 | tf_op jit(solution)/shard_map/ppermute | solution.py:27
  188.2 9.6 %between.1 = (bf16[128,1024]{1,0:T(8,128)(2,1)}, f32[128,1024]{1,0:T(8,128)}, f32[128,1024]{1,0:T(8,128)}, f32[128,1024]{1,0:T(8,128)}, bf16[128,2048]{1,0:T(8,1...) custom-call(bf16[1024,1024]{1,0:T(8,128)(2,1)} %bitcast.96, ...), custom_call_target="tpu_custom_call" | custom-call | flops 1800000000 | bytes 20000000 | tf_op jit(solution)/shard_map/between/pallas_call | solution.py:78
  197.9 7.0 %all-to-all-start.2 = ((bf16[128,8,1024]{2,1,0:T(8,128)(2,1)}), bf16[128,8,1024]{2,1,0:T(8,128)(2,1)S(1)}, u32[]{:S(2)}, u32[]{:S(2)}) async-start(bf16[128,8,1024]{2,1,0:T(8,128)(2,1)} %bitcast.114), calls=%async_computation.2 | async-start | bytes 4194304 | tf_op jit(solution)/shard_map/all_to_all | solution.py:1011
  206.3 33.8 %collective-permute-done.6.partner = bf16[128,2048]{1,0:T(8,128)(2,1)S(1)} collective-permute-done((bf16[128,2048]{1,0:T(8,128)(2,1)S(1)}, bf16[128,2048]{1,0:T(8,128)(2,1)S(1)}, u32[]{:S(2)}, u32[]{:S(2)}) %collective-permute-start.6) | collective-permute-done | bytes 524320 | tf_op jit(solution)/shard_map/ppermute | solution.py:35
  241.5 17.3 %owner_both.1 = (bf16[512,1024]{1,0:T(8,128)(2,1)}, bf16[512,1024]{1,0:T(8,128)(2,1)}, bf16[512,2048]{1,0:T(8,128)(2,1)}, bf16[512,2048]{1,0:T(8,128)(2,1)}, bf16[1024,1024]{1,0:T(8,128)(2,1)}) custom-call(bf16[1024,1024]{1,0:T(8,128)(2,1)} %bitcast.113, bf16[1024,2048]{1,0:T(8,128)(2,1)} %bitcast.124, bf16[2048,1024]{1,0:T(8,128)(2,1)} %bitcast.125), custom_call_target="tpu_custom_call" | custom-call | flops 8999999488 | bytes 20000000 | tf_op jit(solution)/shard_map/owner_both/pallas_call | solution.py:781
  258.8 9.9 %all-to-all-start.3 = ((bf16[128,8,1024]{2,1,0:T(8,128)(2,1)}), bf16[128,8,1024]{2,1,0:T(8,128)(2,1)S(1)}, u32[]{:S(2)}, u32[]{:S(2)}) async-start(bf16[128,8,1024]{2,1,0:T(8,128)(2,1)} %bitcast.110), calls=%async_computation.3 | async-start | bytes 4194304 | tf_op jit(solution)/shard_map/all_to_all | solution.py:1011
  270.5 10.8 %feed.1 = (f32[128,2048]{1,0:T(8,128)}, bf16[128,2048]{1,0:T(8,128)(2,1)}, bf16[256,2048]{1,0:T(8,128)(2,1)}, bf16[256,2048]{1,0:T(8,128)(2,1)}, bf16[256,2048]{1,0:T(8,128)(2,1)}) custom-call(s32[2]{0:T(128)} %pad_add_fusion.place, bf16[128,2048]{1,0:T(8,128)(2,1)} %get-tuple-element.124.mine.feed, bf16[128,2048]{1,0:T(8,128)(2,1)} %copy-done.8, ...), custom_call_target="tpu_custom_call" | custom-call | flops 1000000 | bytes 1000000 | tf_op jit(solution)/shard_map/feed/pallas_call | solution.py:78
  285.6 8.1 %feed_gradients.1.packed = bf16[1024,4224]{1,0:T(8,128)(2,1)} custom-call(s32[2]{0:T(128)} %pad_add_fusion.place, bf16[128,2048]{1,0:T(8,128)(2,1)} %get-tuple-element.124.mine.feed, bf16[128,2048]{1,0:T(8,128)(2,1)} %copy-done.8, bf16[256,2048]{1,0:T(8,128)(2,1)} %copy-done.16, bf16[256,2048]{1,0:T(8,128)(2,1)} %get-tuple-element.128.active, ...), custom_call_target="tpu_custom_call" | custom-call | flops 1000000 | bytes 1000000 | tf_op jit(solution)/shard_map/feed_gradients/pallas_call | solution.py:960
  299.2 6.3 %collective-permute-done.10.flipped = bf16[128,2048]{1,0:T(8,128)(2,1)} collective-permute-done((bf16[128,2048]{1,0:T(8,128)(2,1)}, bf16[128,2048]{1,0:T(8,128)(2,1)}, u32[]{:S(2)}, u32[]{:S(2)}) %collective-permute-start.10) | collective-permute-done | bytes 524320 | tf_op jit(solution)/shard_map/ppermute | solution.py:35
  305.4 14.1 %turn.1 = (bf16[128,1024]{1,0:T(8,128)(2,1)}, f32[128,1024]{1,0:T(8,128)}, bf16[128,2048]{1,0:T(8,128)(2,1)}, bf16[128,2048]{1,0:T(8,128)(2,1)}, f32[8,1024]{1,0...) custom-call(s32[2]{0:T(128)} %pad_add_fusion.place, bf16[1024,1024]{1,0:T(8,128)(2,1)} %bitcast.98, ...), custom_call_target="tpu_custom_call" | custom-call | flops 1000000 | bytes 1000000 | tf_op jit(solution)/shard_map/turn/pallas_call | solution.py:78
  322.5 6.0 %second_weights.1 = bf16[1024,4224]{1,0:T(8,128)(2,1)} custom-call(bf16[1024,4224]{1,0:T(8,128)(2,1)} %feed_gradients.1.packed, bf16[128,2048]{1,0:T(8,128)(2,1)} %get-tuple-element.134.pair, bf16[128,2048]{1,0:T(8,128)(2,1)} %collective-permute-done.9.pair_twin, bf16[128,2048]{1,0:T(8,128)(2,1)} %get-tuple-element.180.mine, ...), custom_call_target="tpu_custom_call", output_to_operand_aliasing={{}: (0, {})} | custom-call | flops 1000000 | bytes 1000000 | tf_op jit(solution)/shard_map/second_weights/pallas_call | solution.py:659
  328.6 9.3 %all-to-all-start.4 = ((bf16[128,8,1024]{2,1,0:T(8,128)(2,1)}), bf16[128,8,1024]{2,1,0:T(8,128)(2,1)S(1)}, u32[]{:S(2)}, u32[]{:S(2)}) async-start(bf16[128,8,1024]{2,1,0:T(8,128)(2,1)} %bitcast.108), calls=%async_computation.4 | async-start | bytes 4194304 | tf_op jit(solution)/shard_map/all_to_all | solution.py:1011
  343.0 7.5 %fusion.23 = f32[2048,1024]{1,0:T(8,128)} fusion(bf16[512,2048]{1,0:T(8,128)(2,1)} %get-tuple-element.147, bf16[512,1024]{1,0:T(8,128)(2,1)S(1)} %copy-done.51), kind=kOutput, calls=%fused_computation.86 | convolution fusion | flops 2147483648 | bytes 11534336 | tf_op jit(solution)/shard_map/dot_general | solution.py:43
  350.5 5.8 %fusion.22 = f32[1024,2048]{1,0:T(8,128)} fusion(bf16[512,1024]{1,0:T(8,128)(2,1)S(1)} %copy-done.53, bf16[512,2048]{1,0:T(8,128)(2,1)S(1)} %copy-done.52), kind=kOutput, calls=%fused_computation.85 | convolution fusion | flops 2147483648 | bytes 11534336 | tf_op jit(solution)/shard_map/dot_general | solution.py:43
  362.7 11.7 %collective-permute-done.13 = bf16[128,1024]{1,0:T(8,128)(2,1)S(1)} collective-permute-done((bf16[128,1024]{1,0:T(8,128)(2,1)S(1)}, bf16[128,1024]{1,0:T(8,128)(2,1)S(1)}, u32[]{:S(2)}, u32[]{:S(2)}) %collective-permute-start.13) | collective-permute-done | bytes 262176 | tf_op jit(solution)/shard_map/ppermute | solution.py:27
  379.5 8.8 %owner_back.1 = (bf16[1024,1024]{1,0:T(8,128)(2,1)}, bf16[1024,1024]{1,0:T(8,128)(2,1)}) custom-call(bf16[1024,1024]{1,0:T(8,128)(2,1)} %bitcast.106, bf16[1024,1024]{1,0:T(8,128)(2,1)} %get-tuple-element.152.slope, bf16[1024,1024]{1,0:T(8,128)(2,1)} %bitcast.127, bf16[1024,1024]{1,0:T(8,128)(2,1)} %bitcast.129), custom_call_target="tpu_custom_call" | custom-call | flops 4300000256 | bytes 12000000 | tf_op jit(solution)/shard_map/owner_back/pallas_call | solution.py:781
  394.0 7.5 %feed_one_back.1 = (f32[128,1024]{1,0:T(8,128)}, bf16[128,1024]{1,0:T(8,128)(2,1)}, bf16[128,1024]{1,0:T(8,128)(2,1)}, bf16[128,1024]{1,0:T(8,128)(2,1)}, bf16[5...) custom-call(s32[2]{0:T(128)} %pad_add_fusion.place, bf16[512,1024]{1,0:T(8,128)(2,1)} %constant_dynamic-update-slice_fusion.4.group.inc, ...), custom_call_target="tpu_custom_call" | custom-call | flops 1000000 | bytes 1000000 | tf_op jit(solution)/shard_map/feed_one_back/pallas_call | solution.py:78
  404.8 6.2 %fusion.25 = f32[1024,1024]{1,0:T(8,128)} fusion(bf16[1024,1024]{1,0:T(8,128)(2,1)} %get-tuple-element.155, bf16[1024,1024]{1,0:T(8,128)(2,1)S(1)} %bitcast.107), kind=kOutput, calls=%fused_computation.88 | convolution fusion | flops 2147483648 | bytes 8388608 | tf_op jit(solution)/shard_map/dot_general | solution.py:43
  417.4 6.8 %feed_weights.1 = bf16[1024,1024]{1,0:T(8,128)(2,1)} custom-call(s32[2]{0:T(128)} %pad_add_fusion.place, bf16[512,1024]{1,0:T(8,128)(2,1)} %copy-done.6, bf16[512,1024]{1,0:T(8,128)(2,1)} %collective-permute-done.17.group_twin, bf16[512,1024]{1,0:T(8,128)(2,1)} %get-tuple-element.164.grad_hidden, bf16[512,1024]{1,0:T(8,128)(2,1)} %get-tuple-element.157.active, ...), custom_call_target="tpu_custom_call" | custom-call | flops 1000000 | bytes 1000000 | tf_op jit(solution)/shard_map/feed_weights/pallas_call | solution.py:78
  424.3 9.8 %collective-permute-done.15.part_b = bf16[128,1024]{1,0:T(8,128)(2,1)S(1)} collective-permute-done((bf16[128,1024]{1,0:T(8,128)(2,1)}, bf16[128,1024]{1,0:T(8,128)(2,1)S(1)}, u32[]{:S(2)}, u32[]{:S(2)}) %collective-permute-start.15) | collective-permute-done | bytes 262176 | tf_op jit(solution)/shard_map/ppermute | solution.py:27
  440.8 13.5 %back.1 = (f32[128,1024]{1,0:T(8,128)}, bf16[4,128,512]{2,1,0:T(8,128)(2,1)}, bf16[4,128,512]{2,1,0:T(8,128)(2,1)}, f32[8,1024]{1,0:T(8,128)}) custom-call(s32[2]{0:T(128)} %pad_add_fusion.place, bf16[1024,1024]{1,0:T(8,128)(2,1)} %bitcast.97, s32[128,1]{1,0:T(8,128)} %get-tuple-element.215.slot_column, f32[128,1024]{1,0:T(8,128)} %get-tuple-element.167.upstream, ...), custom_call_target="tpu_custom_call" | custom-call | flops 1000000 | bytes 1000000 | tf_op jit(solution)/shard_map/back/pallas_call | solution.py:78
  459.7 7.9 %collective-permute-done.23.part_c = bf16[256,512]{1,0:T(8,128)(2,1)S(1)} collective-permute-done((bf16[256,512]{1,0:T(8,128)(2,1)S(1)}, bf16[256,512]{1,0:T(8,128)(2,1)S(1)}, u32[]{:S(2)}, u32[]{:S(2)}) %collective-permute-start.23) | collective-permute-done | bytes 262176 | tf_op jit(solution)/shard_map/ppermute | solution.py:27
  483.9 7.5 %all-to-all-start.7 = ((bf16[32,32,640]{2,1,0:T(8,128)(2,1)}), bf16[32,32,640]{2,1,0:T(8,128)(2,1)S(1)}, u32[]{:S(2)}, u32[]{:S(2)}) async-start(bf16[32,32,640]{2,1,0:T(8,128)(2,1)} %bitcast.100), calls=%async_computation.7 | async-start | bytes 2621440 | tf_op jit(solution)/shard_map/all_to_all | solution.py:1355
  495.1 15.2 %all-gather.15.cloned.1.call-done = bf16[256,4224]{1,0:T(8,128)(2,1)} async-done(((bf16[64,4224]{1,0:T(8,128)(2,1)}), bf16[256,4224]{1,0:T(8,128)(2,1)}) %all-gather.15.cloned.1.call-update) | async-done | bytes 2162704 | tf_op jit(solution)/shard_map/all_gather | solution.py:1354
  (254 shorter events, 124.8 us)
Async XLA Ops:
  7.3 70.0 %all-gather.7.cloned.1.call-start = ((), (), s32[]{:S(2)}) async-start(), calls=%async_computation.9 | async-start | bytes 13246464 | tf_op jit(solution)/shard_map/all_gather | solution.py:1214
  11.4 151.0 %all-gather.9.cloned.1.call-start = ((), (), s32[]{:S(2)}) async-start(), calls=%async_computation.10 | async-start | bytes 8921088 | tf_op jit(solution)/shard_map/all_gather | solution.py:1226
  12.6 257.8 %all-gather.11.cloned.1.call-start = ((), (), s32[]{:S(2)}) async-start(), calls=%async_computation.11 | async-start | bytes 8650752 | tf_op jit(solution)/shard_map/all_gather | solution.py:1232
  84.8 45.4 %all-to-all-start = ((bf16[128,8,1024]{2,1,0:T(8,128)(2,1)}), bf16[128,8,1024]{2,1,0:T(8,128)(2,1)S(1)}, u32[]{:S(2)}, u32[]{:S(2)}) async-start(bf16[128,8,1024]{2,1,0:T(8,128)(2,1)} %bitcast.112), calls=%async_computation | async-start | bytes 4194304 | tf_op jit(solution)/shard_map/all_to_all | solution.py:1011
  93.1 31.2 %collective-permute-start = (bf16[128,1024]{1,0:T(8,128)(2,1)S(1)}, bf16[128,1024]{1,0:T(8,128)(2,1)S(1)}, u32[]{:S(2)}, u32[]{:S(2)}) collective-permute-start(bf16[128,1024]{1,0:T(8,128)(2,1)S(1)} %copy-done.15), channel_id=1, source_target_pairs={{0,32},{32,64},{64,96},{96,0},{1,33},{33,65},{65,97},{97,1},{2,34}... | collective-permute-start | bytes 786440 | tf_op jit(solution)/shard_map/ppermute | solution.py:27
  94.2 30.1 %collective-permute-start.1 = (bf16[128,1024]{1,0:T(8,128)(2,1)S(1)}, bf16[128,1024]{1,0:T(8,128)(2,1)S(1)}, u32[]{:S(2)}, u32[]{:S(2)}) collective-permute-start(bf16[128,1024]{1,0:T(8,128)(2,1)S(1)} %copy-done.15), channel_id=1, source_target_pairs={{0,96},{32,0},{64,32},{96,64},{1,97},{33,1},{65,33},{97,65},{2,98}... | collective-permute-start | bytes 786440 | tf_op jit(solution)/shard_map/ppermute | solution.py:27
  96.4 33.7 %collective-permute-start.2 = (bf16[128,1024]{1,0:T(8,128)(2,1)S(1)}, bf16[128,1024]{1,0:T(8,128)(2,1)S(1)}, u32[]{:S(2)}, u32[]{:S(2)}) collective-permute-start(bf16[128,1024]{1,0:T(8,128)(2,1)S(1)} %copy-done.15), channel_id=1, source_target_pairs={{0,64},{32,96},{64,0},{96,32},{1,65},{33,97},{65,1},{97,33},{2,66}... | collective-permute-start | bytes 786440 | tf_op jit(solution)/shard_map/ppermute | solution.py:27
  140.6 46.2 %all-to-all-start.1 = ((bf16[128,8,1024]{2,1,0:T(8,128)(2,1)}), bf16[128,8,1024]{2,1,0:T(8,128)(2,1)S(1)}, u32[]{:S(2)}, u32[]{:S(2)}) async-start(bf16[128,8,1024]{2,1,0:T(8,128)(2,1)} %bitcast.111), calls=%async_computation.1 | async-start | bytes 4194304 | tf_op jit(solution)/shard_map/all_to_all | solution.py:1011
  156.9 22.4 %collective-permute-start.3 = (bf16[128,1024]{1,0:T(8,128)(2,1)}, bf16[128,1024]{1,0:T(8,128)(2,1)S(1)}, u32[]{:S(2)}, u32[]{:S(2)}) collective-permute-start(bf16[128,1024]{1,0:T(8,128)(2,1)} %get-tuple-element.119), channel_id=1, source_target_pairs={{0,96},{32,0},{64,32},{96,64},{1,97},{33,1},{65,33},{97,65},{2,98}... | collective-permute-start | bytes 786440 | tf_op jit(solution)/shard_map/ppermute | solution.py:27
  159.9 20.8 %collective-permute-start.4 = (bf16[128,1024]{1,0:T(8,128)(2,1)}, bf16[128,1024]{1,0:T(8,128)(2,1)S(1)}, u32[]{:S(2)}, u32[]{:S(2)}) collective-permute-start(bf16[128,1024]{1,0:T(8,128)(2,1)} %get-tuple-element.120), channel_id=1, source_target_pairs={{0,32},{32,64},{64,96},{96,0},{1,33},{33,65},{65,97},{97,1},{2,34}... | collective-permute-start | bytes 786440 | tf_op jit(solution)/shard_map/ppermute | solution.py:27
  159.9 26.9 %collective-permute-start.5 = (bf16[128,1024]{1,0:T(8,128)(2,1)}, bf16[128,1024]{1,0:T(8,128)(2,1)S(1)}, u32[]{:S(2)}, u32[]{:S(2)}) collective-permute-start(bf16[128,1024]{1,0:T(8,128)(2,1)} %get-tuple-element.121), channel_id=1, source_target_pairs={{0,64},{32,96},{64,0},{96,32},{1,65},{33,97},{65,1},{97,33},{2,66}... | collective-permute-start | bytes 786440 | tf_op jit(solution)/shard_map/ppermute | solution.py:27
  197.9 42.3 %all-to-all-start.2 = ((bf16[128,8,1024]{2,1,0:T(8,128)(2,1)}), bf16[128,8,1024]{2,1,0:T(8,128)(2,1)S(1)}, u32[]{:S(2)}, u32[]{:S(2)}) async-start(bf16[128,8,1024]{2,1,0:T(8,128)(2,1)} %bitcast.114), calls=%async_computation.2 | async-start | bytes 4194304 | tf_op jit(solution)/shard_map/all_to_all | solution.py:1011
  204.9 94.3 %all-gather.13.cloned.1.call-start = ((), (), s32[]{:S(2)}) async-start(), calls=%async_computation.12 | async-start | bytes 4718592 | tf_op jit(solution)/shard_map/all_gather | solution.py:1263
  204.9 35.2 %collective-permute-start.6 = (bf16[128,2048]{1,0:T(8,128)(2,1)S(1)}, bf16[128,2048]{1,0:T(8,128)(2,1)S(1)}, u32[]{:S(2)}, u32[]{:S(2)}) collective-permute-start(bf16[128,2048]{1,0:T(8,128)(2,1)S(1)} %copy-done.3), channel_id=1, source_target_pairs={{0,32},{32,0},{64,96},{96,64},{1,33},{33,1},{65,97},{97,65},{2,34}... | collective-permute-start | bytes 1572872 | tf_op jit(solution)/shard_map/ppermute | solution.py:35
  258.8 40.3 %all-to-all-start.3 = ((bf16[128,8,1024]{2,1,0:T(8,128)(2,1)}), bf16[128,8,1024]{2,1,0:T(8,128)(2,1)S(1)}, u32[]{:S(2)}, u32[]{:S(2)}) async-start(bf16[128,8,1024]{2,1,0:T(8,128)(2,1)} %bitcast.110), calls=%async_computation.3 | async-start | bytes 4194304 | tf_op jit(solution)/shard_map/all_to_all | solution.py:1011
  268.8 210.0 %reduce-scatter.2.cloned.1.call-start = ((), (), s32[]{:S(2)}) async-start(), calls=%async_computation.13 | async-start | bytes 9191424 | tf_op jit(solution)/shard_map/reduce_scatter | solution.py:1316
  282.3 16.8 %collective-permute-start.9 = (bf16[128,2048]{1,0:T(8,128)(2,1)}, bf16[128,2048]{1,0:T(8,128)(2,1)}, u32[]{:S(2)}, u32[]{:S(2)}) collective-permute-start(bf16[128,2048]{1,0:T(8,128)(2,1)} %get-tuple-element.134.pair), channel_id=1, source_target_pairs={{0,1},{1,0},{2,3},{3,2},{4,5},{5,4},{6,7},{7,6},{8,9},{9,8},{10,11... | collective-permute-start | bytes 1572872 | tf_op jit(solution)/shard_map/ppermute | solution.py:27
  282.4 23.0 %collective-permute-start.10 = (bf16[128,2048]{1,0:T(8,128)(2,1)}, bf16[128,2048]{1,0:T(8,128)(2,1)}, u32[]{:S(2)}, u32[]{:S(2)}) collective-permute-start(bf16[128,2048]{1,0:T(8,128)(2,1)} %get-tuple-element.139), channel_id=1, source_target_pairs={{0,32},{32,0},{64,96},{96,64},{1,33},{33,1},{65,97},{97,65},{2,34}... | collective-permute-start | bytes 1572872 | tf_op jit(solution)/shard_map/ppermute | solution.py:35
  328.6 49.6 %all-to-all-start.4 = ((bf16[128,8,1024]{2,1,0:T(8,128)(2,1)}), bf16[128,8,1024]{2,1,0:T(8,128)(2,1)S(1)}, u32[]{:S(2)}, u32[]{:S(2)}) async-start(bf16[128,8,1024]{2,1,0:T(8,128)(2,1)} %bitcast.108), calls=%async_computation.4 | async-start | bytes 4194304 | tf_op jit(solution)/shard_map/all_to_all | solution.py:1011
  337.8 23.4 %collective-permute-start.11 = (bf16[128,1024]{1,0:T(8,128)(2,1)S(1)}, bf16[128,1024]{1,0:T(8,128)(2,1)S(1)}, u32[]{:S(2)}, u32[]{:S(2)}) collective-permute-start(bf16[128,1024]{1,0:T(8,128)(2,1)S(1)} %copy-done.27), channel_id=1, source_target_pairs={{0,32},{32,64},{64,96},{96,0},{1,33},{33,65},{65,97},{97,1},{2,34}... | collective-permute-start | bytes 786440 | tf_op jit(solution)/shard_map/ppermute | solution.py:27
  339.2 22.8 %collective-permute-start.12 = (bf16[128,1024]{1,0:T(8,128)(2,1)S(1)}, bf16[128,1024]{1,0:T(8,128)(2,1)S(1)}, u32[]{:S(2)}, u32[]{:S(2)}) collective-permute-start(bf16[128,1024]{1,0:T(8,128)(2,1)S(1)} %copy-done.27), channel_id=1, source_target_pairs={{0,96},{32,0},{64,32},{96,64},{1,97},{33,1},{65,33},{97,65},{2,98}... | collective-permute-start | bytes 786440 | tf_op jit(solution)/shard_map/ppermute | solution.py:27
  341.3 33.1 %collective-permute-start.13 = (bf16[128,1024]{1,0:T(8,128)(2,1)S(1)}, bf16[128,1024]{1,0:T(8,128)(2,1)S(1)}, u32[]{:S(2)}, u32[]{:S(2)}) collective-permute-start(bf16[128,1024]{1,0:T(8,128)(2,1)S(1)} %copy-done.27), channel_id=1, source_target_pairs={{0,64},{32,96},{64,0},{96,32},{1,65},{33,97},{65,1},{97,33},{2,66}... | collective-permute-start | bytes 786440 | tf_op jit(solution)/shard_map/ppermute | solution.py:27
  388.3 46.5 %all-to-all-start.5 = ((bf16[128,8,1024]{2,1,0:T(8,128)(2,1)}), bf16[128,8,1024]{2,1,0:T(8,128)(2,1)S(1)}, u32[]{:S(2)}, u32[]{:S(2)}) async-start(bf16[128,8,1024]{2,1,0:T(8,128)(2,1)} %bitcast.109), calls=%async_computation.5 | async-start | bytes 4194304 | tf_op jit(solution)/shard_map/all_to_all | solution.py:1011
  393.4 17.5 %collective-permute-start.17 = (bf16[512,1024]{1,0:T(8,128)(2,1)S(1)}, bf16[512,1024]{1,0:T(8,128)(2,1)}, u32[]{:S(2)}, u32[]{:S(2)}) collective-permute-start(bf16[512,1024]{1,0:T(8,128)(2,1)S(1)} %copy-done.7), channel_id=1, source_target_pairs={{0,1},{1,0},{2,3},{3,2},{4,5},{5,4},{6,7},{7,6},{8,9},{9,8},{10,11... | collective-permute-start | bytes 3145736 | tf_op jit(solution)/shard_map/ppermute | solution.py:27
  393.5 24.0 %collective-permute-start.19 = (bf16[512,1024]{1,0:T(8,128)(2,1)}, bf16[512,1024]{1,0:T(8,128)(2,1)}, u32[]{:S(2)}, u32[]{:S(2)}) collective-permute-start(bf16[512,1024]{1,0:T(8,128)(2,1)} %constant_dynamic-update-slice_fusion.4.group.inc), channel_id=1, source_target_pairs={{0,1},{1,0},{2,3},{3,2},{4,5},{5,4},{6,7},{7,6},{8,9},{9,8},{10,11... | collective-permute-start | bytes 3145736 | tf_op jit(solution)/shard_map/ppermute | solution.py:27
  401.5 15.9 %collective-permute-start.18 = (bf16[512,1024]{1,0:T(8,128)(2,1)}, bf16[512,1024]{1,0:T(8,128)(2,1)}, u32[]{:S(2)}, u32[]{:S(2)}) collective-permute-start(bf16[512,1024]{1,0:T(8,128)(2,1)} %get-tuple-element.165), channel_id=1, source_target_pairs={{0,1},{1,0},{2,3},{3,2},{4,5},{5,4},{6,7},{7,6},{8,9},{9,8},{10,11... | collective-permute-start | bytes 3145736 | tf_op jit(solution)/shard_map/ppermute | solution.py:27
  401.6 22.6 %collective-permute-start.14 = (bf16[128,1024]{1,0:T(8,128)(2,1)}, bf16[128,1024]{1,0:T(8,128)(2,1)S(1)}, u32[]{:S(2)}, u32[]{:S(2)}) collective-permute-start(bf16[128,1024]{1,0:T(8,128)(2,1)} %get-tuple-element.160), channel_id=1, source_target_pairs={{0,96},{32,0},{64,32},{96,64},{1,97},{33,1},{65,33},{97,65},{2,98}... | collective-permute-start | bytes 786440 | tf_op jit(solution)/shard_map/ppermute | solution.py:27
  404.5 29.5 %collective-permute-start.15 = (bf16[128,1024]{1,0:T(8,128)(2,1)}, bf16[128,1024]{1,0:T(8,128)(2,1)S(1)}, u32[]{:S(2)}, u32[]{:S(2)}) collective-permute-start(bf16[128,1024]{1,0:T(8,128)(2,1)} %get-tuple-element.161), channel_id=1, source_target_pairs={{0,32},{32,64},{64,96},{96,0},{1,33},{33,65},{65,97},{97,1},{2,34}... | collective-permute-start | bytes 786440 | tf_op jit(solution)/shard_map/ppermute | solution.py:27
  410.9 23.8 %collective-permute-start.16 = (bf16[128,1024]{1,0:T(8,128)(2,1)S(1)}, bf16[128,1024]{1,0:T(8,128)(2,1)S(1)}, u32[]{:S(2)}, u32[]{:S(2)}) collective-permute-start(bf16[128,1024]{1,0:T(8,128)(2,1)S(1)} %copy-done.50), channel_id=1, source_target_pairs={{0,64},{32,96},{64,0},{96,32},{1,65},{33,97},{65,1},{97,33},{2,66}... | collective-permute-start | bytes 786440 | tf_op jit(solution)/shard_map/ppermute | solution.py:27
  436.1 42.6 %all-to-all-start.6 = ((bf16[16,64,1024]{2,1,0:T(8,128)(2,1)}), bf16[16,64,1024]{2,1,0:T(8,128)(2,1)S(1)}, u32[]{:S(2)}, u32[]{:S(2)}) async-start(bf16[16,64,1024]{2,1,0:T(8,128)(2,1)} %bitcast.95), calls=%async_computation.6 | async-start | bytes 4194304 | tf_op jit(solution)/shard_map/all_to_all | solution.py:1017
  440.7 69.6 %all-gather.15.cloned.1.call-start = ((), (), s32[]{:S(2)}) async-start(), calls=%async_computation.14 | async-start | bytes 2703360 | tf_op jit(solution)/shard_map/all_gather | solution.py:1354
  483.9 27.8 %all-to-all-start.7 = ((bf16[32,32,640]{2,1,0:T(8,128)(2,1)}), bf16[32,32,640]{2,1,0:T(8,128)(2,1)S(1)}, u32[]{:S(2)}, u32[]{:S(2)}) async-start(bf16[32,32,640]{2,1,0:T(8,128)(2,1)} %bitcast.100), calls=%async_computation.7 | async-start | bytes 2621440 | tf_op jit(solution)/shard_map/all_to_all | solution.py:1355
  (70 other events, 403.8 us)
Sparse Core Ops, SparseCore 0:
  11.5 65.7 all-gather.6
  80.1 70.2 all-gather.8
  152.7 60.7 all-gather.10
  240.3 37.3 all-gather.12
  328.7 138.4 reduce-scatter.1
  478.9 31.3 all-gather.14

commit v4 on v3

--- a/solution.py
+++ b/solution.py
@@ -19,7 +19,7 @@
 epsilon = 1e-05
 bf16 = jnp.bfloat16
 f32 = jnp.float32
-LIMIT = 56 * 1024 * 1024
+LIMIT = 52 * 1024 * 1024
 
 
 def shift(value, axis, step):

time: 541 us -> 535 us (0.989)
  local copies, waits for them, and re-layouts: 24.8 us -> 16.8 us
    unnamed x120 -> x86, local copies, waits for them, and re-layouts: 14.3 us -> 7.01 us
  transfers between devices with their start and end apart: 47 -> 47, of which waited for: 22 -> 25; matrix products, arithmetic and copies ran while one was open for 7% -> 7% of each run, Pallas kernels for 22% -> 22%
where the time goes in v4:
time: 535 us; the launch traced here: 525 us
  waiting for transfers between devices  227 us (42%)
  Pallas kernels  136 us (25%)
  starting transfers between devices  99.4 us (19%)
  matrix products  25.6 us (5%)
  local copies, waits for them, and re-layouts  16.8 us (3%)
  between operations  15.4 us (3%)
    ppermute x31, waiting for transfers between devices, shift(): lax.ppermute(value, axis, [(i, (i + step) % size) for i in range(size)])  101 us
    pallas_call x12, Pallas kernels, call(): pl.pallas_call(body, out_shape=outs, in_specs=[pl.BlockSpec(memory_space=...  87.3 us
    all_gather x1, waiting for transfers between devices, on_device(): lax.all_gather(jnp.concatenate([pack_attention(inner_first, outer_first,...  61 us
    all_to_all x6, starting transfers between devices, exchange(): moved = lax.all_to_all(blocks, ALL, split_axis=0, concat_axis=0, tiled=True)  50.1 us
    ppermute x2, waiting for transfers between devices, flip(): return lax.ppermute(value, 'z', [(0, 1), (1, 0), (2, 3), (3, 2)])  39.6 us
    pallas_call x3, Pallas kernels, grid_call(): pl.pallas_call(body, grid=grid, in_specs=in_specs, out_shape=outs, out_sp...  35.7 us
    ppermute x31, starting transfers between devices, shift(): lax.ppermute(value, axis, [(i, (i + step) % size) for i in range(size)])  34.7 us
    dot_general x4, matrix products, dot_tn(): lax.dot_general(a, b, (((0,), (0,)), ((), ())), preferred_element_type=f32)  25.6 us
  transfers between devices with their start and end apart: 47, of which 25 were waited for; matrix products, arithmetic and copies ran while one was open for 7% of the time, Pallas kernels for 22%

profile of v4, /device:TPU:0, one launch (start us, length us, event | category | flops | bytes accessed | tf_op | source)
XLA Modules:
  0.0 525.3 jit_solution(5051276538609583152)
XLA Ops:
  16.3 61.0 %all-gather.7.cloned.1.call-done.far = bf16[1024,6272]{1,0:T(8,128)(2,1)} async-done(((bf16[32,6272]{1,0:T(8,128)(2,1)}), bf16[1024,6272]{1,0:T(8,128)(2,1)}) %all-gather.7.cloned.1.call-update) | async-done | bytes 12845072 | tf_op jit(solution)/shard_map/all_gather | solution.py:1214
  77.3 6.5 %front.1 = (bf16[128,2048]{1,0:T(8,128)(2,1)}, bf16[128,3072]{1,0:T(8,128)(2,1)}, f32[128,1024]{1,0:T(8,128)S(1)}, bf16[128,1024]{1,0:T(8,128)(2,1)S(1)}, f32[12...) custom-call(bf16[128,1024]{1,0:T(8,128)(2,1)S(1)} %copy-done.7, bf16[1024,6272]{1,0:T(8,128)(2,1)} %all-gather.7.cloned.1.call-done.far, ...), custom_call_target="tpu_custom_call" | custom-call | flops 1300000000 | bytes 14000000 | tf_op jit(solution)/shard_map/front/pallas_call | solution.py:78
  84.6 8.8 %all-to-all-start = ((bf16[128,8,1024]{2,1,0:T(8,128)(2,1)}), bf16[128,8,1024]{2,1,0:T(8,128)(2,1)}, u32[]{:S(2)}, u32[]{:S(2)}) async-start(bf16[128,8,1024]{2,1,0:T(8,128)(2,1)} %bitcast.104), calls=%async_computation | async-start | bytes 4194304 | tf_op jit(solution)/shard_map/all_to_all | solution.py:1011
  98.3 25.3 %collective-permute-done = bf16[128,1024]{1,0:T(8,128)(2,1)S(1)} collective-permute-done((bf16[128,1024]{1,0:T(8,128)(2,1)S(1)}, bf16[128,1024]{1,0:T(8,128)(2,1)S(1)}, u32[]{:S(2)}, u32[]{:S(2)}) %collective-permute-start) | collective-permute-done | bytes 262176 | tf_op jit(solution)/shard_map/ppermute | solution.py:27
  123.7 6.5 %collective-permute-done.2 = bf16[128,1024]{1,0:T(8,128)(2,1)S(1)} collective-permute-done((bf16[128,1024]{1,0:T(8,128)(2,1)S(1)}, bf16[128,1024]{1,0:T(8,128)(2,1)S(1)}, u32[]{:S(2)}, u32[]{:S(2)}) %collective-permute-start.2) | collective-permute-done | bytes 262176 | tf_op jit(solution)/shard_map/ppermute | solution.py:27
  130.2 9.4 %owner.1 = (bf16[1024,1024]{1,0:T(8,128)(2,1)}, bf16[1024,1024]{1,0:T(8,128)(2,1)}, bf16[1024,1024]{1,0:T(8,128)(2,1)}) custom-call(bf16[1024,1024]{1,0:T(8,128)(2,1)} %bitcast.7.rows, bf16[1024,1024]{1,0:T(8,128)(2,1)} %bitcast.117, bf16[1024,1024]{1,0:T(8,128)(2,1)} %bitcast.119), custom_call_target="tpu_custom_call" | custom-call | flops 4300000256 | bytes 12000000 | tf_op jit(solution)/shard_map/owner/pallas_call | solution.py:781
  139.7 8.1 %all-to-all-start.1 = ((bf16[128,8,1024]{2,1,0:T(8,128)(2,1)}), bf16[128,8,1024]{2,1,0:T(8,128)(2,1)}, u32[]{:S(2)}, u32[]{:S(2)}) async-start(bf16[128,8,1024]{2,1,0:T(8,128)(2,1)} %bitcast.103), calls=%async_computation.1 | async-start | bytes 4194304 | tf_op jit(solution)/shard_map/all_to_all | solution.py:1011
  147.8 8.1 %feed_one.1 = (f32[128,1024]{1,0:T(8,128)S(1)}, bf16[128,1024]{1,0:T(8,128)(2,1)S(1)}, bf16[128,1024]{1,0:T(8,128)(2,1)S(1)}, bf16[128,1024]{1,0:T(8,128)(2,1)S(...) custom-call(bf16[512,1024]{1,0:T(8,128)(2,1)} %copy-done.3, ...), custom_call_target="tpu_custom_call" | custom-call | flops 1000000 | bytes 1000000 | tf_op jit(solution)/shard_map/feed_one/pallas_call | solution.py:78
  161.8 16.2 %collective-permute-done.3.part_a = bf16[128,1024]{1,0:T(8,128)(2,1)S(1)} collective-permute-done((bf16[128,1024]{1,0:T(8,128)(2,1)S(1)}, bf16[128,1024]{1,0:T(8,128)(2,1)S(1)}, u32[]{:S(2)}, u32[]{:S(2)}) %collective-permute-start.3) | collective-permute-done | bytes 262176 | tf_op jit(solution)/shard_map/ppermute | solution.py:27
  185.6 10.2 %between.1 = (bf16[128,1024]{1,0:T(8,128)(2,1)}, f32[128,1024]{1,0:T(8,128)S(1)}, f32[128,1024]{1,0:T(8,128)}, f32[128,1024]{1,0:T(8,128)}, bf16[128,2048]{1,0:T...) custom-call(bf16[1024,1024]{1,0:T(8,128)(2,1)} %bitcast.11.back, ...), custom_call_target="tpu_custom_call" | custom-call | flops 1800000000 | bytes 20000000 | tf_op jit(solution)/shard_map/between/pallas_call | solution.py:78
  196.6 7.0 %all-to-all-start.2 = ((bf16[128,8,1024]{2,1,0:T(8,128)(2,1)}), bf16[128,8,1024]{2,1,0:T(8,128)(2,1)}, u32[]{:S(2)}, u32[]{:S(2)}) async-start(bf16[128,8,1024]{2,1,0:T(8,128)(2,1)} %bitcast.105), calls=%async_computation.2 | async-start | bytes 4194304 | tf_op jit(solution)/shard_map/all_to_all | solution.py:1011
  204.9 33.6 %collective-permute-done.6.partner = bf16[128,2048]{1,0:T(8,128)(2,1)S(1)} collective-permute-done((bf16[128,2048]{1,0:T(8,128)(2,1)S(1)}, bf16[128,2048]{1,0:T(8,128)(2,1)S(1)}, u32[]{:S(2)}, u32[]{:S(2)}) %collective-permute-start.6) | collective-permute-done | bytes 524320 | tf_op jit(solution)/shard_map/ppermute | solution.py:35
  238.6 17.4 %owner_both.1 = (bf16[512,1024]{1,0:T(8,128)(2,1)S(1)}, bf16[512,1024]{1,0:T(8,128)(2,1)}, bf16[512,2048]{1,0:T(8,128)(2,1)}, bf16[512,2048]{1,0:T(8,128)(2,1)}, bf16[1024,1024]{1,0:T(8,128)(2,1)}) custom-call(bf16[1024,1024]{1,0:T(8,128)(2,1)} %bitcast.21.arrived, bf16[1024,2048]{1,0:T(8,128)(2,1)} %bitcast.115, bf16[2048,1024]{1,0:T(8,128)(2,1)} %bitcast.116), custom_call_target="tpu_custom_call" | custom-call | flops 8999999488 | bytes 20000000 | tf_op jit(solution)/shard_map/owner_both/pallas_call | solution.py:781
  257.0 10.3 %all-to-all-start.3 = ((bf16[128,8,1024]{2,1,0:T(8,128)(2,1)}), bf16[128,8,1024]{2,1,0:T(8,128)(2,1)}, u32[]{:S(2)}, u32[]{:S(2)}) async-start(bf16[128,8,1024]{2,1,0:T(8,128)(2,1)} %bitcast.102), calls=%async_computation.3 | async-start | bytes 4194304 | tf_op jit(solution)/shard_map/all_to_all | solution.py:1011
  268.5 10.1 %feed.1 = (f32[128,2048]{1,0:T(8,128)}, bf16[128,2048]{1,0:T(8,128)(2,1)}, bf16[256,2048]{1,0:T(8,128)(2,1)}, bf16[256,2048]{1,0:T(8,128)(2,1)}, bf16[256,2048]{1,0:T(8,128)(2,1)}) custom-call(s32[2]{0:T(128)S(1)} %pad_add_fusion.place, bf16[128,2048]{1,0:T(8,128)(2,1)S(1)} %copy-done.2, bf16[128,2048]{1,0:T(8,128)(2,1)S(1)} %collective-permute-done.6.partner, ...), custom_call_target="tpu_custom_call" | custom-call | flops 1000000 | bytes 1000000 | tf_op jit(solution)/shard_map/feed/pallas_call | solution.py:78
  282.7 7.7 %feed_gradients.1.packed = bf16[1024,4224]{1,0:T(8,128)(2,1)} custom-call(s32[2]{0:T(128)S(1)} %pad_add_fusion.place, bf16[128,2048]{1,0:T(8,128)(2,1)S(1)} %copy-done.2, bf16[128,2048]{1,0:T(8,128)(2,1)S(1)} %collective-permute-done.6.partner, bf16[256,2048]{1,0:T(8,128)(2,1)} %collective-permute-done.7.twins, bf16[256,2048]{1,0:T(8,128)(2,1)} %get-tuple-element.128.active, ...), custom_call_target="tpu_custom_call" | custom-call | flops 1000000 | bytes 1000000 | tf_op jit(solution)/shard_map/feed_gradients/pallas_call | solution.py:960
  290.4 6.8 %all-to-all-done.3 = bf16[128,8,1024]{2,1,0:T(8,128)(2,1)} async-done(((bf16[128,8,1024]{2,1,0:T(8,128)(2,1)}), bf16[128,8,1024]{2,1,0:T(8,128)(2,1)}, u32[]{:S(2)}, u32[]{:S(2)}) %all-to-all-start.3) | async-done | bytes 2097184 | tf_op jit(solution)/shard_map/all_to_all | solution.py:1011
  297.3 6.1 %collective-permute-done.10.flipped = bf16[128,2048]{1,0:T(8,128)(2,1)} collective-permute-done((bf16[128,2048]{1,0:T(8,128)(2,1)}, bf16[128,2048]{1,0:T(8,128)(2,1)}, u32[]{:S(2)}, u32[]{:S(2)}) %collective-permute-start.10) | collective-permute-done | bytes 524320 | tf_op jit(solution)/shard_map/ppermute | solution.py:35
  303.3 13.8 %turn.1 = (bf16[128,1024]{1,0:T(8,128)(2,1)}, f32[128,1024]{1,0:T(8,128)S(1)}, bf16[128,2048]{1,0:T(8,128)(2,1)S(1)}, bf16[128,2048]{1,0:T(8,128)(2,1)}, f32[8,1...) custom-call(s32[2]{0:T(128)S(1)} %pad_add_fusion.place, ...), custom_call_target="tpu_custom_call" | custom-call | flops 1000000 | bytes 1000000 | tf_op jit(solution)/shard_map/turn/pallas_call | solution.py:78
  326.5 10.0 %all-to-all-start.4 = ((bf16[128,8,1024]{2,1,0:T(8,128)(2,1)}), bf16[128,8,1024]{2,1,0:T(8,128)(2,1)}, u32[]{:S(2)}, u32[]{:S(2)}) async-start(bf16[128,8,1024]{2,1,0:T(8,128)(2,1)} %bitcast.29), calls=%async_computation.4 | async-start | bytes 4194304 | tf_op jit(solution)/shard_map/all_to_all | solution.py:1011
  341.6 7.5 %fusion.23 = f32[2048,1024]{1,0:T(8,128)} fusion(bf16[512,2048]{1,0:T(8,128)(2,1)} %get-tuple-element.147, bf16[512,1024]{1,0:T(8,128)(2,1)S(1)} %copy-done.34), kind=kOutput, calls=%fused_computation.86 | convolution fusion | flops 2147483648 | bytes 11534336 | tf_op jit(solution)/shard_map/dot_general | solution.py:43
  359.4 13.3 %collective-permute-done.13 = bf16[128,1024]{1,0:T(8,128)(2,1)S(1)} collective-permute-done((bf16[128,1024]{1,0:T(8,128)(2,1)S(1)}, bf16[128,1024]{1,0:T(8,128)(2,1)S(1)}, u32[]{:S(2)}, u32[]{:S(2)}) %collective-permute-start.13) | collective-permute-done | bytes 262176 | tf_op jit(solution)/shard_map/ppermute | solution.py:27
  376.4 8.8 %owner_back.1 = (bf16[1024,1024]{1,0:T(8,128)(2,1)}, bf16[1024,1024]{1,0:T(8,128)(2,1)}) custom-call(bf16[1024,1024]{1,0:T(8,128)(2,1)} %bitcast.30.incoming, bf16[1024,1024]{1,0:T(8,128)(2,1)} %get-tuple-element.152.slope, bf16[1024,1024]{1,0:T(8,128)(2,1)} %bitcast.118, bf16[1024,1024]{1,0:T(8,128)(2,1)} %bitcast.120), custom_call_target="tpu_custom_call" | custom-call | flops 4300000256 | bytes 12000000 | tf_op jit(solution)/shard_map/owner_back/pallas_call | solution.py:781
  391.8 7.2 %feed_one_back.1 = (f32[128,1024]{1,0:T(8,128)S(1)}, bf16[128,1024]{1,0:T(8,128)(2,1)S(1)}, bf16[128,1024]{1,0:T(8,128)(2,1)S(1)}, bf16[128,1024]{1,0:T(8,128)(2...) custom-call(s32[2]{0:T(128)S(1)} %pad_add_fusion.place, bf16[512,1024]{1,0:T(8,128)(2,1)} %copy-done.15, ...), custom_call_target="tpu_custom_call" | custom-call | flops 1000000 | bytes 1000000 | tf_op jit(solution)/shard_map/feed_one_back/pallas_call | solution.py:78
  402.2 6.2 %fusion.25 = f32[1024,1024]{1,0:T(8,128)} fusion(bf16[1024,1024]{1,0:T(8,128)(2,1)S(1)} %copy-done.36, bf16[1024,1024]{1,0:T(8,128)(2,1)} %bitcast.30.incoming), kind=kOutput, calls=%fused_computation.88 | convolution fusion | flops 2147483648 | bytes 8388608 | tf_op jit(solution)/shard_map/dot_general | solution.py:43
  410.5 6.0 %fusion.24 = f32[1024,1024]{1,0:T(8,128)} fusion(bf16[1024,1024]{1,0:T(8,128)(2,1)} %bitcast.7.rows, bf16[1024,1024]{1,0:T(8,128)(2,1)S(1)} %copy-done.37), kind=kOutput, calls=%fused_computation.87 | convolution fusion | flops 2147483648 | bytes 8388608 | tf_op jit(solution)/shard_map/dot_general | solution.py:43
  417.9 6.6 %feed_weights.1 = bf16[1024,1024]{1,0:T(8,128)(2,1)} custom-call(s32[2]{0:T(128)S(1)} %pad_add_fusion.place, bf16[512,1024]{1,0:T(8,128)(2,1)S(1)} %copy-done.4, bf16[512,1024]{1,0:T(8,128)(2,1)} %copy-done.16, bf16[512,1024]{1,0:T(8,128)(2,1)} %get-tuple-element.164.grad_hidden, bf16[512,1024]{1,0:T(8,128)(2,1)} %get-tuple-element.157.active, ...), custom_call_target="tpu_custom_call" | custom-call | flops 1000000 | bytes 1000000 | tf_op jit(solution)/shard_map/feed_weights/pallas_call | solution.py:78
  424.5 7.1 %collective-permute-done.16.part_c = bf16[128,1024]{1,0:T(8,128)(2,1)S(1)} collective-permute-done((bf16[128,1024]{1,0:T(8,128)(2,1)S(1)}, bf16[128,1024]{1,0:T(8,128)(2,1)S(1)}, u32[]{:S(2)}, u32[]{:S(2)}) %collective-permute-start.16) | collective-permute-done | bytes 262176 | tf_op jit(solution)/shard_map/ppermute | solution.py:27
  436.7 13.0 %back.1 = (f32[128,1024]{1,0:T(8,128)}, bf16[4,128,512]{2,1,0:T(8,128)(2,1)S(1)}, bf16[4,128,512]{2,1,0:T(8,128)(2,1)}, f32[8,1024]{1,0:T(8,128)S(1)}) custom-call(s32[2]{0:T(128)S(1)} %pad_add_fusion.place, bf16[1024,1024]{1,0:T(8,128)(2,1)} %bitcast.32.back, s32[128,1]{1,0:T(8,128)S(1)} %get-tuple-element.215.slot_column, f32[128,1024]{1,0:T(8,128)} %copy-done.8, ...), custom_call_target="tpu_custom_call" | custom-call | flops 1000000 | bytes 1000000 | tf_op jit(solution)/shard_map/back/pallas_call | solution.py:78
  454.9 8.1 %collective-permute-done.23.part_c = bf16[256,512]{1,0:T(8,128)(2,1)S(1)} collective-permute-done((bf16[256,512]{1,0:T(8,128)(2,1)S(1)}, bf16[256,512]{1,0:T(8,128)(2,1)S(1)}, u32[]{:S(2)}, u32[]{:S(2)}) %collective-permute-start.23) | collective-permute-done | bytes 262176 | tf_op jit(solution)/shard_map/ppermute | solution.py:27
  480.3 6.9 %all-to-all-start.7 = ((bf16[32,32,640]{2,1,0:T(8,128)(2,1)}), bf16[32,32,640]{2,1,0:T(8,128)(2,1)S(1)}, u32[]{:S(2)}, u32[]{:S(2)}) async-start(bf16[32,32,640]{2,1,0:T(8,128)(2,1)} %bitcast.97), calls=%async_computation.7 | async-start | bytes 2621440 | tf_op jit(solution)/shard_map/all_to_all | solution.py:1355
  489.3 14.7 %all-gather.15.cloned.1.call-done = bf16[256,4224]{1,0:T(8,128)(2,1)} async-done(((bf16[64,4224]{1,0:T(8,128)(2,1)}), bf16[256,4224]{1,0:T(8,128)(2,1)}) %all-gather.15.cloned.1.call-update) | async-done | bytes 2162704 | tf_op jit(solution)/shard_map/all_gather | solution.py:1354
  (220 shorter events, 121.6 us)
Async XLA Ops:
  7.3 70.0 %all-gather.7.cloned.1.call-start = ((), (), s32[]{:S(2)}) async-start(), calls=%async_computation.9 | async-start | bytes 13246464 | tf_op jit(solution)/shard_map/all_gather | solution.py:1214
  11.4 150.4 %all-gather.9.cloned.1.call-start = ((), (), s32[]{:S(2)}) async-start(), calls=%async_computation.10 | async-start | bytes 8921088 | tf_op jit(solution)/shard_map/all_gather | solution.py:1226
  12.6 255.9 %all-gather.11.cloned.1.call-start = ((), (), s32[]{:S(2)}) async-start(), calls=%async_computation.11 | async-start | bytes 8650752 | tf_op jit(solution)/shard_map/all_gather | solution.py:1232
  84.6 45.6 %all-to-all-start = ((bf16[128,8,1024]{2,1,0:T(8,128)(2,1)}), bf16[128,8,1024]{2,1,0:T(8,128)(2,1)}, u32[]{:S(2)}, u32[]{:S(2)}) async-start(bf16[128,8,1024]{2,1,0:T(8,128)(2,1)} %bitcast.104), calls=%async_computation | async-start | bytes 4194304 | tf_op jit(solution)/shard_map/all_to_all | solution.py:1011
  93.4 30.2 %collective-permute-start = (bf16[128,1024]{1,0:T(8,128)(2,1)S(1)}, bf16[128,1024]{1,0:T(8,128)(2,1)S(1)}, u32[]{:S(2)}, u32[]{:S(2)}) collective-permute-start(bf16[128,1024]{1,0:T(8,128)(2,1)S(1)} %get-tuple-element.112.normed_two), channel_id=1, source_target_pairs={{0,32},{32,64},{64,96},{96,0},{1,33},{33,65},{65,97},{97,1},{2,34}... | collective-permute-start | bytes 786440 | tf_op jit(solution)/shard_map/ppermute | solution.py:27
  94.5 29.2 %collective-permute-start.1 = (bf16[128,1024]{1,0:T(8,128)(2,1)S(1)}, bf16[128,1024]{1,0:T(8,128)(2,1)S(1)}, u32[]{:S(2)}, u32[]{:S(2)}) collective-permute-start(bf16[128,1024]{1,0:T(8,128)(2,1)S(1)} %get-tuple-element.112.normed_two), channel_id=1, source_target_pairs={{0,96},{32,0},{64,32},{96,64},{1,97},{33,1},{65,33},{97,65},{2,98}... | collective-permute-start | bytes 786440 | tf_op jit(solution)/shard_map/ppermute | solution.py:27
  96.7 33.5 %collective-permute-start.2 = (bf16[128,1024]{1,0:T(8,128)(2,1)S(1)}, bf16[128,1024]{1,0:T(8,128)(2,1)S(1)}, u32[]{:S(2)}, u32[]{:S(2)}) collective-permute-start(bf16[128,1024]{1,0:T(8,128)(2,1)S(1)} %get-tuple-element.112.normed_two), channel_id=1, source_target_pairs={{0,64},{32,96},{64,0},{96,32},{1,65},{33,97},{65,1},{97,33},{2,66}... | collective-permute-start | bytes 786440 | tf_op jit(solution)/shard_map/ppermute | solution.py:27
  139.7 45.9 %all-to-all-start.1 = ((bf16[128,8,1024]{2,1,0:T(8,128)(2,1)}), bf16[128,8,1024]{2,1,0:T(8,128)(2,1)}, u32[]{:S(2)}, u32[]{:S(2)}) async-start(bf16[128,8,1024]{2,1,0:T(8,128)(2,1)} %bitcast.103), calls=%async_computation.1 | async-start | bytes 4194304 | tf_op jit(solution)/shard_map/all_to_all | solution.py:1011
  156.7 21.3 %collective-permute-start.3 = (bf16[128,1024]{1,0:T(8,128)(2,1)S(1)}, bf16[128,1024]{1,0:T(8,128)(2,1)S(1)}, u32[]{:S(2)}, u32[]{:S(2)}) collective-permute-start(bf16[128,1024]{1,0:T(8,128)(2,1)S(1)} %get-tuple-element.119), channel_id=1, source_target_pairs={{0,96},{32,0},{64,32},{96,64},{1,97},{33,1},{65,33},{97,65},{2,98}... | collective-permute-start | bytes 786440 | tf_op jit(solution)/shard_map/ppermute | solution.py:27
  159.7 20.6 %collective-permute-start.4 = (bf16[128,1024]{1,0:T(8,128)(2,1)S(1)}, bf16[128,1024]{1,0:T(8,128)(2,1)S(1)}, u32[]{:S(2)}, u32[]{:S(2)}) collective-permute-start(bf16[128,1024]{1,0:T(8,128)(2,1)S(1)} %get-tuple-element.120), channel_id=1, source_target_pairs={{0,32},{32,64},{64,96},{96,0},{1,33},{33,65},{65,97},{97,1},{2,34}... | collective-permute-start | bytes 786440 | tf_op jit(solution)/shard_map/ppermute | solution.py:27
  159.7 25.9 %collective-permute-start.5 = (bf16[128,1024]{1,0:T(8,128)(2,1)S(1)}, bf16[128,1024]{1,0:T(8,128)(2,1)S(1)}, u32[]{:S(2)}, u32[]{:S(2)}) collective-permute-start(bf16[128,1024]{1,0:T(8,128)(2,1)S(1)} %get-tuple-element.121), channel_id=1, source_target_pairs={{0,64},{32,96},{64,0},{96,32},{1,65},{33,97},{65,1},{97,33},{2,66}... | collective-permute-start | bytes 786440 | tf_op jit(solution)/shard_map/ppermute | solution.py:27
  196.6 41.9 %all-to-all-start.2 = ((bf16[128,8,1024]{2,1,0:T(8,128)(2,1)}), bf16[128,8,1024]{2,1,0:T(8,128)(2,1)}, u32[]{:S(2)}, u32[]{:S(2)}) async-start(bf16[128,8,1024]{2,1,0:T(8,128)(2,1)} %bitcast.105), calls=%async_computation.2 | async-start | bytes 4194304 | tf_op jit(solution)/shard_map/all_to_all | solution.py:1011
  203.6 93.7 %all-gather.13.cloned.1.call-start = ((), (), s32[]{:S(2)}) async-start(), calls=%async_computation.12 | async-start | bytes 4718592 | tf_op jit(solution)/shard_map/all_gather | solution.py:1263
  203.7 34.9 %collective-permute-start.6 = (bf16[128,2048]{1,0:T(8,128)(2,1)S(1)}, bf16[128,2048]{1,0:T(8,128)(2,1)S(1)}, u32[]{:S(2)}, u32[]{:S(2)}) collective-permute-start(bf16[128,2048]{1,0:T(8,128)(2,1)S(1)} %copy-done.2), channel_id=1, source_target_pairs={{0,32},{32,0},{64,96},{96,64},{1,33},{33,1},{65,97},{97,65},{2,34}... | collective-permute-start | bytes 1572872 | tf_op jit(solution)/shard_map/ppermute | solution.py:35
  257.0 40.2 %all-to-all-start.3 = ((bf16[128,8,1024]{2,1,0:T(8,128)(2,1)}), bf16[128,8,1024]{2,1,0:T(8,128)(2,1)}, u32[]{:S(2)}, u32[]{:S(2)}) async-start(bf16[128,8,1024]{2,1,0:T(8,128)(2,1)} %bitcast.102), calls=%async_computation.3 | async-start | bytes 4194304 | tf_op jit(solution)/shard_map/all_to_all | solution.py:1011
  267.3 205.7 %reduce-scatter.2.cloned.1.call-start = ((), (), s32[]{:S(2)}) async-start(), calls=%async_computation.13 | async-start | bytes 9191424 | tf_op jit(solution)/shard_map/reduce_scatter | solution.py:1316
  279.6 17.6 %collective-permute-start.9 = (bf16[128,2048]{1,0:T(8,128)(2,1)S(1)}, bf16[128,2048]{1,0:T(8,128)(2,1)S(1)}, u32[]{:S(2)}, u32[]{:S(2)}) collective-permute-start(bf16[128,2048]{1,0:T(8,128)(2,1)S(1)} %copy-done.9), channel_id=1, source_target_pairs={{0,1},{1,0},{2,3},{3,2},{4,5},{5,4},{6,7},{7,6},{8,9},{9,8},{10,11... | collective-permute-start | bytes 1572872 | tf_op jit(solution)/shard_map/ppermute | solution.py:27
  279.7 23.6 %collective-permute-start.10 = (bf16[128,2048]{1,0:T(8,128)(2,1)}, bf16[128,2048]{1,0:T(8,128)(2,1)}, u32[]{:S(2)}, u32[]{:S(2)}) collective-permute-start(bf16[128,2048]{1,0:T(8,128)(2,1)} %get-tuple-element.139), channel_id=1, source_target_pairs={{0,32},{32,0},{64,96},{96,64},{1,33},{33,1},{65,97},{97,65},{2,34}... | collective-permute-start | bytes 1572872 | tf_op jit(solution)/shard_map/ppermute | solution.py:35
  326.5 49.9 %all-to-all-start.4 = ((bf16[128,8,1024]{2,1,0:T(8,128)(2,1)}), bf16[128,8,1024]{2,1,0:T(8,128)(2,1)}, u32[]{:S(2)}, u32[]{:S(2)}) async-start(bf16[128,8,1024]{2,1,0:T(8,128)(2,1)} %bitcast.29), calls=%async_computation.4 | async-start | bytes 4194304 | tf_op jit(solution)/shard_map/all_to_all | solution.py:1011
  336.5 22.7 %collective-permute-start.11 = (bf16[128,1024]{1,0:T(8,128)(2,1)S(1)}, bf16[128,1024]{1,0:T(8,128)(2,1)S(1)}, u32[]{:S(2)}, u32[]{:S(2)}) collective-permute-start(bf16[128,1024]{1,0:T(8,128)(2,1)S(1)} %get-tuple-element.150), channel_id=1, source_target_pairs={{0,32},{32,64},{64,96},{96,0},{1,33},{33,65},{65,97},{97,1},{2,34}... | collective-permute-start | bytes 786440 | tf_op jit(solution)/shard_map/ppermute | solution.py:27
  337.8 21.6 %collective-permute-start.12 = (bf16[128,1024]{1,0:T(8,128)(2,1)S(1)}, bf16[128,1024]{1,0:T(8,128)(2,1)S(1)}, u32[]{:S(2)}, u32[]{:S(2)}) collective-permute-start(bf16[128,1024]{1,0:T(8,128)(2,1)S(1)} %get-tuple-element.150), channel_id=1, source_target_pairs={{0,96},{32,0},{64,32},{96,64},{1,97},{33,1},{65,33},{97,65},{2,98}... | collective-permute-start | bytes 786440 | tf_op jit(solution)/shard_map/ppermute | solution.py:27
  340.0 32.7 %collective-permute-start.13 = (bf16[128,1024]{1,0:T(8,128)(2,1)S(1)}, bf16[128,1024]{1,0:T(8,128)(2,1)S(1)}, u32[]{:S(2)}, u32[]{:S(2)}) collective-permute-start(bf16[128,1024]{1,0:T(8,128)(2,1)S(1)} %get-tuple-element.150), channel_id=1, source_target_pairs={{0,64},{32,96},{64,0},{96,32},{1,65},{33,97},{65,1},{97,33},{2,66}... | collective-permute-start | bytes 786440 | tf_op jit(solution)/shard_map/ppermute | solution.py:27
  385.2 46.3 %all-to-all-start.5 = ((bf16[128,8,1024]{2,1,0:T(8,128)(2,1)}), bf16[128,8,1024]{2,1,0:T(8,128)(2,1)}, u32[]{:S(2)}, u32[]{:S(2)}) async-start(bf16[128,8,1024]{2,1,0:T(8,128)(2,1)} %bitcast.101), calls=%async_computation.5 | async-start | bytes 4194304 | tf_op jit(solution)/shard_map/all_to_all | solution.py:1011
  391.2 17.2 %collective-permute-start.17 = (bf16[512,1024]{1,0:T(8,128)(2,1)S(1)}, bf16[512,1024]{1,0:T(8,128)(2,1)S(1)}, u32[]{:S(2)}, u32[]{:S(2)}) collective-permute-start(bf16[512,1024]{1,0:T(8,128)(2,1)S(1)} %copy-done.4), channel_id=1, source_target_pairs={{0,1},{1,0},{2,3},{3,2},{4,5},{5,4},{6,7},{7,6},{8,9},{9,8},{10,11... | collective-permute-start | bytes 3145736 | tf_op jit(solution)/shard_map/ppermute | solution.py:27
  391.3 25.3 %collective-permute-start.19 = (bf16[512,1024]{1,0:T(8,128)(2,1)S(1)}, bf16[512,1024]{1,0:T(8,128)(2,1)S(1)}, u32[]{:S(2)}, u32[]{:S(2)}) collective-permute-start(bf16[512,1024]{1,0:T(8,128)(2,1)S(1)} %constant_dynamic-update-slice_fusion.4.group.inc), channel_id=1, source_target_pairs={{0,1},{1,0},{2,3},{3,2},{4,5},{5,4},{6,7},{7,6},{8,9},{9,8},{10,11... | collective-permute-start | bytes 3145736 | tf_op jit(solution)/shard_map/ppermute | solution.py:27
  398.9 17.6 %collective-permute-start.18 = (bf16[512,1024]{1,0:T(8,128)(2,1)}, bf16[512,1024]{1,0:T(8,128)(2,1)S(1)}, u32[]{:S(2)}, u32[]{:S(2)}) collective-permute-start(bf16[512,1024]{1,0:T(8,128)(2,1)} %get-tuple-element.165), channel_id=1, source_target_pairs={{0,1},{1,0},{2,3},{3,2},{4,5},{5,4},{6,7},{7,6},{8,9},{9,8},{10,11... | collective-permute-start | bytes 3145736 | tf_op jit(solution)/shard_map/ppermute | solution.py:27
  399.2 25.3 %collective-permute-start.14 = (bf16[128,1024]{1,0:T(8,128)(2,1)S(1)}, bf16[128,1024]{1,0:T(8,128)(2,1)S(1)}, u32[]{:S(2)}, u32[]{:S(2)}) collective-permute-start(bf16[128,1024]{1,0:T(8,128)(2,1)S(1)} %get-tuple-element.160), channel_id=1, source_target_pairs={{0,96},{32,0},{64,32},{96,64},{1,97},{33,1},{65,33},{97,65},{2,98}... | collective-permute-start | bytes 786440 | tf_op jit(solution)/shard_map/ppermute | solution.py:27
  402.0 22.5 %collective-permute-start.15 = (bf16[128,1024]{1,0:T(8,128)(2,1)S(1)}, bf16[128,1024]{1,0:T(8,128)(2,1)S(1)}, u32[]{:S(2)}, u32[]{:S(2)}) collective-permute-start(bf16[128,1024]{1,0:T(8,128)(2,1)S(1)} %get-tuple-element.161), channel_id=1, source_target_pairs={{0,32},{32,64},{64,96},{96,0},{1,33},{33,65},{65,97},{97,1},{2,34}... | collective-permute-start | bytes 786440 | tf_op jit(solution)/shard_map/ppermute | solution.py:27
  408.4 23.2 %collective-permute-start.16 = (bf16[128,1024]{1,0:T(8,128)(2,1)S(1)}, bf16[128,1024]{1,0:T(8,128)(2,1)S(1)}, u32[]{:S(2)}, u32[]{:S(2)}) collective-permute-start(bf16[128,1024]{1,0:T(8,128)(2,1)S(1)} %get-tuple-element.162), channel_id=1, source_target_pairs={{0,64},{32,96},{64,0},{96,32},{1,65},{33,97},{65,1},{97,33},{2,66}... | collective-permute-start | bytes 786440 | tf_op jit(solution)/shard_map/ppermute | solution.py:27
  431.6 41.4 %all-to-all-start.6 = ((bf16[16,64,1024]{2,1,0:T(8,128)(2,1)}), bf16[16,64,1024]{2,1,0:T(8,128)(2,1)}, u32[]{:S(2)}, u32[]{:S(2)}) async-start(bf16[16,64,1024]{2,1,0:T(8,128)(2,1)} %bitcast.95), calls=%async_computation.6 | async-start | bytes 4194304 | tf_op jit(solution)/shard_map/all_to_all | solution.py:1017
  436.7 67.3 %all-gather.15.cloned.1.call-start = ((), (), s32[]{:S(2)}) async-start(), calls=%async_computation.14 | async-start | bytes 2703360 | tf_op jit(solution)/shard_map/all_gather | solution.py:1354
  480.3 26.8 %all-to-all-start.7 = ((bf16[32,32,640]{2,1,0:T(8,128)(2,1)}), bf16[32,32,640]{2,1,0:T(8,128)(2,1)S(1)}, u32[]{:S(2)}, u32[]{:S(2)}) async-start(bf16[32,32,640]{2,1,0:T(8,128)(2,1)} %bitcast.97), calls=%async_computation.7 | async-start | bytes 2621440 | tf_op jit(solution)/shard_map/all_to_all | solution.py:1355
  (53 other events, 398.2 us)
Sparse Core Ops, SparseCore 0:
  11.5 65.7 all-gather.6
  80.1 70.1 all-gather.8
  153.2 66.8 all-gather.10
  238.7 39.2 all-gather.12
  326.6 137.2 reduce-scatter.1
  473.2 30.7 all-gather.14
